TPU v7x, 128 devices: a whole 4x4x4 slice. The times are simulated.
128 devices in a mesh: slide: 4 (over y), tile: 32 (over z, x, core).
Axes of the slice: x: 4, y: 4, z: 4, core: 2. Of those that a mesh axis runs over, the one named last changes fastest.
Arguments:
- tiles: bfloat16 [128, 256, 1536], P('tile'), may hold values from -6 to 6
- w_in: bfloat16 [1536, 6144], P(None, 'slide'), may hold values from -0.15625 to 0.15625
- w_out: bfloat16 [6144, 1536], P('slide'), may hold values from -0.078125 to 0.078125
- w_proj: bfloat16 [1536, 768], replicated, may hold values from -0.15625 to 0.15625
- w_qkv: bfloat16 [768, 2304], replicated, may hold values from -0.25 to 0.25
- w_attn_out: bfloat16 [768, 768], replicated, may hold values from -0.21875 to 0.21875
- slide_of_tile: int32 [128], replicated, may hold values from 0 to 15, as said below
- order_of_tile: int32 [128], replicated, may hold values from 0 to 56, as said below
- slide_counts: int32 [16], replicated, may hold values from 1 to 57, as said below
- seg_len: int32 [3], replicated, may hold values from 2 to 16
- slide_cot: float32 [16, 768], P('slide'), may hold values from -6 to 6
Outputs:
- slide_embed: float32 [16, 768], P('slide')
- grad_in: float32 [1536, 6144], P('tile', 'slide')
- grad_out: float32 [6144, 1536], P(('slide', 'tile'))
Inputs may be any that keep to these rules, and one draw needn't show every extreme that they name: Every slide has at least one tile; slide_counts sums to 128; exactly one slide has the most tiles. `slide_of_tile`: slide g is named by exactly slide_counts[g] tiles. `order_of_tile`: the tiles of slide g carry the positions 0 to slide_counts[g] - 1, each once.
All inputs are finite; a program needn't handle non-finite values.
Results may differ from a plain program's by a relative error of at most 0.02.
Values may be sent and summed in bfloat16 or wider, within the bound.
No kernel may reach another device: no remote copies, remote signals or barrier semaphores. Data moves between devices by JAX's collectives and lax.ppermute only.
A program may use at most 128 MiB of HBM per device.

v0:
```python
import math

import jax
import jax.numpy as jnp
from jax import lax
from jax.sharding import PartitionSpec as P

SH = 16


epsilon = 1e-06


def normalize(values):
    values = values.astype(jnp.float32)
    centre = jnp.mean(values, axis=-1, keepdims=True)
    shifted = values - centre
    spread = jnp.mean(shifted * shifted, axis=-1, keepdims=True)
    return (shifted * lax.rsqrt(spread + epsilon)).astype(jnp.bfloat16)


def gelu_pair(preact):
    normal_cdf = 0.5 * (1.0 + lax.erf(preact * 0.7071067811865476))
    normal_pdf = jnp.exp(-0.5 * preact * preact) * 0.3989422804014327
    return (preact * normal_cdf, normal_cdf + preact * normal_pdf)


def multiplicity(slide_query, order_query, slide_key, order_key, seg_len):
    same_slide = slide_query[:, None] == slide_key[None, :]
    counted = jnp.zeros(same_slide.shape, jnp.float32)
    for branch in range(seg_len.shape[0]):
        seg_width = seg_len[branch]
        dilation = 2**branch
        same_block = order_query[:, None] // seg_width == order_key[None, :] // seg_width
        same_phase = order_query[:, None] % dilation == order_key[None, :] % dilation
        counted = counted + (same_slide & same_block & same_phase).astype(jnp.float32)
    return counted


def attend(query_rows, key_rows, value_rows, weight, head_count):
    query_count = query_rows.shape[0]
    key_count = key_rows.shape[0]
    head_dim = query_rows.shape[1] // head_count
    query_heads = query_rows.reshape(query_count, head_count, head_dim)
    key_heads = key_rows.reshape(key_count, head_count, head_dim)
    value_heads = value_rows.reshape(key_count, head_count, head_dim)
    scores = jnp.einsum(
        "qhd,khd->hqk", query_heads, key_heads, precision=lax.Precision.HIGHEST
    ) / math.sqrt(head_dim)
    allowed = (weight > 0.0)[None]
    scores = jnp.where(allowed, scores, -1e30)
    row_max = jnp.max(scores, axis=-1, keepdims=True)
    numerator = weight[None] * jnp.exp(scores - row_max)
    denominator = jnp.sum(numerator, axis=-1, keepdims=True)
    context = jnp.einsum(
        "hqk,khd->qhd", numerator / denominator, value_heads, precision=lax.Precision.HIGHEST
    )
    return context.reshape(query_count, head_count * head_dim)


def on_device(
    tiles,
    w_in,
    w_out,
    w_proj,
    w_qkv,
    w_attn_out,
    slide_of_tile,
    order_of_tile,
    slide_counts,
    seg_len,
    slide_cot,
):
    tile_count, patches, width = tiles.shape
    local_hidden = w_in.shape[1]
    slide_width = w_proj.shape[1]
    normed = normalize(tiles.reshape(tile_count * patches, width))
    preact = jnp.dot(normed, w_in, preferred_element_type=jnp.float32)
    gelu_value, gelu_slope = gelu_pair(preact)
    hidden = gelu_value.astype(jnp.bfloat16)
    pooled = jnp.mean(hidden.reshape(tile_count, patches, local_hidden), axis=1, dtype=jnp.float32)
    token_out = jnp.dot(hidden, w_out, preferred_element_type=jnp.float32)
    branch_part = jnp.mean(token_out.reshape(tile_count, patches, width), axis=1)
    branch_term = lax.psum(branch_part, "slide")
    token_mean = jnp.mean(tiles, axis=1, dtype=jnp.float32)
    embedding = (token_mean + branch_term).astype(jnp.bfloat16)
    tile_pos = lax.axis_index("tile")
    slide_row = lax.axis_index("slide")
    first_tile = tile_pos * tile_count
    own_slide = lax.dynamic_slice_in_dim(slide_of_tile, first_tile, tile_count)
    own_order = lax.dynamic_slice_in_dim(order_of_tile, first_tile, tile_count)
    slide_rows = jnp.dot(embedding, w_proj, preferred_element_type=jnp.float32).astype(jnp.bfloat16)
    own_qkv = jnp.dot(slide_rows, w_qkv, preferred_element_type=jnp.float32).astype(jnp.bfloat16)
    key_rows, value_rows = (
        lax.all_gather(own_qkv[:, slide_width : 2 * slide_width], "tile", axis=0, tiled=True),
        lax.all_gather(own_qkv[:, 2 * slide_width :], "tile", axis=0, tiled=True),
    )
    query_wide = lax.optimization_barrier(own_qkv[:, :slide_width]).astype(jnp.float32)
    key_wide = lax.optimization_barrier(key_rows).astype(jnp.float32)
    value_wide = lax.optimization_barrier(value_rows).astype(jnp.float32)
    rows_wide = lax.optimization_barrier(slide_rows).astype(jnp.float32)
    weight = multiplicity(own_slide, own_order, slide_of_tile, order_of_tile, seg_len)
    group_size = slide_cot.shape[0]
    slide_ids = slide_row * group_size + jnp.arange(group_size, dtype=jnp.int32)
    group_counts = lax.dynamic_slice_in_dim(
        slide_counts, slide_row * group_size, group_size
    ).astype(jnp.float32)
    assign = (own_slide[None, :] == slide_ids[:, None]).astype(jnp.float32) / group_counts[:, None]
    out_wide = w_attn_out.astype(jnp.float32)

    def slide_fn(query_rows, all_keys, all_values, base_rows):
        context = attend(query_rows, all_keys, all_values, weight, SH)
        attended = base_rows + jnp.dot(context, out_wide, precision=lax.Precision.HIGHEST)
        return jnp.dot(assign, attended, precision=lax.Precision.HIGHEST)

    partial_value, pullback = jax.vjp(slide_fn, query_wide, key_wide, value_wide, rows_wide)
    slide_embed = lax.psum(partial_value, "tile")
    d_query, d_keys, d_values, d_direct = pullback(slide_cot)
    qkv_wide = w_qkv.astype(jnp.float32)
    d_keys_own, d_values_own = (
        lax.psum_scatter(d_keys, "tile", scatter_dimension=0, tiled=True),
        lax.psum_scatter(d_values, "tile", scatter_dimension=0, tiled=True),
    )
    d_qkv = jnp.concatenate([d_query, d_keys_own, d_values_own], axis=1)
    d_slide = d_direct + jnp.dot(d_qkv, qkv_wide.T, precision=lax.Precision.HIGHEST)
    d_part = jnp.dot(d_slide, w_proj.astype(jnp.float32).T, precision=lax.Precision.HIGHEST)
    d_embed = lax.psum(d_part, "slide")
    out_term = lax.dot_general(
        pooled,
        d_embed,
        (((0,), (0,)), ((), ())),
        precision=lax.Precision.HIGHEST,
        preferred_element_type=jnp.float32,
    )
    grad_out = lax.psum_scatter(out_term, "tile", scatter_dimension=0, tiled=True)
    d_pooled = lax.dot_general(
        d_embed,
        w_out,
        (((1,), (1,)), ((), ())),
        precision=lax.Precision.HIGHEST,
        preferred_element_type=jnp.float32,
    )
    d_preact = (
        (gelu_slope.reshape(tile_count, patches, local_hidden) * (d_pooled / patches)[:, None, :])
        .reshape(tile_count * patches, local_hidden)
        .astype(jnp.bfloat16)
    )
    grad_in = lax.psum_scatter(
        lax.dot_general(
            normed, d_preact, (((0,), (0,)), ((), ())), preferred_element_type=jnp.float32
        ),
        "tile",
        scatter_dimension=0,
        tiled=True,
    )
    return (slide_embed, grad_in, grad_out)


def solution(mesh):
    placed = (
        P("tile", None, None),
        P(None, "slide"),
        P("slide", None),
        P(),
        P(),
        P(),
        P(),
        P(),
        P(),
        P(),
        P("slide", None),
    )
    return jax.shard_map(
        on_device,
        mesh=mesh,
        in_specs=placed,
        out_specs=(P("slide", None), P("tile", "slide"), P(("slide", "tile"), None)),
        check_vma=False,
    )
```

profile of v0, /device:TPU:0, one launch (start us, length us, event | category | flops | bytes accessed | tf_op | source)
XLA Modules:
  0.0 491.4 jit_solution(348819147215150078)
XLA Ops:
  11.3 2.1 and_select_fusion.9
  13.4 3.3 and_select_fusion.8
  16.7 2.0 and_select_fusion.7
  21.6 2.3 fusion.45
  24.6 3.7 convert_reduce_fusion.2
  30.2 8.0 %convert_reduce_fusion = (f32[4,1536]{1,0:T(4,128)}, bf16[1024,1536]{1,0:T(8,128)(2,1)S(1)}, f32[1024,1536]{1,0:T(8,128)}) fusion(bf16[1024,1536]{1,0:T(8,128)(2,1)S(1)} %fusion.7, bf16[1536,1536]{1,0:T(8,128)(2,1)S(1)} %bitcast.82), kind=kOutput, calls=%fused_computation.7 | convolution fusion | flops 4842842112 | bytes 17326080 | tf_op jit(solution)/shard_map/dot_general | solution.py:78
  38.3 5.3 %bitcast_reduce_fusion = f32[4,1536]{1,0:T(4,128)S(1)} fusion(bf16[1024,1536]{1,0:T(8,128)(2,1)S(1)} %get-tuple-element.8, bf16[1536,1536]{1,0:T(8,128)(2,1)S(1)} %bitcast.72), kind=kOutput, calls=%fused_computation.8 | convolution fusion | flops 4833404928 | bytes 7888896 | tf_op jit(solution)/shard_map/dot_general | solution.py:82
  44.1 18.6 %psum.21 = f32[4,1536]{1,0:T(4,128)} all-reduce(f32[4,1536]{1,0:T(4,128)} %broadcast_multiply_fusion), channel_id=1, replica_groups=mesh['slide'=4,'tile'=32] {'slide'}, use_global_device_ids=true, to_apply=%region_4.0 | all-reduce | flops 6144 | bytes 49152 | tf_op jit(solution)/shard_map/psum | solution.py:84
  62.7 2.1 convolution_convert_fusion.1
  66.8 28.6 %all-gather.1 = bf16[32,4,768]{2,1,0:T(4,128)(2,1)} all-gather(bf16[1,4,768]{2,1,0:T(4,128)(2,1)} %get-tuple-element.19), channel_id=1, replica_groups=mesh['slide'=4,'tile'=32] {'tile'}, dimensions={0}, use_global_device_ids=true | all-gather | bytes 202752 | tf_op jit(solution)/shard_map/all_gather | solution.py:95
  95.4 1.7 reshape.524
  97.0 1.7 copy.29
  102.2 25.8 %all-gather = bf16[32,4,768]{2,1,0:T(4,128)(2,1)} all-gather(bf16[1,4,768]{2,1,0:T(4,128)(2,1)} %get-tuple-element.20), channel_id=1, replica_groups=mesh['slide'=4,'tile'=32] {'tile'}, dimensions={0}, use_global_device_ids=true | all-gather | bytes 202752 | tf_op jit(solution)/shard_map/all_gather | solution.py:96
  128.0 1.7 reshape.522
  129.6 1.7 copy.28
  131.4 2.4 fusion.14
  133.8 2.4 convert_reduce_fusion.3
  136.8 1.9 copy.36
  140.5 1.9 fusion.23
  142.4 1.9 copy.35
  144.4 1.5 convolution_bitcast_fusion
  149.2 96.2 %all-reduce.5.cloned.1.call-done = (f32[128,768]{1,0:T(8,128)}, f32[128,768]{1,0:T(8,128)}) async-done(((f32[128,768]{1,0:T(8,128)}, f32[128,768]{1,0:T(8,128)}), (f32[128,768]{1,0:T(8,128)}, f32[128,768]{1,0:T(8,128)})) %all-reduce.5.cloned.1.call-update) | async-done | bytes 786448
  246.9 3.5 convolution_add_fusion
  250.4 4.2 fusion.46
  254.7 18.2 %psum.23 = f32[4,1536]{1,0:T(4,128)} all-reduce(f32[4,1536]{1,0:T(4,128)} %fusion.46), channel_id=1, replica_groups=mesh['slide'=4,'tile'=32] {'slide'}, use_global_device_ids=true, to_apply=%region_13.14 | all-reduce | flops 6144 | bytes 49152 | tf_op jit(solution)/shard_map/psum | solution.py:127
  272.9 6.1 %convolution_multiply_fusion = f32[4,1536]{1,0:T(4,128)S(1)} fusion(f32[4,1536]{1,0:T(4,128)} %psum.23, bf16[1536,1536]{1,0:T(8,128)(2,1)} %param.13), kind=kOutput, calls=%fused_computation.18 | convolution fusion | flops 113252352 | bytes 4767744 | tf_op jit(solution)/shard_map/dot_general | solution.py:136
  279.0 5.1 %fusion.5 = bf16[1024,1536]{1,0:T(8,128)(2,1)S(1)} fusion(f32[1024,1536]{1,0:T(8,128)} %get-tuple-element.35, f32[4,1536]{1,0:T(4,128)S(1)} %convolution_multiply_fusion), kind=kLoop, calls=%fused_computation.6 | loop fusion | flops 15728640 | bytes 9461760 | tf_op jit(solution)/shard_map/convert_element_type | solution.py:146
  284.1 7.7 %fusion.47 = f32[1536,1536]{1,0:T(8,128)} fusion(bf16[1024,1536]{1,0:T(8,128)(2,1)S(1)} %copy-done.3, bf16[1024,1536]{1,0:T(8,128)(2,1)S(1)} %fusion.5), kind=kOutput, calls=%fused_computation.105 | convolution fusion | flops 4831838208 | bytes 15728640 | tf_op jit(solution)/shard_map/dot_general | solution.py:149
  292.1 10.8 %fusion.21 = f32[1536,1536]{1,0:T(8,128)} fusion(f32[4,1536]{1,0:T(4,128)} %psum.23, f32[4,1536]{1,0:T(4,128)} %get-tuple-element.7), kind=kOutput, calls=%fused_computation.43 | convolution fusion | flops 113252352 | bytes 9486336 | tf_op jit(solution)/shard_map/dot_general | solution.py:128
  306.5 1.9 convolution_add_fusion.1
  309.4 124.7 %psum.22 = f32[4,768]{1,0:T(4,128)} all-reduce(f32[4,768]{1,0:T(4,128)S(1)} %fusion.31), channel_id=1, replica_groups=mesh['slide'=4,'tile'=32] {'tile'}, use_global_device_ids=true, to_apply=%region_7.8 | all-reduce | flops 3072 | bytes 24576 | tf_op jit(solution)/shard_map/psum | solution.py:117
  434.1 50.8 %reduce-scatter.5.cloned.1.call-done = f32[48,1536]{1,0:T(8,128)} async-done(((f32[1536,1536]{1,0:T(8,128)}), f32[48,1536]{1,0:T(8,128)}) %reduce-scatter.5.cloned.1.call-update) | async-done | bytes 294928 | tf_op jit(solution)/shard_map/reduce_scatter | solution.py:135
  (84 shorter events, 25.0 us)
Async XLA Ops:
  7.2 57.7 %copy-start = (bf16[768,2304]{1,0:T(8,128)(2,1)S(1)}, bf16[768,2304]{1,0:T(8,128)(2,1)}, u32[]{:S(2)}) copy-start(bf16[768,2304]{1,0:T(8,128)(2,1)} %param.15) | copy-start | bytes 10616836
  7.2 238.2 %all-reduce.5.cloned.1.call-start = ((), (), s32[]{:S(2)}) async-start(), calls=%async_computation.4 | async-start | bytes 1572864
  11.3 8.1 %copy-start.15 = (s32[4]{0:T(128)}, s32[4]{0:T(128)S(1)}, u32[]{:S(2)}) copy-start(s32[4]{0:T(128)S(1)} %dynamic_slice.9) | copy-start | bytes 52
  19.4 0.6 copy-start.16
  19.4 0.6 copy-start.17
  21.0 0.6 copy-start.11
  24.6 3.7 copy-start.1
  24.6 5.5 %slice-start.2 = ((s8[4718592]{0:T(1024)(128)(4,1)}), s8[4194304]{0:T(1024)(128)(4,1)S(1)}, s32[]{:S(2)}) async-start(s8[4718592]{0:T(1024)(128)(4,1)} %bitcast.81), calls=%async_computation.7 | async-start | bytes 8388608
  28.3 1.8 slice-start.3
  29.3 8.9 %slice-start = ((s8[4718592]{0:T(1024)(128)(4,1)}), s8[524288]{0:T(1024)(128)(4,1)S(1)}, s32[]{:S(2)}) async-start(s8[4718592]{0:T(1024)(128)(4,1)} %bitcast.71), calls=%async_computation.5 | async-start | bytes 1048576
  30.2 8.1 %copy-start.2 = (bf16[1024,1536]{1,0:T(8,128)(2,1)}, bf16[1024,1536]{1,0:T(8,128)(2,1)S(1)}, u32[]{:S(2)}) copy-start(bf16[1024,1536]{1,0:T(8,128)(2,1)S(1)} %fusion.7) | copy-start | bytes 9437188
  30.2 8.1 %slice-start.1 = ((s8[4718592]{0:T(1024)(128)(4,1)}), s8[4194304]{0:T(1024)(128)(4,1)S(1)}, s32[]{:S(2)}) async-start(s8[4718592]{0:T(1024)(128)(4,1)} %bitcast.71), calls=%async_computation.6 | async-start | bytes 8388608
  64.8 1.2 copy-start.10
  99.6 1.2 copy-start.14
  99.6 2.6 copy-start.13
  100.8 0.6 copy-start.4
  100.8 0.8 copy-start.6
  101.6 0.6 copy-start.8
  139.7 2.6 copy-start.5
  140.5 1.9 copy-start.12
  144.3 289.8 %reduce-scatter.3.cloned.1.call-start = ((), (), s32[]{:S(2)}) async-start(), calls=%async_computation.2 | async-start | bytes 9732096 | tf_op jit(solution)/shard_map/reduce_scatter | solution.py:148
  279.0 5.1 %copy-start.3 = (bf16[1024,1536]{1,0:T(8,128)(2,1)S(1)}, bf16[1024,1536]{1,0:T(8,128)(2,1)}, u32[]{:S(2)}) copy-start(bf16[1024,1536]{1,0:T(8,128)(2,1)} %copy-done.2) | copy-start | bytes 9437188
  291.8 193.1 %reduce-scatter.5.cloned.1.call-start = ((), (), s32[]{:S(2)}) async-start(), calls=%async_computation.3 | async-start | bytes 9732096 | tf_op jit(solution)/shard_map/reduce_scatter | solution.py:135
  302.9 0.7 copy-start.7
  302.9 0.7 copy-start.9
Sparse Core Ops, SparseCore 0:
  144.4 100.9 all-reduce.4
  291.9 93.2 reduce-scatter.2
  390.0 94.7 reduce-scatter.4
where the time goes:
time: 493 us; the launch traced here: 491 us
  blocking collectives  216 us (44%)
  waiting for transfers between devices  147 us (30%)
  matrix products  65.3 us (13%)
  local copies, waits for them, and re-layouts  23.2 us (5%)
  other arithmetic  23.1 us (5%)
  between operations  16.6 us (3%)
    psum x1, blocking collectives, on_device(): slide_embed = lax.psum(partial_value, 'tile')  125 us
    unnamed x4, waiting for transfers between devices  96.2 us
    reduce_scatter x1, waiting for transfers between devices, on_device(): lax.psum_scatter(out_term, 'tile', scatter_dimension=0, tiled=True)  50.8 us
    all_gather x1, blocking collectives, on_device(): lax.all_gather(own_qkv[:, slide_width:2 * slide_width], 'tile', axis=0, t...  28.6 us
    all_gather x1, blocking collectives, on_device(): lax.all_gather(own_qkv[:, 2 * slide_width:], 'tile', axis=0, tiled=True)  25.8 us
    psum x1, blocking collectives, on_device(): branch_term = lax.psum(branch_part, 'slide')  18.6 us
    psum x1, blocking collectives, on_device(): d_embed = lax.psum(d_part, 'slide')  18.2 us
    dot_general x1, matrix products, on_device(): lax.dot_general(pooled, d_embed, (((0,), (0,)), ((), ())), precision=lax....  10.8 us
  transfers between devices with their start and end apart: 3, of which 2 were waited for; matrix products, arithmetic and copies ran while one was open for 4% of the time, Pallas kernels for 0%

commit v1 on v0

v1 whole, which is shorter than its diff:
```python
import math

import jax
import jax.numpy as jnp
from jax import lax
from jax.experimental import pallas as pl
from jax.experimental.pallas import tpu as pltpu
from jax.sharding import PartitionSpec as P

HEADS = 16
EPSILON = 1e-06
MIB = 1 << 20
BF = jnp.bfloat16
F4 = jnp.float32


def dot_nn(a, b):
    return lax.dot_general(a, b, (((1,), (0,)), ((), ())), preferred_element_type=F4)


def dot_nt(a, b):
    return lax.dot_general(a, b, (((1,), (1,)), ((), ())), preferred_element_type=F4)


def dot_tn(a, b):
    return lax.dot_general(a, b, (((0,), (0,)), ((), ())), preferred_element_type=F4)


def halves(value):
    high = value.astype(BF)
    return high, (value - high.astype(F4)).astype(BF)


def standardise(values):
    width = values.shape[1]
    centre = jnp.sum(values, axis=1, keepdims=True) * (1.0 / width)
    shifted = values - centre
    spread = jnp.sum(shifted * shifted, axis=1, keepdims=True) * (1.0 / width)
    return shifted * lax.rsqrt(spread + EPSILON)


def gelu_pair(a):
    bell = jnp.exp(a * a * -0.5)
    t = 1.0 / (1.0 + jnp.abs(a) * (0.3275911 * 0.7071067811865476))
    series = t * (0.127414796 + t * (-0.142248368 + t * (0.7107068705 + t * (-0.7265760135 + t * 0.5307027145))))
    tail = series * bell
    phi = jnp.where(a < 0.0, tail, 1.0 - tail)
    return a * phi, phi + a * (bell * 0.3989422804014327)


def forward_kernel(tiles, w_in, w_out, cot, slope, pooled, shared, token_mean, normed, total):
    step = pl.program_id(0)
    tile_count = token_mean.shape[0]
    patches = tiles.shape[0] // tile_count

    @pl.when(step == 0)
    def _():
        for tile in range(tile_count):
            rows = pl.ds(tile * patches, patches)
            values = tiles[rows, :].astype(F4)
            token_mean[pl.ds(tile, 1), :] = jnp.sum(values, axis=0, keepdims=True) * (1.0 / patches)
            normed[rows, :] = standardise(values).astype(BF)
        total[...] = jnp.zeros_like(total)

    means = []
    for tile in range(tile_count):
        rows = pl.ds(tile * patches, patches)
        value, rate = gelu_pair(dot_nn(normed[rows, :], w_in[...]))
        slope[rows, :] = rate.astype(BF)
        means.append(jnp.sum(value, axis=0, keepdims=True) * (1.0 / patches))
    high, low = halves(jnp.concatenate(means, axis=0))
    both = jnp.concatenate([high, low], axis=0)
    pooled[...] = both
    total[...] += dot_nn(both, w_out[...])

    @pl.when(step == pl.num_programs(0) - 1)
    def _():
        width = total.shape[1]
        shared[:, :width] = total[:tile_count, :] + total[tile_count:, :]
        shared[:, width:] = cot[...]


def forward(tiles, w_in, w_out, cot, tile_count):
    tokens, width = tiles.shape
    hidden = w_in.shape[1]
    block = 256
    slide_width = cot.shape[1]
    return pl.pallas_call(
        forward_kernel,
        grid=(hidden // block,),
        in_specs=[
            pl.BlockSpec((tokens, width), lambda j: (0, 0)),
            pl.BlockSpec((width, block), lambda j: (0, j)),
            pl.BlockSpec((block, width), lambda j: (j, 0)),
            pl.BlockSpec((tile_count, slide_width), lambda j: (0, 0)),
        ],
        out_specs=[
            pl.BlockSpec((tokens, block), lambda j: (0, j)),
            pl.BlockSpec((2 * tile_count, block), lambda j: (0, j)),
            pl.BlockSpec((tile_count, width + slide_width), lambda j: (0, 0)),
            pl.BlockSpec((tile_count, width), lambda j: (0, 0)),
        ],
        out_shape=[
            jax.ShapeDtypeStruct((tokens, hidden), BF),
            jax.ShapeDtypeStruct((2 * tile_count, hidden), BF),
            jax.ShapeDtypeStruct((tile_count, width + slide_width), F4),
            jax.ShapeDtypeStruct((tile_count, width), F4),
        ],
        scratch_shapes=[pltpu.VMEM((tokens, width), BF), pltpu.VMEM((2 * tile_count, width), F4)],
        compiler_params=pltpu.CompilerParams(vmem_limit_bytes=40 * MIB),
        name="forward",
    )(tiles, w_in, w_out, cot)


def transpose_kernel(place_a, place_b, tiles, out_a, out_b):
    normed_t = standardise(tiles[...].astype(F4)).astype(BF).T
    rows = out_a.shape[0] // place_a.shape[0]
    for block in range(place_a.shape[0]):
        piece = normed_t[block * rows : (block + 1) * rows, :]
        out_a[pl.ds(pl.multiple_of(place_a[block] * rows, 16), rows), :] = piece
        out_b[pl.ds(pl.multiple_of(place_b[block] * rows, 16), rows), :] = piece


def transposed(tiles, place_a, place_b, patches):
    tokens, width = tiles.shape
    spec = pl.BlockSpec((width, patches), lambda i: (0, i))
    return pl.pallas_call(
        transpose_kernel,
        grid=(tokens // patches,),
        in_specs=[
            pl.BlockSpec(memory_space=pltpu.SMEM),
            pl.BlockSpec(memory_space=pltpu.SMEM),
            pl.BlockSpec((patches, width), lambda i: (i, 0)),
        ],
        out_specs=[spec, spec],
        out_shape=[jax.ShapeDtypeStruct((width, tokens), BF)] * 2,
        compiler_params=pltpu.CompilerParams(vmem_limit_bytes=24 * MIB),
        cost_estimate=pl.CostEstimate(flops=20_000_000, bytes_accessed=9_000_000, transcendentals=0),
        name="transposed",
    )(place_a, place_b, tiles)


def embed_kernel(place, own, one, two, three, token_mean, counts, pooled, out, cot_all):
    width = token_mean.shape[1]
    half = width // 2
    total = (own[:, :width] + two[:, :width]) + (one[:, :width] + three[:, :width])
    embedding = total + token_mean[...]
    eight = jnp.concatenate([embedding[:, :half], embedding[:, half:]], axis=0)
    out[:, :half] = jnp.concatenate([eight] * (out.shape[0] // 8), axis=0).astype(BF)
    out[:, half:] = pooled[...]
    parts = [own[:, width:], one[:, width:], two[:, width:], three[:, width:]]
    blocks = []
    for group in range(4):
        back = jnp.bitwise_and(place[0] - group, 3)
        block = parts[0]
        for shift in range(1, 4):
            block = jnp.where(back == shift, parts[shift], block)
        blocks.append(block)
    cot_all[...] = jnp.concatenate(blocks, axis=0) / counts[...].astype(F4)


def embed(place, parts, token_mean, counts, pooled, peers):
    tile_count, width = token_mean.shape
    slide_width = parts[0].shape[1] - width
    return pl.pallas_call(
        embed_kernel,
        in_specs=[pl.BlockSpec(memory_space=pltpu.SMEM)] + [pl.BlockSpec(memory_space=pltpu.VMEM)] * 7,
        out_shape=[
            jax.ShapeDtypeStruct((peers * 8, width // 2 + 128), BF),
            jax.ShapeDtypeStruct((16, slide_width), F4),
        ],
        name="embed",
    )(place, *parts, token_mean, counts, pooled)


def attention_kernel(
    place,
    seg_len,
    gathered,
    w_proj_hbm,
    w_qkv_hbm,
    w_attn_hbm,
    w_out_hbm,
    cot_all,
    slide_of,
    order_of,
    d_pooled,
    d_embed,
    context,
    slide_rows,
    pooled_pair,
    w_proj,
    w_qkv,
    w_attn,
    w_out,
    d_qkv,
    sems,
):
    copies = [
        pltpu.make_async_copy(src, dst, sems.at[i])
        for i, (src, dst) in enumerate(
            [(w_proj_hbm, w_proj), (w_qkv_hbm, w_qkv), (w_attn_hbm, w_attn), (w_out_hbm, w_out)]
        )
    ]
    for copy in copies:
        copy.start()
    tiles = slide_of.shape[1]
    half = w_proj.shape[0] // 2
    width = w_proj.shape[1]
    head = width // HEADS

    row = lax.broadcasted_iota(jnp.int32, (tiles, 2 * tiles), 0)
    col = lax.broadcasted_iota(jnp.int32, (tiles, 2 * tiles), 1)
    first = (row // 4) * 8 + row % 4
    every = gathered[...]
    left = dot_nn((col == first).astype(F4).astype(BF), every).astype(BF)
    right = dot_nn((col == first + 4).astype(F4).astype(BF), every).astype(BF)
    pooled_pair[:, :128] = left[:, half:]
    pooled_pair[:, 128:] = right[:, half:]

    slide = slide_of[...].astype(F4)
    order = order_of[...].astype(F4)
    weight = jnp.zeros((tiles, tiles), F4)
    for branch in range(3):
        length = seg_len[branch].astype(F4)
        block = jnp.floor((order + 0.5) / length)
        dilation = float(2**branch)
        phase = order - dilation * jnp.floor(order * (1.0 / dilation))
        code = jnp.broadcast_to((slide * 64.0 + block) * 4.0 + phase, (tiles, tiles))
        weight = weight + (code == code.T).astype(F4)
    slide_col = jnp.broadcast_to(slide, (tiles, tiles)).T
    lane = lax.broadcasted_iota(jnp.int32, (tiles, 16), 1).astype(F4)
    member = (slide_col[:, :16] == lane).astype(F4).astype(BF)
    cot_high, cot_low = halves(cot_all[...])
    d_attended = dot_nn(member, cot_high) + dot_nn(member, cot_low)

    copies[0].wait()
    rows = (dot_nn(left[:, :half], w_proj[:half, :]) + dot_nn(right[:, :half], w_proj[half:, :])).astype(BF)
    slide_rows[...] = rows
    copies[1].wait()
    qkv = dot_nn(rows, w_qkv[...]).astype(BF)
    copies[2].wait()
    d_context = dot_nt(d_attended.astype(BF), w_attn[...]).astype(BF)

    scale = 1.0 / math.sqrt(head)
    sums = {}

    def accumulate(name, start, value):
        for offset in range(0, value.shape[1], 128):
            key = (name, (start + offset) // 128)
            piece = value[:, offset : offset + 128]
            sums[key] = sums[key] + piece if key in sums else piece

    for index in range(HEADS):
        low = index * head
        start = low // 128 * 128
        stop = -(-(low + head) // 128) * 128
        place_in = lax.broadcasted_iota(jnp.int32, (1, stop - start), 1) + start
        mask = ((place_in >= low) & (place_in < low + head)).astype(F4)
        mask_bf = mask.astype(BF)
        query = qkv[:, start:stop] * mask_bf
        key_rows = qkv[:, width + start : width + stop]
        value_rows = qkv[:, 2 * width + start : 2 * width + stop]
        d_out = d_context[:, start:stop] * mask_bf
        scores = jnp.where(weight > 0.0, dot_nt(query, key_rows) * scale, -1e30)
        numerator = weight * jnp.exp(scores - jnp.max(scores, axis=1, keepdims=True))
        share = numerator * (1.0 / jnp.sum(numerator, axis=1, keepdims=True))
        d_share = dot_nt(d_out, value_rows)
        d_scores = share * (d_share - jnp.sum(share * d_share, axis=1, keepdims=True)) * scale
        share = share.astype(BF)
        d_scores = d_scores.astype(BF)
        accumulate("context", start, dot_nn(share, value_rows) * mask)
        accumulate("query", start, dot_nn(d_scores, key_rows) * mask)
        accumulate("key", start, dot_tn(d_scores, query))
        accumulate("value", start, dot_tn(share, d_out))
    for tile in range(width // 128):
        context[:, 128 * tile : 128 * (tile + 1)] = sums["context", tile]
        for part, name in enumerate(("query", "key", "value")):
            at = part * width + 128 * tile
            d_qkv[:, at : at + 128] = sums[name, tile].astype(BF)

    d_slide = d_attended + dot_nt(d_qkv[...], w_qkv[...])
    d_embed[...] = dot_nt(d_slide.astype(BF), w_proj[...])
    copies[3].wait()
    eight = d_embed[pl.ds(pl.multiple_of(place[1] // 2 * 8, 8), 8), :]
    high, low = halves(eight)
    back = dot_nt(high, w_out[...]) + dot_nt(low, w_out[...])
    d_pooled[...] = jnp.where(place[1] % 2 == 0, back[:4, :], back[4:, :]) * (1.0 / 256.0)


def attention(place, seg_len, gathered, w_proj, w_qkv, w_attn, w_out, cot_all, slide_of, order_of):
    tiles = slide_of.shape[1]
    width, slide_width = w_proj.shape
    hidden = w_out.shape[0]
    smem = pl.BlockSpec(memory_space=pltpu.SMEM)
    vmem = pl.BlockSpec(memory_space=pltpu.VMEM)
    hbm = pl.BlockSpec(memory_space=pl.ANY)
    return pl.pallas_call(
        attention_kernel,
        in_specs=[smem, smem, vmem, hbm, hbm, hbm, hbm, vmem, vmem, vmem],
        out_shape=[
            jax.ShapeDtypeStruct((4, hidden), F4),
            jax.ShapeDtypeStruct((tiles, width), F4),
            jax.ShapeDtypeStruct((tiles, slide_width), F4),
            jax.ShapeDtypeStruct((tiles, slide_width), BF),
            jax.ShapeDtypeStruct((tiles, 256), BF),
        ],
        scratch_shapes=[
            pltpu.VMEM(w_proj.shape, BF),
            pltpu.VMEM(w_qkv.shape, BF),
            pltpu.VMEM(w_attn.shape, BF),
            pltpu.VMEM(w_out.shape, BF),
            pltpu.VMEM((tiles, 3 * slide_width), BF),
            pltpu.SemaphoreType.DMA((4,)),
        ],
        compiler_params=pltpu.CompilerParams(vmem_limit_bytes=40 * MIB),
        name="attention",
    )(place, seg_len, gathered, w_proj, w_qkv, w_attn, w_out, cot_all, slide_of, order_of)


def outputs_kernel(place, context, slide_rows, w_attn, slide_of, counts, pooled_pair, d_embed, slide_embed, grad_out):
    tiles = slide_of.shape[1]
    high, low = halves(context[...])
    attended = slide_rows[...].astype(F4) + dot_nn(high, w_attn[...]) + dot_nn(low, w_attn[...])
    group = lax.broadcasted_iota(jnp.int32, (16, tiles), 0)
    member = (slide_of[...] == group).astype(F4).astype(BF)
    high, low = halves(attended)
    sums = (dot_nn(member, high) + dot_nn(member, low)) / counts[...].astype(F4)
    own = sums[0:4, :]
    for index in range(1, 4):
        own = jnp.where(place[0] == index, sums[4 * index : 4 * index + 4, :], own)
    slide_embed[...] = own
    high, low = halves(d_embed[...])
    pair = pooled_pair[...]
    both = dot_tn(pair, high) + dot_tn(pair, low)
    rows = grad_out.shape[0]
    grad_out[...] = both[:rows, :] + both[128 : 128 + rows, :]


def outputs(place, context, slide_rows, w_attn, slide_of, counts, pooled_pair, d_embed, rows):
    slide_width = w_attn.shape[0]
    width = d_embed.shape[1]
    return pl.pallas_call(
        outputs_kernel,
        in_specs=[pl.BlockSpec(memory_space=pltpu.SMEM)] + [pl.BlockSpec(memory_space=pltpu.VMEM)] * 7,
        out_shape=[jax.ShapeDtypeStruct((4, slide_width), F4), jax.ShapeDtypeStruct((rows, width), F4)],
        compiler_params=pltpu.CompilerParams(vmem_limit_bytes=16 * MIB),
        cost_estimate=pl.CostEstimate(flops=1_000_000_000, bytes_accessed=4_000_000, transcendentals=0),
        name="outputs",
    )(place, context, slide_rows, w_attn, slide_of, counts, pooled_pair, d_embed)


def grad_kernel(normed_t, slope, d_pooled, send, keep):
    tile_count = d_pooled.shape[0]
    patches = slope.shape[0] // tile_count
    parts = []
    for tile in range(tile_count):
        rate = slope[pl.ds(tile * patches, patches), :].astype(F4)
        parts.append((rate * d_pooled[pl.ds(tile, 1), :]).astype(BF))
    d_preact = jnp.concatenate(parts, axis=0)
    rows = send.shape[0]
    send[...] = dot_nn(normed_t[:rows, :], d_preact).astype(BF)
    keep[...] = dot_nn(normed_t[rows:, :], d_preact).astype(BF)


def grad_half(normed_t, slope, d_pooled, which, block=256):
    width, tokens = normed_t.shape
    hidden = slope.shape[1] // 2
    steps = hidden // block
    out = pl.BlockSpec((width // 2, block), lambda j: (0, j))
    return pl.pallas_call(
        grad_kernel,
        grid=(steps,),
        in_specs=[
            pl.BlockSpec((width, tokens), lambda j: (0, 0)),
            pl.BlockSpec((tokens, block), lambda j: (0, j + which * steps)),
            pl.BlockSpec((d_pooled.shape[0], block), lambda j: (0, j + which * steps)),
        ],
        out_specs=[out, out],
        out_shape=[jax.ShapeDtypeStruct((width // 2, hidden), BF)] * 2,
        compiler_params=pltpu.CompilerParams(vmem_limit_bytes=24 * MIB),
        cost_estimate=pl.CostEstimate(flops=2 * width * tokens * hidden, bytes_accessed=7_000_000, transcendentals=0),
        name="grad_half",
    )(normed_t, slope, d_pooled)


def add_pair_kernel(keep, received, *outs):
    rows = outs[0].shape[0]
    for index, out in enumerate(outs):
        at = pl.ds(index * rows, rows)
        out[...] = (keep[at, :].astype(F4) + received[at, :].astype(F4)).astype(BF)


def add_pair(keep, received):
    rows, columns = keep.shape
    return pl.pallas_call(
        add_pair_kernel,
        out_shape=[jax.ShapeDtypeStruct((rows // 4, columns), BF)] * 4,
        compiler_params=pltpu.CompilerParams(vmem_limit_bytes=16 * MIB),
        name="add_pair",
    )(keep, received)


def add_four_kernel(one, two, three, four, *outs):
    rows = outs[0].shape[0]
    for index, out in enumerate(outs):
        at = pl.ds(index * rows, rows)
        total = (one[at, :].astype(F4) + two[at, :].astype(F4)) + (three[at, :].astype(F4) + four[at, :].astype(F4))
        out[...] = total.astype(BF)


def add_four(parts):
    rows, columns = parts[0].shape
    return pl.pallas_call(
        add_four_kernel,
        out_shape=[jax.ShapeDtypeStruct((rows // 4, columns), BF)] * 4,
        compiler_params=pltpu.CompilerParams(vmem_limit_bytes=16 * MIB),
        name="add_four",
    )(*parts)


def finish_kernel(*refs):
    out = refs[-1]
    half = out.shape[1] // 2
    for side in range(2):
        one, two, three, four = [ref[...].astype(F4) for ref in refs[4 * side : 4 * side + 4]]
        out[:, side * half : (side + 1) * half] = (one + two) + (three + four)


def finish(parts):
    rows, columns = parts[0].shape
    return pl.pallas_call(
        finish_kernel,
        out_shape=jax.ShapeDtypeStruct((rows, 2 * columns), F4),
        name="finish",
    )(*parts)


def moved(value, dz, dx, dc):
    pairs = []
    for z in range(4):
        for x in range(4):
            for c in range(2):
                pairs.append(((z * 4 + x) * 2 + c, ((z + dz) % 4 * 4 + (x + dx) % 4) * 2 + (c + dc) % 2))
    return lax.ppermute(value, "tile", pairs)


def on_device(
    tiles,
    w_in,
    w_out,
    w_proj,
    w_qkv,
    w_attn_out,
    slide_of_tile,
    order_of_tile,
    slide_counts,
    seg_len,
    slide_cot,
):
    tile_count, patches, width = tiles.shape
    hidden = w_in.shape[1]
    peers = 32
    flat = tiles.reshape(tile_count * patches, width)
    tile_pos = lax.axis_index("tile")
    slide_pos = lax.axis_index("slide")
    place = jnp.stack([slide_pos, tile_pos]).astype(jnp.int32)
    counts = slide_counts.reshape(-1, 1)
    slide_of = slide_of_tile.reshape(1, -1)
    order_of = order_of_tile.reshape(1, -1)

    block = jnp.arange(peers, dtype=jnp.int32)
    z, x, c = block // 8, block // 2 % 4, block % 2
    dz = (z - tile_pos // 8) % 4
    dx = (x - tile_pos // 2 % 4) % 4
    stay = (c == tile_pos % 2).astype(jnp.int32)
    place_a = (stay * 16 + dx * 4 + dz).astype(jnp.int32)
    place_b = (stay * 16 + dz * 4 + dx).astype(jnp.int32)

    slope, pooled, shared, token_mean = forward(flat, w_in, w_out, slide_cot, tile_count)
    parts = [shared] + [
        lax.ppermute(shared, "slide", [(i, (i + k) % 4) for i in range(4)]) for k in (1, 2, 3)
    ]
    order_a, order_b = transposed(flat, place_a, place_b, patches)
    slices = pooled.reshape(2 * tile_count, peers, hidden // peers).transpose(1, 0, 2)
    slices = jnp.pad(slices.reshape(peers * 2 * tile_count, -1), ((0, 0), (0, 128 - hidden // peers)))
    mine, cot_all = embed(place, parts, token_mean, counts, slices, peers)
    gathered = lax.all_to_all(
        mine.reshape(peers, 8, -1), "tile", split_axis=0, concat_axis=0, tiled=True
    ).reshape(peers * 8, -1)
    d_pooled, d_embed, context, slide_rows, pooled_pair = attention(
        place, seg_len, gathered, w_proj, w_qkv, w_attn_out, w_out, cot_all, slide_of, order_of
    )
    send_a, keep_a = grad_half(order_a, slope, d_pooled, 0)
    send_b, keep_b = grad_half(order_b, slope, d_pooled, 1)
    a = add_pair(keep_a, moved(send_a, 0, 0, 1))
    b = add_pair(keep_b, moved(send_b, 0, 0, 1))
    a = add_four([a[0]] + [moved(a[k], 0, k, 0) for k in (1, 2, 3)])
    b = add_four([b[0]] + [moved(b[k], k, 0, 0) for k in (1, 2, 3)])
    slide_embed, grad_out = outputs(
        place, context, slide_rows, w_attn_out, slide_of, counts, pooled_pair, d_embed, hidden // peers
    )
    a = [a[0]] + [moved(a[k], k, 0, 0) for k in (1, 2, 3)]
    b = [b[0]] + [moved(b[k], 0, k, 0) for k in (1, 2, 3)]
    return (slide_embed, finish(a + b), grad_out)


def solution(mesh):
    placed = (
        P("tile", None, None),
        P(None, "slide"),
        P("slide", None),
        P(),
        P(),
        P(),
        P(),
        P(),
        P(),
        P(),
        P("slide", None),
    )
    return jax.shard_map(
        on_device,
        mesh=mesh,
        in_specs=placed,
        out_specs=(P("slide", None), P("tile", "slide"), P(("slide", "tile"), None)),
        check_vma=False,
    )
```

time: 493 us -> 121 us (0.25)
  blocking collectives: 216 us -> 0 us
  waiting for transfers between devices: 147 us -> 18.9 us
  matrix products: 65.3 us -> 0 us
  Pallas kernels: 0 us -> 49.5 us
  starting transfers between devices: 0.34 us -> 29.5 us
  other arithmetic: 23.1 us -> 0.63 us
  between operations: 16.6 us -> 0.96 us
    psum x3 -> x0, blocking collectives: 162 us -> none  [the longest x1 125 us: on_device(): slide_embed = lax.psum(partial_value, 'tile')]
    unnamed x4 -> x0, waiting for transfers between devices: 96.2 us -> none
    dot_general x19 -> x0, matrix products: 65.3 us -> none  [the longest x1 10.8 us: on_device(): lax.dot_general(pooled, d_embed, (((0,), (0,)), ((), ())), precision=lax....]
    all_gather x2 -> x0, blocking collectives: 54.4 us -> none  [the longest x1 28.6 us: on_device(): lax.all_gather(own_qkv[:, slide_width:2 * slide_width], 'tile', axis=0, t...]
    reduce_scatter x2 -> x0, waiting for transfers between devices: 50.8 us -> none  [the longest x1 50.8 us: on_device(): lax.psum_scatter(out_term, 'tile', scatter_dimension=0, tiled=True)]
    pallas_call x0 -> x12, Pallas kernels: none -> 49.5 us  [the longest x1 16.6 us: attention(): pl.pallas_call(attention_kernel, in_specs=[smem, smem, vmem, hbm, hbm, hb...]
    ppermute x0 -> x17, starting transfers between devices: none -> 20.9 us  [the longest x14 16.2 us: moved(): return lax.ppermute(value, 'tile', pairs)]
    ppermute x0 -> x17, waiting for transfers between devices: none -> 15.7 us  [the longest x14 13.6 us: moved(): return lax.ppermute(value, 'tile', pairs)]
  transfers between devices with their start and end apart: 3 -> 18, of which waited for: 2 -> 7; matrix products, arithmetic and copies ran while one was open for 4% -> 2% of each run, Pallas kernels for 0% -> 9%
where the time goes in v1:
time: 121 us
  Pallas kernels  49.5 us (41%)
  starting transfers between devices  29.5 us (24%)
  local copies, waits for them, and re-layouts  21.2 us (18%)
  waiting for transfers between devices  18.9 us (16%)
    unnamed x68, local copies, waits for them, and re-layouts  19.7 us
    pallas_call x1, Pallas kernels, attention(): pl.pallas_call(attention_kernel, in_specs=[smem, smem, vmem, hbm, hbm, hb...  16.6 us
    ppermute x14, starting transfers between devices, moved(): return lax.ppermute(value, 'tile', pairs)  16.2 us
    pallas_call x1, Pallas kernels, forward(): pl.pallas_call(forward_kernel, grid=(hidden // block,), in_specs=[pl.Bloc...  15.3 us
    ppermute x14, waiting for transfers between devices, moved(): return lax.ppermute(value, 'tile', pairs)  13.6 us
    all_to_all x1, starting transfers between devices, on_device(): lax.all_to_all(mine.reshape(peers, 8, -1), 'tile', split_axis=0, concat_a...  8.59 us
    pallas_call x2, Pallas kernels, grad_half(): pl.pallas_call(grad_kernel, grid=(steps,), in_specs=[pl.BlockSpec((width,...  6.48 us
    ppermute x3, starting transfers between devices, on_device(): lax.ppermute(shared, 'slide', [(i, (i + k) % 4) for i in range(4)])  4.69 us
  transfers between devices with their start and end apart: 18, of which 7 were waited for; matrix products, arithmetic and copies ran while one was open for 2% of the time, Pallas kernels for 9%

profile of v1, /device:TPU:0, one launch (start us, length us, event | category | flops | bytes accessed | tf_op | source)
XLA Modules:
  0.0 120.7 jit_solution(9594382664003277759)
XLA Ops:
  0.6 1.9 %copy-done.1 = bf16[4,256,1536]{2,1,0:T(8,128)(2,1)S(1)} copy-done((bf16[4,256,1536]{2,1,0:T(8,128)(2,1)S(1)}, bf16[4,256,1536]{2,1,0:T(8,128)(2,1)}, u32[]{:S(2)}) %copy-start.1) | copy-done | bytes 3145752
  2.5 2.3 %copy-done.3 = bf16[1536,1536]{1,0:T(8,128)(2,1)S(1)} copy-done((bf16[1536,1536]{1,0:T(8,128)(2,1)S(1)}, bf16[1536,1536]{1,0:T(8,128)(2,1)}, u32[]{:S(2)}) %copy-start.3) | copy-done | bytes 4718616
  5.6 15.3 %forward.1 = (bf16[1024,1536]{1,0:T(8,128)(2,1)S(1)}, bf16[8,1536]{1,0:T(8,128)(2,1)S(1)}, f32[4,2304]{1,0:T(4,128)S(1)}, f32[4,1536]{1,0:T(4,128)S(1)}) custom-call(bf16[1024,1536]{1,0:T(8,128)(2,1)S(1)} %bitcast.13, bf16[1536,1536]{1,0:T(8,128)(2,1)S(1)} %copy-done.3, bf16[1536,1536]{1,0:T(8,128)(2,1)} %w_out_hbm.1, f32[4,768]{1,0:T(4,128)S(1)} %copy-done.13), custom_call_target="tpu_custom_call" | custom-call | tf_op jit(solution)/shard_map/forward/pallas_call | solution.py:88
  21.5 1.6 %copy-done.18 = bf16[1024,1536]{1,0:T(8,128)(2,1)} copy-done((bf16[1024,1536]{1,0:T(8,128)(2,1)}, bf16[1024,1536]{1,0:T(8,128)(2,1)S(1)}, u32[]{:S(2)}) %copy-start.18) | copy-done | bytes 3145752
  23.1 3.1 %collective-permute-start.2 = (f32[4,2304]{1,0:T(4,128)S(1)}, f32[4,2304]{1,0:T(4,128)S(1)}, u32[]{:S(2)}, u32[]{:S(2)}) collective-permute-start(f32[4,2304]{1,0:T(4,128)S(1)} %get-tuple-element.38.own), channel_id=1, source_target_pairs={{0,96},{32,0},{64,32},{96,64},{1,97},{33,1},{65,33},{97,65},{2,98}... | collective-permute-start | bytes 110600 | tf_op jit(solution)/shard_map/ppermute | solution.py:482
  26.8 1.0 collective-permute-start
  29.9 1.7 %collective-permute-done.1.two = f32[4,2304]{1,0:T(4,128)S(1)} collective-permute-done((f32[4,2304]{1,0:T(4,128)S(1)}, f32[4,2304]{1,0:T(4,128)S(1)}, u32[]{:S(2)}, u32[]{:S(2)}) %collective-permute-start.1) | collective-permute-done | bytes 36896 | tf_op jit(solution)/shard_map/ppermute | solution.py:482
  32.7 1.8 %embed.1 = (bf16[256,896]{1,0:T(8,128)(2,1)}, f32[16,768]{1,0:T(8,128)}) custom-call(s32[2]{0:T(128)} %pad_add_fusion.place, f32[4,2304]{1,0:T(4,128)} %copy-done.10, f32[4,2304]{1,0:T(4,128)} %copy-done.32, f32[4,2304]{1,0:T(4,128)} %copy-done.31, f32[4,2304]{1,0:T(4,128)} %copy-done.30, f32[4,1536]{1,0:T(4,128)} %copy-done.12, s32[16,1]{1,0:T(8,128)} %copy.15.counts, ...), custom_call_target="tpu_custom_call" | custom-call | tf_op jit(solution)/shard_map/embed/pallas_call | solution.py:165
  34.5 8.6 %all-to-all-start = ((bf16[32,8,896]{2,1,0:T(8,128)(2,1)}), bf16[32,8,896]{2,1,0:T(8,128)(2,1)}, u32[]{:S(2)}, u32[]{:S(2)}) async-start(bf16[32,8,896]{2,1,0:T(8,128)(2,1)} %bitcast.18), calls=%async_computation | async-start | bytes 917504 | tf_op jit(solution)/shard_map/all_to_all | solution.py:488
  43.1 4.2 %transposed.1 = (bf16[1536,1024]{1,0:T(8,128)(2,1)S(1)}, bf16[1536,1024]{1,0:T(8,128)(2,1)S(1)}) custom-call(s32[32]{0:T(128)S(1)} %get-tuple-element.74.place_a, s32[32]{0:T(128)S(1)} %get-tuple-element.73.place_b, bf16[1024,1536]{1,0:T(8,128)(2,1)S(1)} %bitcast.14), custom_call_target="tpu_custom_call" | custom-call | flops 20000000 | bytes 9000000 | tf_op jit(solution)/shard_map/transposed/pallas_call | solution.py:127
  47.3 1.7 %copy-done.20 = bf16[1536,1024]{1,0:T(8,128)(2,1)} copy-done((bf16[1536,1024]{1,0:T(8,128)(2,1)}, bf16[1536,1024]{1,0:T(8,128)(2,1)S(1)}, u32[]{:S(2)}) %copy-start.20) | copy-done | bytes 3145752
  49.0 1.7 %copy-done.22 = bf16[1536,1024]{1,0:T(8,128)(2,1)} copy-done((bf16[1536,1024]{1,0:T(8,128)(2,1)}, bf16[1536,1024]{1,0:T(8,128)(2,1)S(1)}, u32[]{:S(2)}) %copy-start.22) | copy-done | bytes 3145752
  50.7 3.2 %all-to-all-done = bf16[32,8,896]{2,1,0:T(8,128)(2,1)} async-done(((bf16[32,8,896]{2,1,0:T(8,128)(2,1)}), bf16[32,8,896]{2,1,0:T(8,128)(2,1)}, u32[]{:S(2)}, u32[]{:S(2)}) %all-to-all-start) | async-done | bytes 458784 | tf_op jit(solution)/shard_map/all_to_all | solution.py:488
  53.9 2.3 %copy-done = bf16[1536,1536]{1,0:T(8,128)(2,1)S(1)} copy-done((bf16[1536,1536]{1,0:T(8,128)(2,1)S(1)}, bf16[1536,1536]{1,0:T(8,128)(2,1)}, u32[]{:S(2)}) %copy-start) | copy-done | bytes 4718616
  56.2 2.0 %copy-done.4 = bf16[768,2304]{1,0:T(8,128)(2,1)S(1)} copy-done((bf16[768,2304]{1,0:T(8,128)(2,1)S(1)}, bf16[768,2304]{1,0:T(8,128)(2,1)}, u32[]{:S(2)}) %copy-start.4) | copy-done | bytes 3538968
  58.2 1.7 %copy-done.5 = bf16[1536,768]{1,0:T(8,128)(2,1)S(1)} copy-done((bf16[1536,768]{1,0:T(8,128)(2,1)S(1)}, bf16[1536,768]{1,0:T(8,128)(2,1)}, u32[]{:S(2)}) %copy-start.5) | copy-done | bytes 2359320
  59.9 1.3 %copy-done.6 = bf16[768,768]{1,0:T(8,128)(2,1)S(1)} copy-done((bf16[768,768]{1,0:T(8,128)(2,1)S(1)}, bf16[768,768]{1,0:T(8,128)(2,1)}, u32[]{:S(2)}) %copy-start.6) | copy-done | bytes 1179672
  61.2 16.6 %attention.1 = (f32[4,1536]{1,0:T(4,128)S(1)}, f32[128,1536]{1,0:T(8,128)S(1)}, f32[128,768]{1,0:T(8,128)S(1)}, bf16[128,768]{1,0:T(8,128)(2,1)S(1)}, bf16[128,256]{1,0:T(8,128)(2,1)S(1)}) custom-call(s32[2]{0:T(128)S(1)} %copy-done.14, s32[3]{0:T(128)S(1)} %copy-done.15, bf16[256,896]{1,0:T(8,128)(2,1)} %bitcast.7.gathered, ...), custom_call_target="tpu_custom_call" | custom-call | tf_op jit(solution)/shard_map/attention/pallas_call | solution.py:298
  77.8 3.2 %grad_half.2 = (bf16[768,768]{1,0:T(8,128)(2,1)S(1)}, bf16[768,768]{1,0:T(8,128)(2,1)S(1)}) custom-call(bf16[1536,1024]{1,0:T(8,128)(2,1)S(1)} %copy-done.23, bf16[1024,1536]{1,0:T(8,128)(2,1)S(1)} %copy-done.19, f32[4,1536]{1,0:T(4,128)S(1)} %get-tuple-element.50.d_pooled), custom_call_target="tpu_custom_call" | custom-call | flops 2415919104 | bytes 7000000 | tf_op jit(solution)/shard_map/grad_half/pallas_call | solution.py:371
  81.2 3.2 %grad_half.3 = (bf16[768,768]{1,0:T(8,128)(2,1)S(1)}, bf16[768,768]{1,0:T(8,128)(2,1)S(1)}) custom-call(bf16[1536,1024]{1,0:T(8,128)(2,1)S(1)} %copy-done.21, bf16[1024,1536]{1,0:T(8,128)(2,1)S(1)} %copy-done.19, f32[4,1536]{1,0:T(4,128)S(1)} %get-tuple-element.50.d_pooled), custom_call_target="tpu_custom_call" | custom-call | flops 2415919104 | bytes 7000000 | tf_op jit(solution)/shard_map/grad_half/pallas_call | solution.py:371
  85.9 2.1 %collective-permute-start.5 = (bf16[192,768]{1,0:T(8,128)(2,1)S(1)}, bf16[192,768]{1,0:T(8,128)(2,1)S(1)}, u32[]{:S(2)}, u32[]{:S(2)}) collective-permute-start(bf16[192,768]{1,0:T(8,128)(2,1)S(1)} %get-tuple-element.55), channel_id=1, source_target_pairs={{0,4},{1,5},{2,6},{3,7},{4,0},{5,1},{6,2},{7,3},{8,12},{9,13},{10,... | collective-permute-start | bytes 884744 | tf_op jit(solution)/shard_map/ppermute | solution.py:445
  88.0 1.2 %collective-permute-start.6 = (bf16[192,768]{1,0:T(8,128)(2,1)S(1)}, bf16[192,768]{1,0:T(8,128)(2,1)S(1)}, u32[]{:S(2)}, u32[]{:S(2)}) collective-permute-start(bf16[192,768]{1,0:T(8,128)(2,1)S(1)} %get-tuple-element.56), channel_id=1, source_target_pairs={{0,6},{1,7},{2,0},{3,1},{4,2},{5,3},{6,4},{7,5},{8,14},{9,15},{10,... | collective-permute-start | bytes 884744 | tf_op jit(solution)/shard_map/ppermute | solution.py:445
  90.0 2.4 %collective-permute-start.12 = (bf16[192,768]{1,0:T(8,128)(2,1)S(1)}, bf16[192,768]{1,0:T(8,128)(2,1)S(1)}, u32[]{:S(2)}, u32[]{:S(2)}) collective-permute-start(bf16[192,768]{1,0:T(8,128)(2,1)S(1)} %get-tuple-element.66), channel_id=1, source_target_pairs={{0,16},{1,17},{2,18},{3,19},{4,20},{5,21},{6,22},{7,23},{8,24},{9,... | collective-permute-start | bytes 884744 | tf_op jit(solution)/shard_map/ppermute | solution.py:445
  92.4 9.5 %collective-permute-done.4.two = bf16[192,768]{1,0:T(8,128)(2,1)S(1)} collective-permute-done((bf16[192,768]{1,0:T(8,128)(2,1)S(1)}, bf16[192,768]{1,0:T(8,128)(2,1)S(1)}, u32[]{:S(2)}, u32[]{:S(2)}) %collective-permute-start.4) | collective-permute-done | bytes 294944 | tf_op jit(solution)/shard_map/ppermute | solution.py:445
  101.8 1.1 collective-permute-start.13
  103.1 1.0 collective-permute-start.7
  104.1 1.5 %collective-permute-start.8 = (bf16[48,768]{1,0:T(8,128)(2,1)S(1)}, bf16[48,768]{1,0:T(8,128)(2,1)S(1)}, u32[]{:S(2)}, u32[]{:S(2)}) collective-permute-start(bf16[48,768]{1,0:T(8,128)(2,1)S(1)} %get-tuple-element.59), channel_id=1, source_target_pairs={{0,16},{1,17},{2,18},{3,19},{4,20},{5,21},{6,22},{7,23},{8,24},{9,... | collective-permute-start | bytes 221192 | tf_op jit(solution)/shard_map/ppermute | solution.py:445
  105.6 1.8 %collective-permute-start.9 = (bf16[48,768]{1,0:T(8,128)(2,1)S(1)}, bf16[48,768]{1,0:T(8,128)(2,1)S(1)}, u32[]{:S(2)}, u32[]{:S(2)}) collective-permute-start(bf16[48,768]{1,0:T(8,128)(2,1)S(1)} %get-tuple-element.60), channel_id=1, source_target_pairs={{0,24},{1,25},{2,26},{3,27},{4,28},{5,29},{6,30},{7,31},{8,0},{9,1... | collective-permute-start | bytes 221192 | tf_op jit(solution)/shard_map/ppermute | solution.py:445
  107.4 2.8 %collective-permute-done.13.four = bf16[192,768]{1,0:T(8,128)(2,1)S(1)} collective-permute-done((bf16[192,768]{1,0:T(8,128)(2,1)S(1)}, bf16[192,768]{1,0:T(8,128)(2,1)S(1)}, u32[]{:S(2)}, u32[]{:S(2)}) %collective-permute-start.13) | collective-permute-done | bytes 294944 | tf_op jit(solution)/shard_map/ppermute | solution.py:445
  111.7 2.5 %collective-permute-start.16 = (bf16[48,768]{1,0:T(8,128)(2,1)S(1)}, bf16[48,768]{1,0:T(8,128)(2,1)S(1)}, u32[]{:S(2)}, u32[]{:S(2)}) collective-permute-start(bf16[48,768]{1,0:T(8,128)(2,1)S(1)} %get-tuple-element.71), channel_id=1, source_target_pairs={{0,6},{1,7},{2,0},{3,1},{4,2},{5,3},{6,4},{7,5},{8,14},{9,15},{10,... | collective-permute-start | bytes 221192 | tf_op jit(solution)/shard_map/ppermute | solution.py:445
  114.2 2.5 %outputs.1 = (f32[4,768]{1,0:T(4,128)}, f32[48,1536]{1,0:T(8,128)}) custom-call(s32[2]{0:T(128)S(1)} %copy-done.14, f32[128,768]{1,0:T(8,128)S(1)} %get-tuple-element.43.context, bf16[128,768]{1,0:T(8,128)(2,1)S(1)} %get-tuple-element.44.slide_rows, bf16[768,768]{1,0:T(8,128)(2,1)S(1)} %copy-done.6, s32[1,128]{1,0:T(1,128)S(1)} %bitcast.17, ...), custom_call_target="tpu_custom_call" | custom-call | flops 1000000000 | bytes 4000000 | tf_op jit(solution)/shard_map/outputs/pallas_call | solution.py:343
  118.8 1.9 %finish.1 = f32[48,1536]{1,0:T(8,128)} custom-call(bf16[48,768]{1,0:T(8,128)(2,1)} %copy-done.7, bf16[48,768]{1,0:T(8,128)(2,1)} %copy-done.24, bf16[48,768]{1,0:T(8,128)(2,1)} %copy-done.25, bf16[48,768]{1,0:T(8,128)(2,1)} %copy-done.26, bf16[48,768]{1,0:T(8,128)(2,1)} %copy-done.8, bf16[48,768]{1,0:T(8,128)(2,1)} %copy-done.27, ...), custom_call_target="tpu_custom_call" | custom-call | tf_op jit(solution)/shard_map/finish/pallas_call | solution.py:432
  (90 shorter events, 11.2 us)
Async XLA Ops:
  5.6 22.8 %copy-start.33 = (s32[16]{0:T(128)S(1)}, s32[16]{0:T(128)}, u32[]{:S(2)}) copy-start(s32[16]{0:T(128)} %param.19) | copy-start | bytes 196
  5.6 37.5 %copy-start.2 = (bf16[4,256,1536]{2,1,0:T(8,128)(2,1)S(1)}, bf16[4,256,1536]{2,1,0:T(8,128)(2,1)}, u32[]{:S(2)}) copy-start(bf16[4,256,1536]{2,1,0:T(8,128)(2,1)} %param.11) | copy-start | bytes 9437188
  23.1 9.0 %copy-start.10 = (f32[4,2304]{1,0:T(4,128)}, f32[4,2304]{1,0:T(4,128)S(1)}, u32[]{:S(2)}) copy-start(f32[4,2304]{1,0:T(4,128)S(1)} %get-tuple-element.38.own) | copy-start | bytes 110596
  23.1 6.8 %collective-permute-start.2 = (f32[4,2304]{1,0:T(4,128)S(1)}, f32[4,2304]{1,0:T(4,128)S(1)}, u32[]{:S(2)}, u32[]{:S(2)}) collective-permute-start(f32[4,2304]{1,0:T(4,128)S(1)} %get-tuple-element.38.own), channel_id=1, source_target_pairs={{0,96},{32,0},{64,32},{96,64},{1,97},{33,1},{65,33},{97,65},{2,98}... | collective-permute-start | bytes 110600 | tf_op jit(solution)/shard_map/ppermute | solution.py:482
  26.2 5.5 %collective-permute-start.1 = (f32[4,2304]{1,0:T(4,128)S(1)}, f32[4,2304]{1,0:T(4,128)S(1)}, u32[]{:S(2)}, u32[]{:S(2)}) collective-permute-start(f32[4,2304]{1,0:T(4,128)S(1)} %get-tuple-element.38.own), channel_id=1, source_target_pairs={{0,64},{32,96},{64,0},{96,32},{1,65},{33,97},{65,1},{97,33},{2,66}... | collective-permute-start | bytes 110600 | tf_op jit(solution)/shard_map/ppermute | solution.py:482
  26.8 5.2 %collective-permute-start = (f32[4,2304]{1,0:T(4,128)S(1)}, f32[4,2304]{1,0:T(4,128)S(1)}, u32[]{:S(2)}, u32[]{:S(2)}) collective-permute-start(f32[4,2304]{1,0:T(4,128)S(1)} %get-tuple-element.38.own), channel_id=1, source_target_pairs={{0,32},{32,64},{64,96},{96,0},{1,33},{33,65},{65,97},{97,1},{2,34}... | collective-permute-start | bytes 110600 | tf_op jit(solution)/shard_map/ppermute | solution.py:482
  29.2 24.7 %copy-start.14 = (s32[2]{0:T(128)S(1)}, s32[2]{0:T(128)}, u32[]{:S(2)}) copy-start(s32[2]{0:T(128)} %pad_add_fusion.place) | copy-start | bytes 28
  29.2 24.7 %copy-start.15 = (s32[3]{0:T(128)S(1)}, s32[3]{0:T(128)}, u32[]{:S(2)}) copy-start(s32[3]{0:T(128)} %seg_len.1) | copy-start | bytes 40
  29.2 24.7 %copy-start.16 = (s32[128]{0:T(128)S(1)}, s32[128]{0:T(128)}, u32[]{:S(2)}) copy-start(s32[128]{0:T(128)} %param.18) | copy-start | bytes 1540
  29.2 24.6 %copy-start.17 = (s32[128]{0:T(128)S(1)}, s32[128]{0:T(128)}, u32[]{:S(2)}) copy-start(s32[128]{0:T(128)} %param.17) | copy-start | bytes 1540
  34.5 19.4 %copy-start.9 = (f32[16,768]{1,0:T(8,128)S(1)}, f32[16,768]{1,0:T(8,128)}, u32[]{:S(2)}) copy-start(f32[16,768]{1,0:T(8,128)} %get-tuple-element.42.cot_all) | copy-start | bytes 147460
  34.5 19.4 %all-to-all-start = ((bf16[32,8,896]{2,1,0:T(8,128)(2,1)}), bf16[32,8,896]{2,1,0:T(8,128)(2,1)}, u32[]{:S(2)}, u32[]{:S(2)}) async-start(bf16[32,8,896]{2,1,0:T(8,128)(2,1)} %bitcast.18), calls=%async_computation | async-start | bytes 917504 | tf_op jit(solution)/shard_map/all_to_all | solution.py:488
  61.2 16.6 %copy-start.19 = (bf16[1024,1536]{1,0:T(8,128)(2,1)S(1)}, bf16[1024,1536]{1,0:T(8,128)(2,1)}, u32[]{:S(2)}) copy-start(bf16[1024,1536]{1,0:T(8,128)(2,1)} %copy-done.18) | copy-start | bytes 9437188
  61.2 16.6 %copy-start.23 = (bf16[1536,1024]{1,0:T(8,128)(2,1)S(1)}, bf16[1536,1024]{1,0:T(8,128)(2,1)}, u32[]{:S(2)}) copy-start(bf16[1536,1024]{1,0:T(8,128)(2,1)} %copy-done.22) | copy-start | bytes 9437188
  77.8 3.5 %copy-start.21 = (bf16[1536,1024]{1,0:T(8,128)(2,1)S(1)}, bf16[1536,1024]{1,0:T(8,128)(2,1)}, u32[]{:S(2)}) copy-start(bf16[1536,1024]{1,0:T(8,128)(2,1)} %copy-done.20) | copy-start | bytes 9437188
  81.0 3.9 %collective-permute-start.3 = (bf16[768,768]{1,0:T(8,128)(2,1)S(1)}, bf16[768,768]{1,0:T(8,128)(2,1)S(1)}, u32[]{:S(2)}, u32[]{:S(2)}) collective-permute-start(bf16[768,768]{1,0:T(8,128)(2,1)S(1)} %get-tuple-element.52), channel_id=1, source_target_pairs={{0,1},{1,0},{2,3},{3,2},{4,5},{5,4},{6,7},{7,6},{8,9},{9,8},{10,11... | collective-permute-start | bytes 3538952 | tf_op jit(solution)/shard_map/ppermute | solution.py:445
  84.5 4.7 %collective-permute-start.10 = (bf16[768,768]{1,0:T(8,128)(2,1)S(1)}, bf16[768,768]{1,0:T(8,128)(2,1)S(1)}, u32[]{:S(2)}, u32[]{:S(2)}) collective-permute-start(bf16[768,768]{1,0:T(8,128)(2,1)S(1)} %get-tuple-element.63), channel_id=1, source_target_pairs={{0,1},{1,0},{2,3},{3,2},{4,5},{5,4},{6,7},{7,6},{8,9},{9,8},{10,11... | collective-permute-start | bytes 3538952 | tf_op jit(solution)/shard_map/ppermute | solution.py:445
  85.2 16.6 %collective-permute-start.4 = (bf16[192,768]{1,0:T(8,128)(2,1)S(1)}, bf16[192,768]{1,0:T(8,128)(2,1)S(1)}, u32[]{:S(2)}, u32[]{:S(2)}) collective-permute-start(bf16[192,768]{1,0:T(8,128)(2,1)S(1)} %get-tuple-element.54), channel_id=1, source_target_pairs={{0,2},{1,3},{2,4},{3,5},{4,6},{5,7},{6,0},{7,1},{8,10},{9,11},{10,... | collective-permute-start | bytes 884744 | tf_op jit(solution)/shard_map/ppermute | solution.py:445
  85.9 17.1 %collective-permute-start.5 = (bf16[192,768]{1,0:T(8,128)(2,1)S(1)}, bf16[192,768]{1,0:T(8,128)(2,1)S(1)}, u32[]{:S(2)}, u32[]{:S(2)}) collective-permute-start(bf16[192,768]{1,0:T(8,128)(2,1)S(1)} %get-tuple-element.55), channel_id=1, source_target_pairs={{0,4},{1,5},{2,6},{3,7},{4,0},{5,1},{6,2},{7,3},{8,12},{9,13},{10,... | collective-permute-start | bytes 884744 | tf_op jit(solution)/shard_map/ppermute | solution.py:445
  88.0 15.0 %collective-permute-start.6 = (bf16[192,768]{1,0:T(8,128)(2,1)S(1)}, bf16[192,768]{1,0:T(8,128)(2,1)S(1)}, u32[]{:S(2)}, u32[]{:S(2)}) collective-permute-start(bf16[192,768]{1,0:T(8,128)(2,1)S(1)} %get-tuple-element.56), channel_id=1, source_target_pairs={{0,6},{1,7},{2,0},{3,1},{4,2},{5,3},{6,4},{7,5},{8,14},{9,15},{10,... | collective-permute-start | bytes 884744 | tf_op jit(solution)/shard_map/ppermute | solution.py:445
  89.2 25.0 %copy-start.11 = (s32[16,1]{1,0:T(8,128)S(1)}, s32[16,1]{1,0:T(8,128)}, u32[]{:S(2)}) copy-start(s32[16,1]{1,0:T(8,128)} %copy.15.counts) | copy-start | bytes 196
  89.5 16.1 %collective-permute-start.11 = (bf16[192,768]{1,0:T(8,128)(2,1)S(1)}, bf16[192,768]{1,0:T(8,128)(2,1)S(1)}, u32[]{:S(2)}, u32[]{:S(2)}) collective-permute-start(bf16[192,768]{1,0:T(8,128)(2,1)S(1)} %get-tuple-element.65), channel_id=1, source_target_pairs={{0,8},{1,9},{2,10},{3,11},{4,12},{5,13},{6,14},{7,15},{8,16},{9,17... | collective-permute-start | bytes 884744 | tf_op jit(solution)/shard_map/ppermute | solution.py:445
  90.0 17.4 %collective-permute-start.12 = (bf16[192,768]{1,0:T(8,128)(2,1)S(1)}, bf16[192,768]{1,0:T(8,128)(2,1)S(1)}, u32[]{:S(2)}, u32[]{:S(2)}) collective-permute-start(bf16[192,768]{1,0:T(8,128)(2,1)S(1)} %get-tuple-element.66), channel_id=1, source_target_pairs={{0,16},{1,17},{2,18},{3,19},{4,20},{5,21},{6,22},{7,23},{8,24},{9,... | collective-permute-start | bytes 884744 | tf_op jit(solution)/shard_map/ppermute | solution.py:445
  101.8 8.3 %collective-permute-start.13 = (bf16[192,768]{1,0:T(8,128)(2,1)S(1)}, bf16[192,768]{1,0:T(8,128)(2,1)S(1)}, u32[]{:S(2)}, u32[]{:S(2)}) collective-permute-start(bf16[192,768]{1,0:T(8,128)(2,1)S(1)} %get-tuple-element.67), channel_id=1, source_target_pairs={{0,24},{1,25},{2,26},{3,27},{4,28},{5,29},{6,30},{7,31},{8,0},{9,1... | collective-permute-start | bytes 884744 | tf_op jit(solution)/shard_map/ppermute | solution.py:445
  103.1 13.6 %copy-start.7 = (bf16[48,768]{1,0:T(8,128)(2,1)}, bf16[48,768]{1,0:T(8,128)(2,1)S(1)}, u32[]{:S(2)}) copy-start(bf16[48,768]{1,0:T(8,128)(2,1)S(1)} %get-tuple-element.57.refs_0_) | copy-start | bytes 221188
  103.1 8.6 %collective-permute-start.7 = (bf16[48,768]{1,0:T(8,128)(2,1)S(1)}, bf16[48,768]{1,0:T(8,128)(2,1)S(1)}, u32[]{:S(2)}, u32[]{:S(2)}) collective-permute-start(bf16[48,768]{1,0:T(8,128)(2,1)S(1)} %get-tuple-element.58), channel_id=1, source_target_pairs={{0,8},{1,9},{2,10},{3,11},{4,12},{5,13},{6,14},{7,15},{8,16},{9,17... | collective-permute-start | bytes 221192 | tf_op jit(solution)/shard_map/ppermute | solution.py:445
  104.1 12.6 %collective-permute-start.8 = (bf16[48,768]{1,0:T(8,128)(2,1)S(1)}, bf16[48,768]{1,0:T(8,128)(2,1)S(1)}, u32[]{:S(2)}, u32[]{:S(2)}) collective-permute-start(bf16[48,768]{1,0:T(8,128)(2,1)S(1)} %get-tuple-element.59), channel_id=1, source_target_pairs={{0,16},{1,17},{2,18},{3,19},{4,20},{5,21},{6,22},{7,23},{8,24},{9,... | collective-permute-start | bytes 221192 | tf_op jit(solution)/shard_map/ppermute | solution.py:445
  105.6 11.1 %collective-permute-start.9 = (bf16[48,768]{1,0:T(8,128)(2,1)S(1)}, bf16[48,768]{1,0:T(8,128)(2,1)S(1)}, u32[]{:S(2)}, u32[]{:S(2)}) collective-permute-start(bf16[48,768]{1,0:T(8,128)(2,1)S(1)} %get-tuple-element.60), channel_id=1, source_target_pairs={{0,24},{1,25},{2,26},{3,27},{4,28},{5,29},{6,30},{7,31},{8,0},{9,1... | collective-permute-start | bytes 221192 | tf_op jit(solution)/shard_map/ppermute | solution.py:445
  110.9 6.4 %collective-permute-start.14 = (bf16[48,768]{1,0:T(8,128)(2,1)S(1)}, bf16[48,768]{1,0:T(8,128)(2,1)S(1)}, u32[]{:S(2)}, u32[]{:S(2)}) collective-permute-start(bf16[48,768]{1,0:T(8,128)(2,1)S(1)} %get-tuple-element.69), channel_id=1, source_target_pairs={{0,2},{1,3},{2,4},{3,5},{4,6},{5,7},{6,0},{7,1},{8,10},{9,11},{10,... | collective-permute-start | bytes 221192 | tf_op jit(solution)/shard_map/ppermute | solution.py:445
  110.9 6.4 %collective-permute-start.15 = (bf16[48,768]{1,0:T(8,128)(2,1)S(1)}, bf16[48,768]{1,0:T(8,128)(2,1)S(1)}, u32[]{:S(2)}, u32[]{:S(2)}) collective-permute-start(bf16[48,768]{1,0:T(8,128)(2,1)S(1)} %get-tuple-element.70), channel_id=1, source_target_pairs={{0,4},{1,5},{2,6},{3,7},{4,0},{5,1},{6,2},{7,3},{8,12},{9,13},{10,... | collective-permute-start | bytes 221192 | tf_op jit(solution)/shard_map/ppermute | solution.py:445
  111.7 6.4 %copy-start.24 = (bf16[48,768]{1,0:T(8,128)(2,1)}, bf16[48,768]{1,0:T(8,128)(2,1)S(1)}, u32[]{:S(2)}) copy-start(bf16[48,768]{1,0:T(8,128)(2,1)S(1)} %collective-permute-done.7.refs_1_) | copy-start | bytes 221188
  111.7 6.4 %collective-permute-start.16 = (bf16[48,768]{1,0:T(8,128)(2,1)S(1)}, bf16[48,768]{1,0:T(8,128)(2,1)S(1)}, u32[]{:S(2)}, u32[]{:S(2)}) collective-permute-start(bf16[48,768]{1,0:T(8,128)(2,1)S(1)} %get-tuple-element.71), channel_id=1, source_target_pairs={{0,6},{1,7},{2,0},{3,1},{4,2},{5,3},{6,4},{7,5},{8,14},{9,15},{10,... | collective-permute-start | bytes 221192 | tf_op jit(solution)/shard_map/ppermute | solution.py:445
  (20 other events, 27.0 us)

commit v2 on v1

v2 whole, which is shorter than its diff:
```python
import math

import jax
import jax.numpy as jnp
from jax import lax
from jax.experimental import pallas as pl
from jax.experimental.pallas import tpu as pltpu
from jax.sharding import PartitionSpec as P

HEADS = 16
EPSILON = 1e-06
MIB = 1 << 20
BF = jnp.bfloat16
F4 = jnp.float32


def dot_nn(a, b):
    return lax.dot_general(a, b, (((1,), (0,)), ((), ())), preferred_element_type=F4)


def dot_nt(a, b):
    return lax.dot_general(a, b, (((1,), (1,)), ((), ())), preferred_element_type=F4)


def dot_tn(a, b):
    return lax.dot_general(a, b, (((0,), (0,)), ((), ())), preferred_element_type=F4)


def halves(value):
    high = value.astype(BF)
    return high, (value - high.astype(F4)).astype(BF)


def standardise(values):
    width = values.shape[1]
    centre = jnp.sum(values, axis=1, keepdims=True) * (1.0 / width)
    shifted = values - centre
    spread = jnp.sum(shifted * shifted, axis=1, keepdims=True) * (1.0 / width)
    return shifted * lax.rsqrt(spread + EPSILON)


def gelu_pair(a):
    bell = jnp.exp(a * a * -0.5)
    t = 1.0 / (1.0 + jnp.abs(a) * (0.3275911 * 0.7071067811865476))
    series = t * (0.127414796 + t * (-0.142248368 + t * (0.7107068705 + t * (-0.7265760135 + t * 0.5307027145))))
    tail = series * bell
    phi = jnp.where(a < 0.0, tail, 1.0 - tail)
    return a * phi, phi + a * (bell * 0.3989422804014327)


def from_hbm(value):
    return pltpu.with_memory_space_constraint(value, pltpu.HBM)


def from_vmem(value):
    return pltpu.with_memory_space_constraint(value, pltpu.VMEM)


ANY = pl.BlockSpec(memory_space=pl.ANY)
SMEM = pl.BlockSpec(memory_space=pltpu.SMEM)
VMEM = pl.BlockSpec(memory_space=pltpu.VMEM)


def forward_kernel(
    place, tiles_hbm, w_in, w_out, cot, slope_send, slope_keep, pooled, shared, token_mean, normed_hbm, tiles, normed, total, sems
):
    step = pl.program_id(0)
    steps = pl.num_programs(0)
    tile_count = token_mean.shape[0]
    patches = tiles.shape[0] // tile_count
    pieces = [pl.ds(tile * patches, patches) for tile in range(tile_count)]
    out_copies = [
        pltpu.make_async_copy(normed.at[rows], normed_hbm.at[rows], sems.at[tile_count + tile])
        for tile, rows in enumerate(pieces)
    ]

    @pl.when(step == 0)
    def _():
        in_copies = [
            pltpu.make_async_copy(tiles_hbm.at[rows], tiles.at[rows], sems.at[tile]) for tile, rows in enumerate(pieces)
        ]
        for copy in in_copies:
            copy.start()
        for tile, rows in enumerate(pieces):
            in_copies[tile].wait()
            values = tiles[rows, :].astype(F4)
            token_mean[pl.ds(tile, 1), :] = jnp.sum(values, axis=0, keepdims=True) * (1.0 / patches)
            normed[rows, :] = standardise(values).astype(BF)
            out_copies[tile].start()
        total[...] = jnp.zeros_like(total)

    def work(slope):
        means = []
        for rows in pieces:
            value, rate = gelu_pair(dot_nn(normed[rows, :], w_in[...]))
            slope[rows, :] = rate.astype(BF)
            means.append(jnp.sum(value, axis=0, keepdims=True) * (1.0 / patches))
        high, low = halves(jnp.concatenate(means, axis=0))
        both = jnp.concatenate([high, low], axis=0)
        pooled[...] = both
        total[...] += dot_nn(both, w_out[...])

    @pl.when(step < steps // 2)
    def _():
        work(slope_send)

    @pl.when(step >= steps // 2)
    def _():
        work(slope_keep)

    @pl.when(step == steps - 1)
    def _():
        width = total.shape[1]
        shared[:, :width] = total[:tile_count, :] + total[tile_count:, :]
        shared[:, width:] = cot[...]
        for copy in out_copies:
            copy.wait()


def forward(place, tiles, w_in, w_out, cot, tile_count):
    tokens, width = tiles.shape
    hidden = w_in.shape[1]
    block = 256
    steps = hidden // block
    slide_width = cot.shape[1]

    def at(j, place):
        return (j + steps // 2 * (1 - place[2])) % steps

    return pl.pallas_call(
        forward_kernel,
        grid_spec=pltpu.PrefetchScalarGridSpec(
            num_scalar_prefetch=1,
            grid=(steps,),
            in_specs=[
                ANY,
                pl.BlockSpec((width, block), lambda j, place: (0, at(j, place))),
                pl.BlockSpec((block, width), lambda j, place: (at(j, place), 0)),
                pl.BlockSpec((tile_count, slide_width), lambda j, place: (0, 0)),
            ],
            out_specs=[
                pl.BlockSpec((tokens, block), lambda j, place: (0, jnp.minimum(j, steps // 2 - 1))),
                pl.BlockSpec((tokens, block), lambda j, place: (0, jnp.maximum(j - steps // 2, 0))),
                pl.BlockSpec((2 * tile_count, block), lambda j, place: (0, at(j, place))),
                pl.BlockSpec((tile_count, width + slide_width), lambda j, place: (0, 0)),
                pl.BlockSpec((tile_count, width), lambda j, place: (0, 0)),
                ANY,
            ],
            scratch_shapes=[
                pltpu.VMEM((tokens, width), BF),
                pltpu.VMEM((tokens, width), BF),
                pltpu.VMEM((2 * tile_count, width), F4),
                pltpu.SemaphoreType.DMA((2 * tile_count,)),
            ],
        ),
        out_shape=[
            pltpu.HBM((tokens, hidden // 2), BF),
            pltpu.HBM((tokens, hidden // 2), BF),
            jax.ShapeDtypeStruct((2 * tile_count, hidden), BF),
            jax.ShapeDtypeStruct((tile_count, width + slide_width), F4),
            jax.ShapeDtypeStruct((tile_count, width), F4),
            pltpu.HBM((tokens, width), BF),
        ],
        compiler_params=pltpu.CompilerParams(vmem_limit_bytes=32 * MIB),
        name="forward",
    )(place, from_hbm(tiles), from_hbm(w_in), from_hbm(w_out), cot)


def transpose_kernel(after, normed, out):
    out[...] = normed[...].T


def transposed(normed, after, patches):
    tokens, width = normed.shape
    return pl.pallas_call(
        transpose_kernel,
        grid=(tokens // patches,),
        in_specs=[ANY, pl.BlockSpec((patches, width), lambda i: (i, 0))],
        out_specs=pl.BlockSpec((width, patches), lambda i: (0, i)),
        out_shape=pltpu.HBM((width, tokens), BF),
        compiler_params=pltpu.CompilerParams(vmem_limit_bytes=16 * MIB),
        cost_estimate=pl.CostEstimate(flops=20_000_000, bytes_accessed=9_000_000, transcendentals=0),
        name="transposed",
    )(after, from_hbm(normed))


def embed_kernel(
    place, own, one, two, three, token_mean, counts, pooled, normed_in, slope_in, out, cot_all, normed_out, slope_out
):
    width = token_mean.shape[1]
    half = width // 2
    total = (own[:, :width] + two[:, :width]) + (one[:, :width] + three[:, :width])
    embedding = total + token_mean[...]
    eight = jnp.concatenate([embedding[:, :half], embedding[:, half:]], axis=0)
    out[:, :half] = jnp.concatenate([eight] * (out.shape[0] // 8), axis=0).astype(BF)
    out[:, half:] = pooled[...]
    parts = [own[:, width:], one[:, width:], two[:, width:], three[:, width:]]
    blocks = []
    for group in range(4):
        back = jnp.bitwise_and(place[0] - group, 3)
        block = parts[0]
        for shift in range(1, 4):
            block = jnp.where(back == shift, parts[shift], block)
        blocks.append(block)
    cot_all[...] = jnp.concatenate(blocks, axis=0) / counts[...].astype(F4)


def embed(place, parts, token_mean, counts, pooled, normed, slope, peers):
    tile_count, width = token_mean.shape
    slide_width = parts[0].shape[1] - width
    return pl.pallas_call(
        embed_kernel,
        in_specs=[SMEM] + [VMEM] * 7 + [ANY] * 2,
        out_specs=[VMEM] * 2 + [ANY] * 2,
        out_shape=[
            jax.ShapeDtypeStruct((peers * 8, width // 2 + 128), BF),
            jax.ShapeDtypeStruct((16, slide_width), F4),
            pltpu.HBM(normed.shape, BF),
            pltpu.HBM(slope.shape, BF),
        ],
        input_output_aliases={8: 2, 9: 3},
        compiler_params=pltpu.CompilerParams(vmem_limit_bytes=8 * MIB),
        name="embed",
    )(place, *parts, token_mean, counts, pooled, from_hbm(normed), from_hbm(slope))


def attention_kernel(
    place,
    seg_len,
    gathered,
    cot_all,
    slide_of,
    order_of,
    w_proj_hbm,
    w_qkv_hbm,
    w_attn_hbm,
    w_out_hbm,
    normed_own,
    normed_other,
    slope_own,
    slope_other,
    d_preact,
    lhs0,
    lhs1,
    lhs2,
    lhs3,
    d_embed,
    context,
    slide_rows,
    pooled_pair,
    slope,
    w_proj,
    w_qkv,
    w_attn,
    w_out,
    sems,
):
    hidden = w_out.shape[0]
    half_rows = pl.ds(pl.multiple_of(place[2] * hidden, hidden), hidden)
    pairs = [(w_proj_hbm, w_proj), (w_qkv_hbm, w_qkv), (w_attn_hbm, w_attn), (w_out_hbm.at[half_rows], w_out)]
    loads = [pltpu.make_async_copy(src, dst, sems.at[34 + i]) for i, (src, dst) in enumerate(pairs)]
    for load in loads:
        load.start()

    tokens = slope_own.shape[0]
    rows_each = lhs0.shape[0] // 4
    core = place[2]
    copies = [
        pltpu.make_async_copy(slope_own, slope.at[pl.ds(0, tokens)], sems.at[0]),
        pltpu.make_async_copy(slope_other, slope.at[pl.ds(tokens, tokens)], sems.at[1]),
    ]
    for chunk, lhs in enumerate((lhs0, lhs1, lhs2, lhs3)):
        for sub in range(4):
            z = (place[3] + jnp.where(core == 0, sub, chunk)) % 4
            x = (place[4] + jnp.where(core == 0, chunk, sub)) % 4
            source = pl.ds(pl.multiple_of((z * 4 + x) * rows_each, 16), rows_each)
            rows = pl.ds(sub * rows_each, rows_each)
            at = 2 + 2 * (4 * chunk + sub)
            copies.append(pltpu.make_async_copy(normed_own.at[source], lhs.at[rows, pl.ds(0, tokens)], sems.at[at]))
            copies.append(
                pltpu.make_async_copy(normed_other.at[source], lhs.at[rows, pl.ds(tokens, tokens)], sems.at[at + 1])
            )
    for copy in copies:
        copy.start()

    tiles = slide_of.shape[1]
    half = w_proj.shape[0] // 2
    width = w_proj.shape[1]
    head = width // HEADS

    row = lax.broadcasted_iota(jnp.int32, (tiles, 2 * tiles), 0)
    col = lax.broadcasted_iota(jnp.int32, (tiles, 2 * tiles), 1)
    first = (row // 4) * 8 + row % 4
    every = gathered[...]
    left = dot_nn((col == first).astype(F4).astype(BF), every).astype(BF)
    right = dot_nn((col == first + 4).astype(F4).astype(BF), every).astype(BF)
    pooled_pair[:, :128] = left[:, half:]
    pooled_pair[:, 128:] = right[:, half:]
    loads[0].wait()
    rows = (dot_nn(left[:, :half], w_proj[:half, :]) + dot_nn(right[:, :half], w_proj[half:, :])).astype(BF)
    slide_rows[...] = rows
    loads[1].wait()
    qkv = dot_nn(rows, w_qkv[...]).astype(BF)

    slide = slide_of[...].astype(F4)
    order = order_of[...].astype(F4)
    weight = jnp.zeros((tiles, tiles), F4)
    for branch in range(3):
        length = seg_len[branch].astype(F4)
        block = jnp.floor((order + 0.5) / length)
        dilation = float(2**branch)
        phase = order - dilation * jnp.floor(order * (1.0 / dilation))
        code = jnp.broadcast_to((slide * 64.0 + block) * 4.0 + phase, (tiles, tiles))
        weight = weight + (code == code.T).astype(F4)
    slide_col = jnp.broadcast_to(slide, (tiles, tiles)).T
    lane = lax.broadcasted_iota(jnp.int32, (tiles, 16), 1).astype(F4)
    member = (slide_col[:, :16] == lane).astype(F4).astype(BF)
    cot_high, cot_low = halves(cot_all[...])
    d_attended = dot_nn(member, cot_high) + dot_nn(member, cot_low)
    loads[2].wait()
    d_context = dot_nt(d_attended.astype(BF), w_attn[...]).astype(BF)

    scale = 1.0 / math.sqrt(head)
    group_heads = HEADS // 2
    group_width = group_heads * head
    lanes = lax.broadcasted_iota(jnp.int32, (1, group_width), 1)
    masks = [((lanes >= h * head) & (lanes < (h + 1) * head)).astype(F4).astype(BF) for h in range(group_heads)]

    def stacked(value):
        return jnp.concatenate([value * mask for mask in masks], axis=0)

    def beside(parts):
        return jnp.concatenate(parts, axis=1)

    grads = {}
    for group in range(2):
        start = group * group_width
        query = qkv[:, start : start + group_width]
        key_rows = qkv[:, width + start : width + start + group_width]
        value_rows = qkv[:, 2 * width + start : 2 * width + start + group_width]
        d_out = d_context[:, start : start + group_width]
        query_stack, d_out_stack = stacked(query), stacked(d_out)
        scores = dot_nt(query_stack, key_rows)
        d_share = dot_nt(d_out_stack, value_rows)
        shares, d_scores = [], []
        for h in range(group_heads):
            at = slice(h * tiles, (h + 1) * tiles)
            score = jnp.where(weight > 0.0, scores[at] * scale, -1e30)
            numerator = weight * jnp.exp(score - jnp.max(score, axis=1, keepdims=True))
            share = numerator * (1.0 / jnp.sum(numerator, axis=1, keepdims=True))
            slant = share * d_share[at]
            d_score = (slant - share * jnp.sum(slant, axis=1, keepdims=True)) * scale
            shares.append(share.astype(BF))
            d_scores.append(d_score.astype(BF))
        context[:, start : start + group_width] = dot_nn(beside(shares), stacked(value_rows))
        grads["query", group] = dot_nn(beside(d_scores), stacked(key_rows))
        grads["key", group] = dot_nn(beside([part.T for part in d_scores]), query_stack)
        grads["value", group] = dot_nn(beside([part.T for part in shares]), d_out_stack)
    d_qkv = beside([grads[name, group].astype(BF) for name in ("query", "key", "value") for group in range(2)])

    d_slide = d_attended + dot_nt(d_qkv, w_qkv[...])
    d_embed[...] = dot_nt(d_slide.astype(BF), w_proj[...])
    eight = d_embed[pl.ds(pl.multiple_of(place[1] // 2 * 8, 8), 8), :]
    high, low = halves(eight)
    loads[3].wait()
    back = dot_nt(jnp.concatenate([high, low], axis=0), w_out[...])
    back = back[:8, :] + back[8:, :]
    back = jnp.where(core == 0, back, jnp.concatenate([back[4:, :], back[:4, :]], axis=0)) * (4.0 / tokens)
    for copy in copies:
        copy.wait()
    patches = tokens // 4
    for tile in range(8):
        at = pl.ds(tile * patches, patches)
        d_preact[at, :] = (slope[at, :].astype(F4) * back[tile : tile + 1, :]).astype(BF)


def attention(place, seg_len, gathered, weights, cot_all, slide_of, order_of, normed, slopes):
    w_proj, w_qkv, w_attn, w_out = weights
    tiles = slide_of.shape[1]
    width, slide_width = w_proj.shape
    hidden = w_out.shape[0] // 2
    tokens = slopes[0].shape[0]
    return pl.pallas_call(
        attention_kernel,
        in_specs=[SMEM, SMEM] + [VMEM] * 4 + [ANY] * 8,
        out_specs=[VMEM] * 9,
        out_shape=[
            pltpu.VMEM((2 * tokens, hidden), BF),
            *[pltpu.VMEM((width // 4, 2 * tokens), BF)] * 4,
            jax.ShapeDtypeStruct((tiles, width), F4),
            jax.ShapeDtypeStruct((tiles, slide_width), F4),
            jax.ShapeDtypeStruct((tiles, slide_width), BF),
            jax.ShapeDtypeStruct((tiles, 256), BF),
        ],
        scratch_shapes=[
            pltpu.VMEM((2 * tokens, hidden), BF),
            pltpu.VMEM(w_proj.shape, BF),
            pltpu.VMEM(w_qkv.shape, BF),
            pltpu.VMEM(w_attn.shape, BF),
            pltpu.VMEM((hidden, width), BF),
            pltpu.SemaphoreType.DMA((38,)),
        ],
        compiler_params=pltpu.CompilerParams(vmem_limit_bytes=24 * MIB),
        name="attention",
    )(
        place,
        seg_len,
        gathered,
        cot_all,
        slide_of,
        order_of,
        *[from_hbm(value) for value in (*weights, *normed, *slopes)],
    )


def outputs_kernel(place, context, slide_rows, w_attn, slide_of, counts, pooled_pair, d_embed, slide_embed, grad_out):
    tiles = slide_of.shape[1]
    high, low = halves(context[...])
    attended = slide_rows[...].astype(F4) + dot_nn(high, w_attn[...]) + dot_nn(low, w_attn[...])
    group = lax.broadcasted_iota(jnp.int32, (16, tiles), 0)
    member = (slide_of[...] == group).astype(F4).astype(BF)
    high, low = halves(attended)
    sums = (dot_nn(member, high) + dot_nn(member, low)) / counts[...].astype(F4)
    own = sums[0:4, :]
    for index in range(1, 4):
        own = jnp.where(place[0] == index, sums[4 * index : 4 * index + 4, :], own)
    slide_embed[...] = own
    high, low = halves(d_embed[...])
    pair = pooled_pair[...]
    both = dot_tn(pair, high) + dot_tn(pair, low)
    rows = grad_out.shape[0]
    grad_out[...] = both[:rows, :] + both[128 : 128 + rows, :]


def outputs(place, context, slide_rows, w_attn, slide_of, counts, pooled_pair, d_embed, rows):
    slide_width = w_attn.shape[0]
    width = d_embed.shape[1]
    return pl.pallas_call(
        outputs_kernel,
        in_specs=[pl.BlockSpec(memory_space=pltpu.SMEM)] + [pl.BlockSpec(memory_space=pltpu.VMEM)] * 7,
        out_shape=[jax.ShapeDtypeStruct((4, slide_width), F4), jax.ShapeDtypeStruct((rows, width), F4)],
        compiler_params=pltpu.CompilerParams(vmem_limit_bytes=16 * MIB),
        cost_estimate=pl.CostEstimate(flops=1000, bytes_accessed=1000, transcendentals=0),
        name="outputs",
    )(place, context, slide_rows, w_attn, slide_of, counts, pooled_pair, d_embed)


def grad_kernel(lhs, d_preact, out):
    out[...] = dot_nn(lhs[...], d_preact[...]).astype(BF)


def grad_chunk(lhs, d_preact):
    rows, tokens = lhs.shape
    hidden = d_preact.shape[1]
    return pl.pallas_call(
        grad_kernel,
        in_specs=[VMEM] * 2,
        out_specs=VMEM,
        out_shape=jax.ShapeDtypeStruct((rows, hidden), BF),
        compiler_params=pltpu.CompilerParams(vmem_limit_bytes=16 * MIB),
        cost_estimate=pl.CostEstimate(flops=1000, bytes_accessed=1000, transcendentals=0),
        name="grad_chunk",
    )(from_vmem(lhs), from_vmem(d_preact))


def add_four_kernel(one, two, three, four, after, *outs):
    rows = outs[0].shape[0]
    for index, out in enumerate(outs):
        at = pl.ds(index * rows, rows)
        total = (one[at, :].astype(F4) + two[at, :].astype(F4)) + (three[at, :].astype(F4) + four[at, :].astype(F4))
        out[...] = total.astype(BF)


def add_four(parts, after):
    rows, columns = parts[0].shape
    return pl.pallas_call(
        add_four_kernel,
        in_specs=[VMEM] * 4 + [ANY],
        out_shape=[jax.ShapeDtypeStruct((rows // 4, columns), BF)] * 4,
        compiler_params=pltpu.CompilerParams(vmem_limit_bytes=8 * MIB),
        name="add_four",
    )(*parts, after)


def split_kernel(place, one, two, three, four, keep, send):
    total = (one[...].astype(F4) + two[...].astype(F4)) + (three[...].astype(F4) + four[...].astype(F4))
    rows = keep.shape[0]
    top, bottom = total[:rows, :], total[rows:, :]
    keep[...] = jnp.where(place[2] == 0, top, bottom)
    send[...] = jnp.where(place[2] == 0, bottom, top)


def split(place, parts):
    rows, columns = parts[0].shape
    return pl.pallas_call(
        split_kernel,
        in_specs=[SMEM] + [VMEM] * 4,
        out_shape=[jax.ShapeDtypeStruct((rows // 2, columns), F4)] * 2,
        compiler_params=pltpu.CompilerParams(vmem_limit_bytes=8 * MIB),
        name="split",
    )(place, *parts)


def finish_kernel(place, keep, received, out):
    half = out.shape[1] // 2
    first = place[2] == 0
    out[:, :half] = jnp.where(first, keep[...], received[...])
    out[:, half:] = jnp.where(first, received[...], keep[...])


def finish(place, keep, received):
    rows, columns = keep.shape
    return pl.pallas_call(
        finish_kernel,
        in_specs=[SMEM] + [VMEM] * 2,
        out_shape=jax.ShapeDtypeStruct((rows, 2 * columns), F4),
        compiler_params=pltpu.CompilerParams(vmem_limit_bytes=8 * MIB),
        name="finish",
    )(place, keep, received)


def moved(value, step):
    pairs = []
    for z in range(4):
        for x in range(4):
            for c in range(2):
                to_z, to_x, to_c = step(z, x, c)
                pairs.append(((z * 4 + x) * 2 + c, (to_z % 4 * 4 + to_x % 4) * 2 + to_c % 2))
    return lax.ppermute(value, "tile", pairs)


def other_core(value):
    return moved(value, lambda z, x, c: (z, x, c + 1))


def first_axis(value, k):
    return moved(value, lambda z, x, c: (z, x + k, c) if c == 0 else (z + k, x, c))


def second_axis(value, k):
    return moved(value, lambda z, x, c: (z + k, x, c) if c == 0 else (z, x + k, c))


def on_device(
    tiles,
    w_in,
    w_out,
    w_proj,
    w_qkv,
    w_attn_out,
    slide_of_tile,
    order_of_tile,
    slide_counts,
    seg_len,
    slide_cot,
):
    tile_count, patches, width = tiles.shape
    hidden = w_in.shape[1]
    peers = 32
    flat = tiles.reshape(tile_count * patches, width)
    tile_pos = lax.axis_index("tile")
    slide_pos = lax.axis_index("slide")
    place = jnp.stack([slide_pos, tile_pos, tile_pos % 2, tile_pos // 8, tile_pos // 2 % 4]).astype(jnp.int32)
    counts = slide_counts.reshape(-1, 1)
    slide_of = slide_of_tile.reshape(1, -1)
    order_of = order_of_tile.reshape(1, -1)

    slope_send, slope_keep, pooled, shared, token_mean, normed = forward(place, flat, w_in, w_out, slide_cot, tile_count)
    parts = [shared] + [
        lax.ppermute(shared, "slide", [(i, (i + k) % 4) for i in range(4)]) for k in (1, 2, 3)
    ]
    normed_t = transposed(normed, shared, patches)
    slices = pooled.reshape(2 * tile_count, peers, hidden // peers).transpose(1, 0, 2)
    slices = jnp.pad(slices.reshape(peers * 2 * tile_count, -1), ((0, 0), (0, 128 - hidden // peers)))
    mine, cot_all, normed_t, slope_send = embed(
        place, parts, token_mean, counts, slices, normed_t, slope_send, peers
    )
    gathered = lax.all_to_all(
        mine.reshape(peers, 8, -1), "tile", split_axis=0, concat_axis=0, tiled=True
    ).reshape(peers * 8, -1)
    slope_other, normed_other = other_core(slope_send), other_core(normed_t)
    d_preact, *lhs, d_embed, context, slide_rows, pooled_pair = attention(
        place,
        seg_len,
        gathered,
        (w_proj, w_qkv, w_attn_out, w_out),
        cot_all,
        slide_of,
        order_of,
        (normed_t, normed_other),
        (slope_keep, slope_other),
    )
    chunks = {}
    for k in (2, 1, 3):
        chunks[k] = first_axis(grad_chunk(lhs[k], d_preact), k)
    chunks[0] = grad_chunk(lhs[0], d_preact)
    slide_embed, grad_out = outputs(
        place, context, slide_rows, w_attn_out, slide_of, counts, pooled_pair, d_embed, hidden // peers
    )
    parts = add_four([chunks[k] for k in range(4)], slide_embed)
    parts = [parts[0]] + [second_axis(parts[k], k) for k in (1, 2, 3)]
    keep, send = split(place, parts)
    return (slide_embed, finish(place, keep, other_core(send)), grad_out)


def solution(mesh):
    placed = (
        P("tile", None, None),
        P(None, "slide"),
        P("slide", None),
        P(),
        P(),
        P(),
        P(),
        P(),
        P(),
        P(),
        P("slide", None),
    )
    return jax.shard_map(
        on_device,
        mesh=mesh,
        in_specs=placed,
        out_specs=(P("slide", None), P("tile", "slide"), P(("slide", "tile"), None)),
        check_vma=False,
    )
```

time: 121 us -> 98.3 us (0.81)
  blocking collectives: 0 us -> 19 us
  local copies, waits for them, and re-layouts: 21.2 us -> 4.07 us
  starting transfers between devices: 29.5 us -> 12.7 us
  Pallas kernels: 49.5 us -> 44.2 us
  waiting for transfers between devices: 18.9 us -> 16.2 us
    all_to_all x0 -> x1, blocking collectives: none -> 19 us  [on_device(): lax.all_to_all(mine.reshape(peers, 8, -1), 'tile', split_axis=0, concat_a...]
    unnamed x68 -> x18, local copies, waits for them, and re-layouts: 19.7 us -> 3.74 us
    all_to_all x1 -> x0, starting transfers between devices: 8.59 us -> none  [on_device(): lax.all_to_all(mine.reshape(peers, 8, -1), 'tile', split_axis=0, concat_a...]
    ppermute x14 -> x9, starting transfers between devices: 16.2 us -> 7.89 us  [moved(): return lax.ppermute(value, 'tile', pairs)]
    pallas_call x11, Pallas kernels: 47 us -> 41.7 us  [the longest x1 17.7 us: forward(): pl.pallas_call(forward_kernel, grid_spec=pltpu.PrefetchScalarGridSpec(num...]
    all_to_all x1 -> x0, waiting for transfers between devices: 3.18 us -> none  [on_device(): lax.all_to_all(mine.reshape(peers, 8, -1), 'tile', split_axis=0, concat_a...]
    ppermute x14 -> x9, waiting for transfers between devices: 13.6 us -> 16.2 us  [moved(): return lax.ppermute(value, 'tile', pairs)]
    ppermute x3, waiting for transfers between devices: 2.1 us -> 0.01 us  [on_device(): lax.ppermute(shared, 'slide', [(i, (i + k) % 4) for i in range(4)])]
  transfers between devices with their start and end apart: 18 -> 12, of which waited for: 7 -> 6; matrix products, arithmetic and copies ran while one was open for 2% -> 0% of each run, Pallas kernels for 9% -> 10%
where the time goes in v2:
time: 98.3 us; the launch traced here: 96.9 us
  Pallas kernels  44.2 us (45%)
  blocking collectives  19 us (19%)
  waiting for transfers between devices  16.2 us (16%)
  starting transfers between devices  12.7 us (13%)
  local copies, waits for them, and re-layouts  4.07 us (4%)
    all_to_all x1, blocking collectives, on_device(): lax.all_to_all(mine.reshape(peers, 8, -1), 'tile', split_axis=0, concat_a...  19 us
    pallas_call x1, Pallas kernels, forward(): pl.pallas_call(forward_kernel, grid_spec=pltpu.PrefetchScalarGridSpec(num...  17.7 us
    ppermute x9, waiting for transfers between devices, moved(): return lax.ppermute(value, 'tile', pairs)  16.2 us
    pallas_call x1, Pallas kernels, attention(): pl.pallas_call(attention_kernel, in_specs=[SMEM, SMEM] + [VMEM] * 4 + [AN...  10.9 us
    ppermute x9, starting transfers between devices, moved(): return lax.ppermute(value, 'tile', pairs)  7.89 us
    pallas_call x4, Pallas kernels, grad_chunk(): pl.pallas_call(grad_kernel, in_specs=[VMEM] * 2, out_specs=VMEM, out_shap...  5.53 us
    pallas_call x1, Pallas kernels, transposed(): pl.pallas_call(transpose_kernel, grid=(tokens // patches,), in_specs=[ANY...  4.77 us
    ppermute x3, starting transfers between devices, on_device(): lax.ppermute(shared, 'slide', [(i, (i + k) % 4) for i in range(4)])  4.76 us
  transfers between devices with their start and end apart: 12, of which 6 were waited for; matrix products, arithmetic and copies ran while one was open for 0% of the time, Pallas kernels for 10%

profile of v2, /device:TPU:0, one launch (start us, length us, event | category | flops | bytes accessed | tf_op | source)
XLA Modules:
  0.0 96.9 jit_solution(14623473959632865050)
XLA Ops:
  0.8 0.7 copy-done.2
  1.5 17.7 %forward.1 = (bf16[1024,768]{1,0:T(8,128)(2,1)}, bf16[1024,768]{1,0:T(8,128)(2,1)}, bf16[8,1536]{1,0:T(8,128)(2,1)S(1)}, f32[4,2304]{1,0:T(4,128)S(1)}, f32[4,15...) custom-call(s32[5]{0:T(128)S(1)} %stack.23.place, bf16[1024,1536]{1,0:T(8,128)(2,1)} %bitcast.21, bf16[1536,1536]{1,0:T(8,128)(2,1)} %w_in.1, ...), custom_call_target="tpu_custom_call" | custom-call | tf_op jit(solution)/shard_map/forward/pallas_call | solution.py:130
  19.2 3.2 %collective-permute-start.2 = (f32[4,2304]{1,0:T(4,128)S(1)}, f32[4,2304]{1,0:T(4,128)S(1)}, u32[]{:S(2)}, u32[]{:S(2)}) collective-permute-start(f32[4,2304]{1,0:T(4,128)S(1)} %get-tuple-element.30.after.own), channel_id=1, source_target_pairs={{0,96},{32,0},{64,32},{96,64},{1,97},{33,1},{65,33},{97,65},{2,98}... | collective-permute-start | bytes 110600 | tf_op jit(solution)/shard_map/ppermute | solution.py:570
  22.3 0.6 collective-permute-start.1
  23.0 1.0 %collective-permute-start = (f32[4,2304]{1,0:T(4,128)S(1)}, f32[4,2304]{1,0:T(4,128)S(1)}, u32[]{:S(2)}, u32[]{:S(2)}) collective-permute-start(f32[4,2304]{1,0:T(4,128)S(1)} %get-tuple-element.30.after.own), channel_id=1, source_target_pairs={{0,32},{32,64},{64,96},{96,0},{1,33},{33,65},{65,97},{97,1},{2,34}... | collective-permute-start | bytes 110600 | tf_op jit(solution)/shard_map/ppermute | solution.py:570
  24.2 4.8 %transposed.1.normed_in = bf16[1536,1024]{1,0:T(8,128)(2,1)} custom-call(f32[4,2304]{1,0:T(4,128)S(1)} %get-tuple-element.30.after.own, bf16[1024,1536]{1,0:T(8,128)(2,1)} %get-tuple-element.33.normed), custom_call_target="tpu_custom_call" | custom-call | flops 20000000 | bytes 9000000 | tf_op jit(solution)/shard_map/transposed/pallas_call | solution.py:175
  29.0 0.6 embed.1
  29.7 0.5 collective-permute-start.4
  30.2 19.0 %all_to_all.5 = bf16[32,8,896]{2,1,0:T(8,128)(2,1)S(1)} all-to-all(bf16[32,8,896]{2,1,0:T(8,128)(2,1)S(1)} %bitcast.17), channel_id=1, replica_groups=mesh['slide'=4,'tile'=32] {'tile'}, dimensions={0} | all-to-all | bytes 917504 | tf_op jit(solution)/shard_map/all_to_all | solution.py:578
  49.2 1.2 %copy-done.7 = bf16[1024,768]{1,0:T(8,128)(2,1)} copy-done((bf16[1024,768]{1,0:T(8,128)(2,1)}, bf16[1024,768]{1,0:T(8,128)(2,1)S(1)}, u32[]{:S(2)}) %copy-start.7) | copy-done | bytes 1572888
  50.4 1.1 %copy-done.6 = bf16[1536,1024]{1,0:T(8,128)(2,1)} copy-done((bf16[1536,1024]{1,0:T(8,128)(2,1)}, bf16[1536,1024]{1,0:T(8,128)(2,1)S(1)}, u32[]{:S(2)}) %copy-start.6) | copy-done | bytes 3145752
  51.5 10.9 %attention.1 = (bf16[2048,768]{1,0:T(8,128)(2,1)S(1)}, bf16[384,2048]{1,0:T(8,128)(2,1)S(1)}, bf16[384,2048]{1,0:T(8,128)(2,1)S(1)}, bf16[384,2048]{1,0:T(8,128)...) custom-call(s32[5]{0:T(128)S(1)} %stack.23.place, ...), custom_call_target="tpu_custom_call" | custom-call | tf_op jit(solution)/shard_map/attention/pallas_call | solution.py:383
  62.4 1.4 %grad_chunk.6 = bf16[384,768]{1,0:T(8,128)(2,1)S(1)} custom-call(bf16[384,2048]{1,0:T(8,128)(2,1)S(1)} %get-tuple-element.48.lhs, bf16[2048,768]{1,0:T(8,128)(2,1)S(1)} %get-tuple-element.46.d_preact), custom_call_target="tpu_custom_call" | custom-call | flops 1000 | bytes 1000 | tf_op jit(solution)/shard_map/grad_chunk/pallas_call | solution.py:455
  63.8 1.4 %grad_chunk.7 = bf16[384,768]{1,0:T(8,128)(2,1)S(1)} custom-call(bf16[384,2048]{1,0:T(8,128)(2,1)S(1)} %get-tuple-element.49.lhs, bf16[2048,768]{1,0:T(8,128)(2,1)S(1)} %get-tuple-element.46.d_preact), custom_call_target="tpu_custom_call" | custom-call | flops 1000 | bytes 1000 | tf_op jit(solution)/shard_map/grad_chunk/pallas_call | solution.py:455
  65.2 0.8 collective-permute-start.7
  65.9 1.9 %collective-permute-start.6 = (bf16[384,768]{1,0:T(8,128)(2,1)S(1)}, bf16[384,768]{1,0:T(8,128)(2,1)S(1)}, u32[]{:S(2)}, u32[]{:S(2)}) collective-permute-start(bf16[384,768]{1,0:T(8,128)(2,1)S(1)} %grad_chunk.6), channel_id=1, source_target_pairs={{0,4},{1,17},{2,6},{3,19},{4,0},{5,21},{6,2},{7,23},{8,12},{9,25},... | collective-permute-start | bytes 1769480 | tf_op jit(solution)/shard_map/ppermute | solution.py:529
  67.9 1.4 %grad_chunk.5 = bf16[384,768]{1,0:T(8,128)(2,1)S(1)} custom-call(bf16[384,2048]{1,0:T(8,128)(2,1)S(1)} %get-tuple-element.47.lhs, bf16[2048,768]{1,0:T(8,128)(2,1)S(1)} %get-tuple-element.46.d_preact), custom_call_target="tpu_custom_call" | custom-call | flops 1000 | bytes 1000 | tf_op jit(solution)/shard_map/grad_chunk/pallas_call | solution.py:455
  69.3 0.3 collective-permute-start.5
  69.6 1.4 %grad_chunk.4.one = bf16[384,768]{1,0:T(8,128)(2,1)S(1)} custom-call(bf16[384,2048]{1,0:T(8,128)(2,1)S(1)} %get-tuple-element.45.lhs, bf16[2048,768]{1,0:T(8,128)(2,1)S(1)} %get-tuple-element.46.d_preact), custom_call_target="tpu_custom_call" | custom-call | flops 1000 | bytes 1000 | tf_op jit(solution)/shard_map/grad_chunk/pallas_call | solution.py:455
  71.0 2.5 %outputs.1 = (f32[4,768]{1,0:T(4,128)}, f32[48,1536]{1,0:T(8,128)}) custom-call(s32[5]{0:T(128)S(1)} %stack.23.place, f32[128,768]{1,0:T(8,128)S(1)} %get-tuple-element.40.context, bf16[128,768]{1,0:T(8,128)(2,1)S(1)} %get-tuple-element.41.slide_rows, bf16[768,768]{1,0:T(8,128)(2,1)S(1)} %copy-done, s32[1,128]{1,0:T(1,128)S(1)} %bitcast.19, ...), custom_call_target="tpu_custom_call" | custom-call | flops 1000 | bytes 1000 | tf_op jit(solution)/shard_map/outputs/pallas_call | solution.py:438
  73.5 1.6 %collective-permute-done.7.four = bf16[384,768]{1,0:T(8,128)(2,1)S(1)} collective-permute-done((bf16[384,768]{1,0:T(8,128)(2,1)S(1)}, bf16[384,768]{1,0:T(8,128)(2,1)S(1)}, u32[]{:S(2)}, u32[]{:S(2)}) %collective-permute-start.7) | collective-permute-done | bytes 589856 | tf_op jit(solution)/shard_map/ppermute | solution.py:529
  75.1 2.3 %collective-permute-done.6.three = bf16[384,768]{1,0:T(8,128)(2,1)S(1)} collective-permute-done((bf16[384,768]{1,0:T(8,128)(2,1)S(1)}, bf16[384,768]{1,0:T(8,128)(2,1)S(1)}, u32[]{:S(2)}, u32[]{:S(2)}) %collective-permute-start.6) | collective-permute-done | bytes 589856 | tf_op jit(solution)/shard_map/ppermute | solution.py:529
  77.4 6.2 %collective-permute-done.5.two = bf16[384,768]{1,0:T(8,128)(2,1)S(1)} collective-permute-done((bf16[384,768]{1,0:T(8,128)(2,1)S(1)}, bf16[384,768]{1,0:T(8,128)(2,1)S(1)}, u32[]{:S(2)}, u32[]{:S(2)}) %collective-permute-start.5) | collective-permute-done | bytes 589856 | tf_op jit(solution)/shard_map/ppermute | solution.py:529
  83.7 0.7 copy-done.1
  84.7 0.7 collective-permute-start.8
  85.4 2.0 %collective-permute-start.9 = (bf16[96,768]{1,0:T(8,128)(2,1)S(1)}, bf16[96,768]{1,0:T(8,128)(2,1)S(1)}, u32[]{:S(2)}, u32[]{:S(2)}) collective-permute-start(bf16[96,768]{1,0:T(8,128)(2,1)S(1)} %get-tuple-element.52), channel_id=1, source_target_pairs={{0,16},{1,5},{2,18},{3,7},{4,20},{5,1},{6,22},{7,3},{8,24},{9,13},... | collective-permute-start | bytes 442376 | tf_op jit(solution)/shard_map/ppermute | solution.py:529
  87.3 1.5 %collective-permute-start.10 = (bf16[96,768]{1,0:T(8,128)(2,1)S(1)}, bf16[96,768]{1,0:T(8,128)(2,1)S(1)}, u32[]{:S(2)}, u32[]{:S(2)}) collective-permute-start(bf16[96,768]{1,0:T(8,128)(2,1)S(1)} %get-tuple-element.53), channel_id=1, source_target_pairs={{0,24},{1,7},{2,26},{3,1},{4,28},{5,3},{6,30},{7,5},{8,0},{9,15},{... | collective-permute-start | bytes 442376 | tf_op jit(solution)/shard_map/ppermute | solution.py:529
  88.8 3.8 %collective-permute-done.8.two = bf16[96,768]{1,0:T(8,128)(2,1)S(1)} collective-permute-done((bf16[96,768]{1,0:T(8,128)(2,1)S(1)}, bf16[96,768]{1,0:T(8,128)(2,1)S(1)}, u32[]{:S(2)}, u32[]{:S(2)}) %collective-permute-start.8) | collective-permute-done | bytes 147488 | tf_op jit(solution)/shard_map/ppermute | solution.py:529
  92.7 0.9 collective-permute-done.10.four
  93.5 0.6 split.1
  94.2 1.4 %collective-permute-done.11.received = f32[48,768]{1,0:T(8,128)S(1)} collective-permute-done((f32[48,768]{1,0:T(8,128)S(1)}, f32[48,768]{1,0:T(8,128)S(1)}, u32[]{:S(2)}, u32[]{:S(2)}) %collective-permute-start.11) | collective-permute-done | bytes 147488 | tf_op jit(solution)/shard_map/ppermute | solution.py:529
  95.6 1.3 %finish.1 = f32[48,1536]{1,0:T(8,128)} custom-call(s32[5]{0:T(128)S(1)} %stack.23.place, f32[48,768]{1,0:T(8,128)S(1)} %get-tuple-element.54.keep, f32[48,768]{1,0:T(8,128)S(1)} %collective-permute-done.11.received), custom_call_target="tpu_custom_call" | custom-call | tf_op jit(solution)/shard_map/finish/pallas_call | solution.py:513
  (28 shorter events, 0.8 us)
Async XLA Ops:
  0.8 0.7 copy-start.2
  1.5 22.5 %copy-start.8 = (s32[16]{0:T(128)S(1)}, s32[16]{0:T(128)}, u32[]{:S(2)}) copy-start(s32[16]{0:T(128)} %param.19) | copy-start | bytes 196
  19.2 9.8 %collective-permute-start.2 = (f32[4,2304]{1,0:T(4,128)S(1)}, f32[4,2304]{1,0:T(4,128)S(1)}, u32[]{:S(2)}, u32[]{:S(2)}) collective-permute-start(f32[4,2304]{1,0:T(4,128)S(1)} %get-tuple-element.30.after.own), channel_id=1, source_target_pairs={{0,96},{32,0},{64,32},{96,64},{1,97},{33,1},{65,33},{97,65},{2,98}... | collective-permute-start | bytes 110600 | tf_op jit(solution)/shard_map/ppermute | solution.py:570
  22.3 6.6 %collective-permute-start.1 = (f32[4,2304]{1,0:T(4,128)S(1)}, f32[4,2304]{1,0:T(4,128)S(1)}, u32[]{:S(2)}, u32[]{:S(2)}) collective-permute-start(f32[4,2304]{1,0:T(4,128)S(1)} %get-tuple-element.30.after.own), channel_id=1, source_target_pairs={{0,64},{32,96},{64,0},{96,32},{1,65},{33,97},{65,1},{97,33},{2,66}... | collective-permute-start | bytes 110600 | tf_op jit(solution)/shard_map/ppermute | solution.py:570
  23.0 6.0 %collective-permute-start = (f32[4,2304]{1,0:T(4,128)S(1)}, f32[4,2304]{1,0:T(4,128)S(1)}, u32[]{:S(2)}, u32[]{:S(2)}) collective-permute-start(f32[4,2304]{1,0:T(4,128)S(1)} %get-tuple-element.30.after.own), channel_id=1, source_target_pairs={{0,32},{32,64},{64,96},{96,0},{1,33},{33,65},{65,97},{97,1},{2,34}... | collective-permute-start | bytes 110600 | tf_op jit(solution)/shard_map/ppermute | solution.py:570
  29.0 22.5 %copy-start.3 = (s32[128]{0:T(128)S(1)}, s32[128]{0:T(128)}, u32[]{:S(2)}) copy-start(s32[128]{0:T(128)} %param.17) | copy-start | bytes 1540
  29.0 22.5 %copy-start.4 = (s32[3]{0:T(128)S(1)}, s32[3]{0:T(128)}, u32[]{:S(2)}) copy-start(s32[3]{0:T(128)} %seg_len.1) | copy-start | bytes 40
  29.0 22.5 %copy-start.5 = (s32[128]{0:T(128)S(1)}, s32[128]{0:T(128)}, u32[]{:S(2)}) copy-start(s32[128]{0:T(128)} %param.18) | copy-start | bytes 1540
  29.6 19.5 %collective-permute-start.3 = (bf16[1536,1024]{1,0:T(8,128)(2,1)}, bf16[1536,1024]{1,0:T(8,128)(2,1)S(1)}, u32[]{:S(2)}, u32[]{:S(2)}) collective-permute-start(bf16[1536,1024]{1,0:T(8,128)(2,1)} %get-tuple-element.37.normed_own), channel_id=1, source_target_pairs={{0,1},{1,0},{2,3},{3,2},{4,5},{5,4},{6,7},{7,6},{8,9},{9,8},{10,11... | collective-permute-start | bytes 9437192 | tf_op jit(solution)/shard_map/ppermute | solution.py:529
  29.7 19.5 %collective-permute-start.4 = (bf16[1024,768]{1,0:T(8,128)(2,1)}, bf16[1024,768]{1,0:T(8,128)(2,1)S(1)}, u32[]{:S(2)}, u32[]{:S(2)}) collective-permute-start(bf16[1024,768]{1,0:T(8,128)(2,1)} %get-tuple-element.39), channel_id=1, source_target_pairs={{0,1},{1,0},{2,3},{3,2},{4,5},{5,4},{6,7},{7,6},{8,9},{9,8},{10,11... | collective-permute-start | bytes 4718600 | tf_op jit(solution)/shard_map/ppermute | solution.py:529
  49.2 1.3 %copy-start.7 = (bf16[1024,768]{1,0:T(8,128)(2,1)}, bf16[1024,768]{1,0:T(8,128)(2,1)S(1)}, u32[]{:S(2)}) copy-start(bf16[1024,768]{1,0:T(8,128)(2,1)S(1)} %collective-permute-done.4.slope_other) | copy-start | bytes 4718596
  49.2 2.3 %copy-start.6 = (bf16[1536,1024]{1,0:T(8,128)(2,1)}, bf16[1536,1024]{1,0:T(8,128)(2,1)S(1)}, u32[]{:S(2)}) copy-start(bf16[1536,1024]{1,0:T(8,128)(2,1)S(1)} %collective-permute-done.3.normed_other) | copy-start | bytes 9437188
  65.2 10.0 %collective-permute-start.7 = (bf16[384,768]{1,0:T(8,128)(2,1)S(1)}, bf16[384,768]{1,0:T(8,128)(2,1)S(1)}, u32[]{:S(2)}, u32[]{:S(2)}) collective-permute-start(bf16[384,768]{1,0:T(8,128)(2,1)S(1)} %grad_chunk.7), channel_id=1, source_target_pairs={{0,6},{1,25},{2,0},{3,27},{4,2},{5,29},{6,4},{7,31},{8,14},{9,1},{... | collective-permute-start | bytes 1769480 | tf_op jit(solution)/shard_map/ppermute | solution.py:529
  65.9 11.5 %collective-permute-start.6 = (bf16[384,768]{1,0:T(8,128)(2,1)S(1)}, bf16[384,768]{1,0:T(8,128)(2,1)S(1)}, u32[]{:S(2)}, u32[]{:S(2)}) collective-permute-start(bf16[384,768]{1,0:T(8,128)(2,1)S(1)} %grad_chunk.6), channel_id=1, source_target_pairs={{0,4},{1,17},{2,6},{3,19},{4,0},{5,21},{6,2},{7,23},{8,12},{9,25},... | collective-permute-start | bytes 1769480 | tf_op jit(solution)/shard_map/ppermute | solution.py:529
  69.3 14.4 %collective-permute-start.5 = (bf16[384,768]{1,0:T(8,128)(2,1)S(1)}, bf16[384,768]{1,0:T(8,128)(2,1)S(1)}, u32[]{:S(2)}, u32[]{:S(2)}) collective-permute-start(bf16[384,768]{1,0:T(8,128)(2,1)S(1)} %grad_chunk.5), channel_id=1, source_target_pairs={{0,2},{1,9},{2,4},{3,11},{4,6},{5,13},{6,0},{7,15},{8,10},{9,17},{... | collective-permute-start | bytes 1769480 | tf_op jit(solution)/shard_map/ppermute | solution.py:529
  69.6 1.4 %copy-start = (bf16[768,768]{1,0:T(8,128)(2,1)S(1)}, bf16[768,768]{1,0:T(8,128)(2,1)}, u32[]{:S(2)}) copy-start(bf16[768,768]{1,0:T(8,128)(2,1)} %w_attn.1) | copy-start | bytes 3538948
  83.7 0.7 copy-start.1
  84.7 8.0 %collective-permute-start.8 = (bf16[96,768]{1,0:T(8,128)(2,1)S(1)}, bf16[96,768]{1,0:T(8,128)(2,1)S(1)}, u32[]{:S(2)}, u32[]{:S(2)}) collective-permute-start(bf16[96,768]{1,0:T(8,128)(2,1)S(1)} %get-tuple-element.51), channel_id=1, source_target_pairs={{0,8},{1,3},{2,10},{3,5},{4,12},{5,7},{6,14},{7,1},{8,16},{9,11},{... | collective-permute-start | bytes 442376 | tf_op jit(solution)/shard_map/ppermute | solution.py:529
  85.4 7.3 %collective-permute-start.9 = (bf16[96,768]{1,0:T(8,128)(2,1)S(1)}, bf16[96,768]{1,0:T(8,128)(2,1)S(1)}, u32[]{:S(2)}, u32[]{:S(2)}) collective-permute-start(bf16[96,768]{1,0:T(8,128)(2,1)S(1)} %get-tuple-element.52), channel_id=1, source_target_pairs={{0,16},{1,5},{2,18},{3,7},{4,20},{5,1},{6,22},{7,3},{8,24},{9,13},... | collective-permute-start | bytes 442376 | tf_op jit(solution)/shard_map/ppermute | solution.py:529
  87.3 6.2 %collective-permute-start.10 = (bf16[96,768]{1,0:T(8,128)(2,1)S(1)}, bf16[96,768]{1,0:T(8,128)(2,1)S(1)}, u32[]{:S(2)}, u32[]{:S(2)}) collective-permute-start(bf16[96,768]{1,0:T(8,128)(2,1)S(1)} %get-tuple-element.53), channel_id=1, source_target_pairs={{0,24},{1,7},{2,26},{3,1},{4,28},{5,3},{6,30},{7,5},{8,0},{9,15},{... | collective-permute-start | bytes 442376 | tf_op jit(solution)/shard_map/ppermute | solution.py:529
  94.1 1.5 %collective-permute-start.11 = (f32[48,768]{1,0:T(8,128)S(1)}, f32[48,768]{1,0:T(8,128)S(1)}, u32[]{:S(2)}, u32[]{:S(2)}) collective-permute-start(f32[48,768]{1,0:T(8,128)S(1)} %get-tuple-element.55), channel_id=1, source_target_pairs={{0,1},{1,0},{2,3},{3,2},{4,5},{5,4},{6,7},{7,6},{8,9},{9,8},{10,11... | collective-permute-start | bytes 442376 | tf_op jit(solution)/shard_map/ppermute | solution.py:529

commit v3 on v2

--- a/solution.py
+++ b/solution.py
@@ -62,97 +62,126 @@
 
 
 def forward_kernel(
-    place, tiles_hbm, w_in, w_out, cot, slope_send, slope_keep, pooled, shared, token_mean, normed_hbm, tiles, normed, total, sems
+    tiles_hbm,
+    w_in_hbm,
+    w_out_hbm,
+    cot_hbm,
+    slope_send,
+    slope_keep,
+    pooled,
+    shared,
+    token_mean,
+    normed_hbm,
+    tiles,
+    normed,
+    w_in,
+    w_out,
+    slope,
+    total,
+    cot,
+    tile_sems,
+    in_sems,
+    out_sems,
+    normed_sems,
+    slope_sems,
+    cot_sem,
 ):
-    step = pl.program_id(0)
-    steps = pl.num_programs(0)
+    core = lax.axis_index("tile") % 2
     tile_count = token_mean.shape[0]
     patches = tiles.shape[0] // tile_count
+    steps, _, block = w_in.shape
+    half = steps // 2
     pieces = [pl.ds(tile * patches, patches) for tile in range(tile_count)]
-    out_copies = [
-        pltpu.make_async_copy(normed.at[rows], normed_hbm.at[rows], sems.at[tile_count + tile])
-        for tile, rows in enumerate(pieces)
-    ]
-
-    @pl.when(step == 0)
-    def _():
-        in_copies = [
-            pltpu.make_async_copy(tiles_hbm.at[rows], tiles.at[rows], sems.at[tile]) for tile, rows in enumerate(pieces)
-        ]
-        for copy in in_copies:
-            copy.start()
-        for tile, rows in enumerate(pieces):
-            in_copies[tile].wait()
-            values = tiles[rows, :].astype(F4)
-            token_mean[pl.ds(tile, 1), :] = jnp.sum(values, axis=0, keepdims=True) * (1.0 / patches)
-            normed[rows, :] = standardise(values).astype(BF)
-            out_copies[tile].start()
-        total[...] = jnp.zeros_like(total)
-
-    def work(slope):
-        means = []
-        for rows in pieces:
-            value, rate = gelu_pair(dot_nn(normed[rows, :], w_in[...]))
-            slope[rows, :] = rate.astype(BF)
-            means.append(jnp.sum(value, axis=0, keepdims=True) * (1.0 / patches))
-        high, low = halves(jnp.concatenate(means, axis=0))
-        both = jnp.concatenate([high, low], axis=0)
-        pooled[...] = both
-        total[...] += dot_nn(both, w_out[...])
-
-    @pl.when(step < steps // 2)
-    def _():
-        work(slope_send)
-
-    @pl.when(step >= steps // 2)
-    def _():
-        work(slope_keep)
-
-    @pl.when(step == steps - 1)
-    def _():
-        width = total.shape[1]
-        shared[:, :width] = total[:tile_count, :] + total[tile_count:, :]
-        shared[:, width:] = cot[...]
-        for copy in out_copies:
-            copy.wait()
-
-
-def forward(place, tiles, w_in, w_out, cot, tile_count):
+
+    def load_tile(tile):
+        return pltpu.make_async_copy(tiles_hbm.at[pieces[tile]], tiles.at[pieces[tile]], tile_sems.at[tile])
+
+    def columns(j):
+        return pl.ds(pl.multiple_of((j + half * (1 - core)) % steps * block, block), block)
+
+    def load_in(j):
+        return pltpu.make_async_copy(w_in_hbm.at[:, columns(j)], w_in.at[j], in_sems.at[j])
+
+    def load_out(j):
+        return pltpu.make_async_copy(w_out_hbm.at[columns(j)], w_out.at[j], out_sems.at[j])
+
+    def store_normed(tile):
+        return pltpu.make_async_copy(normed.at[pieces[tile]], normed_hbm.at[pieces[tile]], normed_sems.at[tile])
+
+    def store_slope(j, target):
+        at = pl.ds(j % half * block, block)
+        return pltpu.make_async_copy(slope.at[j], target.at[:, at], slope_sems.at[j])
+
+    for tile in range(tile_count):
+        load_tile(tile).start()
+    load_in(0).start()
+    load_cot = pltpu.make_async_copy(cot_hbm, cot, cot_sem.at[0])
+    load_cot.start()
+    for tile in range(tile_count):
+        load_tile(tile).wait()
+        if tile == 0:
+            load_in(1).start()
+            load_out(0).start()
+        if tile == 2:
+            load_in(2).start()
+            load_out(1).start()
+        values = tiles[pieces[tile], :].astype(F4)
+        token_mean[pl.ds(tile, 1), :] = jnp.sum(values, axis=0, keepdims=True) * (1.0 / patches)
+        normed[pieces[tile], :] = standardise(values).astype(BF)
+        store_normed(tile).start()
+
+    size = 128
+    blocks = tiles.shape[0] // size
+    per_tile = patches // size
+    total[...] = jnp.zeros_like(total)
+
+    def product(item):
+        j, part = item // blocks, item % blocks
+        if part == 0:
+            load_in(j).wait()
+            if j + 3 < steps:
+                load_in(j + 3).start()
+            if j + 2 < steps:
+                load_out(j + 2).start()
+        return dot_nn(normed[pl.ds(part * size, size), :], w_in[j])
+
+    preact, sums = product(0), []
+    for item in range(steps * blocks):
+        j, part = item // blocks, item % blocks
+        later = product(item + 1) if item + 1 < steps * blocks else None
+        value, rate = gelu_pair(preact)
+        slope[j, pl.ds(part * size, size), :] = rate.astype(BF)
+        sums.append(jnp.sum(value, axis=0, keepdims=True) * (1.0 / patches))
+        preact = later
+        if part == blocks - 1:
+            store_slope(j, slope_send if j < half else slope_keep).start()
+            means = [sum(sums[i : i + per_tile]) for i in range(0, blocks, per_tile)]
+            high, low = halves(jnp.concatenate(means, axis=0))
+            both = jnp.concatenate([high, low], axis=0)
+            pooled[:, columns(j)] = both
+            load_out(j).wait()
+            total[...] += dot_nn(both, w_out[j])
+            sums = []
+    for j in range(steps):
+        store_slope(j, slope_send if j < half else slope_keep).wait()
+    width = total.shape[1]
+    shared[:, :width] = total[:tile_count, :] + total[tile_count:, :]
+    load_cot.wait()
+    shared[:, width:] = cot[...]
+    for tile in range(tile_count):
+        store_normed(tile).wait()
+
+
+def forward(tiles, w_in, w_out, cot, tile_count):
     tokens, width = tiles.shape
     hidden = w_in.shape[1]
     block = 256
     steps = hidden // block
     slide_width = cot.shape[1]
-
-    def at(j, place):
-        return (j + steps // 2 * (1 - place[2])) % steps
-
     return pl.pallas_call(
         forward_kernel,
-        grid_spec=pltpu.PrefetchScalarGridSpec(
-            num_scalar_prefetch=1,
-            grid=(steps,),
-            in_specs=[
-                ANY,
-                pl.BlockSpec((width, block), lambda j, place: (0, at(j, place))),
-                pl.BlockSpec((block, width), lambda j, place: (at(j, place), 0)),
-                pl.BlockSpec((tile_count, slide_width), lambda j, place: (0, 0)),
-            ],
-            out_specs=[
-                pl.BlockSpec((tokens, block), lambda j, place: (0, jnp.minimum(j, steps // 2 - 1))),
-                pl.BlockSpec((tokens, block), lambda j, place: (0, jnp.maximum(j - steps // 2, 0))),
-                pl.BlockSpec((2 * tile_count, block), lambda j, place: (0, at(j, place))),
-                pl.BlockSpec((tile_count, width + slide_width), lambda j, place: (0, 0)),
-                pl.BlockSpec((tile_count, width), lambda j, place: (0, 0)),
-                ANY,
-            ],
-            scratch_shapes=[
-                pltpu.VMEM((tokens, width), BF),
-                pltpu.VMEM((tokens, width), BF),
-                pltpu.VMEM((2 * tile_count, width), F4),
-                pltpu.SemaphoreType.DMA((2 * tile_count,)),
-            ],
-        ),
+        in_specs=[ANY] * 4,
+        out_specs=[ANY, ANY, VMEM, VMEM, VMEM, ANY],
         out_shape=[
             pltpu.HBM((tokens, hidden // 2), BF),
             pltpu.HBM((tokens, hidden // 2), BF),
@@ -161,9 +190,24 @@
             jax.ShapeDtypeStruct((tile_count, width), F4),
             pltpu.HBM((tokens, width), BF),
         ],
-        compiler_params=pltpu.CompilerParams(vmem_limit_bytes=32 * MIB),
+        scratch_shapes=[
+            pltpu.VMEM((tokens, width), BF),
+            pltpu.VMEM((tokens, width), BF),
+            pltpu.VMEM((steps, width, block), BF),
+            pltpu.VMEM((steps, block, width), BF),
+            pltpu.VMEM((steps, tokens, block), BF),
+            pltpu.VMEM((2 * tile_count, width), F4),
+            pltpu.VMEM(cot.shape, F4),
+            pltpu.SemaphoreType.DMA((tile_count,)),
+            pltpu.SemaphoreType.DMA((steps,)),
+            pltpu.SemaphoreType.DMA((steps,)),
+            pltpu.SemaphoreType.DMA((tile_count,)),
+            pltpu.SemaphoreType.DMA((steps,)),
+            pltpu.SemaphoreType.DMA((1,)),
+        ],
+        compiler_params=pltpu.CompilerParams(vmem_limit_bytes=40 * MIB),
         name="forward",
-    )(place, from_hbm(tiles), from_hbm(w_in), from_hbm(w_out), cot)
+    )(from_hbm(tiles), from_hbm(w_in), from_hbm(w_out), from_hbm(cot))
 
 
 def transpose_kernel(after, normed, out):
@@ -227,10 +271,10 @@
 def attention_kernel(
     place,
     seg_len,
-    gathered,
-    cot_all,
     slide_of,
     order_of,
+    gathered_hbm,
+    cot_hbm,
     w_proj_hbm,
     w_qkv_hbm,
     w_attn_hbm,
@@ -244,7 +288,8 @@
     lhs1,
     lhs2,
     lhs3,
-    d_embed,
+    d_qkv,
+    d_direct,
     context,
     slide_rows,
     pooled_pair,
@@ -253,14 +298,17 @@
     w_qkv,
     w_attn,
     w_out,
+    gathered,
+    cot_all,
     sems,
 ):
     hidden = w_out.shape[0]
     half_rows = pl.ds(pl.multiple_of(place[2] * hidden, hidden), hidden)
     pairs = [(w_proj_hbm, w_proj), (w_qkv_hbm, w_qkv), (w_attn_hbm, w_attn), (w_out_hbm.at[half_rows], w_out)]
+    pairs += [(gathered_hbm, gathered), (cot_hbm, cot_all)]
     loads = [pltpu.make_async_copy(src, dst, sems.at[34 + i]) for i, (src, dst) in enumerate(pairs)]
-    for load in loads:
-        load.start()
+    for index in (4, 0, 5, 2, 1):
+        loads[index].start()
 
     tokens = slope_own.shape[0]
     rows_each = lhs0.shape[0] // 4
@@ -280,27 +328,10 @@
             copies.append(
                 pltpu.make_async_copy(normed_other.at[source], lhs.at[rows, pl.ds(tokens, tokens)], sems.at[at + 1])
             )
-    for copy in copies:
-        copy.start()
-
     tiles = slide_of.shape[1]
     half = w_proj.shape[0] // 2
     width = w_proj.shape[1]
     head = width // HEADS
-
-    row = lax.broadcasted_iota(jnp.int32, (tiles, 2 * tiles), 0)
-    col = lax.broadcasted_iota(jnp.int32, (tiles, 2 * tiles), 1)
-    first = (row // 4) * 8 + row % 4
-    every = gathered[...]
-    left = dot_nn((col == first).astype(F4).astype(BF), every).astype(BF)
-    right = dot_nn((col == first + 4).astype(F4).astype(BF), every).astype(BF)
-    pooled_pair[:, :128] = left[:, half:]
-    pooled_pair[:, 128:] = right[:, half:]
-    loads[0].wait()
-    rows = (dot_nn(left[:, :half], w_proj[:half, :]) + dot_nn(right[:, :half], w_proj[half:, :])).astype(BF)
-    slide_rows[...] = rows
-    loads[1].wait()
-    qkv = dot_nn(rows, w_qkv[...]).astype(BF)
 
     slide = slide_of[...].astype(F4)
     order = order_of[...].astype(F4)
@@ -315,10 +346,28 @@
     slide_col = jnp.broadcast_to(slide, (tiles, tiles)).T
     lane = lax.broadcasted_iota(jnp.int32, (tiles, 16), 1).astype(F4)
     member = (slide_col[:, :16] == lane).astype(F4).astype(BF)
+    row = lax.broadcasted_iota(jnp.int32, (tiles, 2 * tiles), 0)
+    col = lax.broadcasted_iota(jnp.int32, (tiles, 2 * tiles), 1)
+    first = (row // 4) * 8 + row % 4
+    loads[4].wait()
+    every = gathered[...]
+    left = dot_nn((col == first).astype(F4).astype(BF), every).astype(BF)
+    right = dot_nn((col == first + 4).astype(F4).astype(BF), every).astype(BF)
+    pooled_pair[:, :128] = left[:, half:]
+    pooled_pair[:, 128:] = right[:, half:]
+    loads[0].wait()
+    rows = (dot_nn(left[:, :half], w_proj[:half, :]) + dot_nn(right[:, :half], w_proj[half:, :])).astype(BF)
+    slide_rows[...] = rows
+    loads[5].wait()
     cot_high, cot_low = halves(cot_all[...])
     d_attended = dot_nn(member, cot_high) + dot_nn(member, cot_low)
     loads[2].wait()
     d_context = dot_nt(d_attended.astype(BF), w_attn[...]).astype(BF)
+    loads[1].wait()
+    loads[3].start()
+    for copy in copies:
+        copy.start()
+    qkv = dot_nn(rows, w_qkv[...]).astype(BF)
 
     scale = 1.0 / math.sqrt(head)
     group_heads = HEADS // 2
@@ -356,11 +405,13 @@
         grads["query", group] = dot_nn(beside(d_scores), stacked(key_rows))
         grads["key", group] = dot_nn(beside([part.T for part in d_scores]), query_stack)
         grads["value", group] = dot_nn(beside([part.T for part in shares]), d_out_stack)
-    d_qkv = beside([grads[name, group].astype(BF) for name in ("query", "key", "value") for group in range(2)])
-
-    d_slide = d_attended + dot_nt(d_qkv, w_qkv[...])
-    d_embed[...] = dot_nt(d_slide.astype(BF), w_proj[...])
-    eight = d_embed[pl.ds(pl.multiple_of(place[1] // 2 * 8, 8), 8), :]
+    d_qkv[...] = beside([grads[name, group].astype(BF) for name in ("query", "key", "value") for group in range(2)])
+    d_direct[...] = d_attended
+
+    near = pl.ds(pl.multiple_of(place[1] // 4 * 16, 16), 16)
+    d_slide = d_direct[near, :] + dot_nt(d_qkv[near, :], w_qkv[...])
+    d_embed = dot_nt(d_slide.astype(BF), w_proj[...])
+    eight = jnp.where(place[1] // 2 % 2 == 0, d_embed[:8, :], d_embed[8:, :])
     high, low = halves(eight)
     loads[3].wait()
     back = dot_nt(jnp.concatenate([high, low], axis=0), w_out[...])
@@ -382,12 +433,13 @@
     tokens = slopes[0].shape[0]
     return pl.pallas_call(
         attention_kernel,
-        in_specs=[SMEM, SMEM] + [VMEM] * 4 + [ANY] * 8,
-        out_specs=[VMEM] * 9,
+        in_specs=[SMEM, SMEM] + [VMEM] * 2 + [ANY] * 10,
+        out_specs=[VMEM] * 10,
         out_shape=[
             pltpu.VMEM((2 * tokens, hidden), BF),
             *[pltpu.VMEM((width // 4, 2 * tokens), BF)] * 4,
-            jax.ShapeDtypeStruct((tiles, width), F4),
+            jax.ShapeDtypeStruct((tiles, 3 * slide_width), BF),
+            jax.ShapeDtypeStruct((tiles, slide_width), F4),
             jax.ShapeDtypeStruct((tiles, slide_width), F4),
             jax.ShapeDtypeStruct((tiles, slide_width), BF),
             jax.ShapeDtypeStruct((tiles, 256), BF),
@@ -398,51 +450,91 @@
             pltpu.VMEM(w_qkv.shape, BF),
             pltpu.VMEM(w_attn.shape, BF),
             pltpu.VMEM((hidden, width), BF),
-            pltpu.SemaphoreType.DMA((38,)),
+            pltpu.VMEM(gathered.shape, BF),
+            pltpu.VMEM(cot_all.shape, F4),
+            pltpu.SemaphoreType.DMA((40,)),
         ],
         compiler_params=pltpu.CompilerParams(vmem_limit_bytes=24 * MIB),
         name="attention",
     )(
         place,
         seg_len,
-        gathered,
-        cot_all,
         slide_of,
         order_of,
-        *[from_hbm(value) for value in (*weights, *normed, *slopes)],
+        *[from_hbm(value) for value in (gathered, cot_all, *weights, normed[0])],
+        normed[1],
+        from_hbm(slopes[0]),
+        slopes[1],
     )
 
 
-def outputs_kernel(place, context, slide_rows, w_attn, slide_of, counts, pooled_pair, d_embed, slide_embed, grad_out):
+def outputs_kernel(
+    place,
+    context,
+    slide_rows,
+    slide_of,
+    counts,
+    pooled_pair,
+    d_qkv,
+    d_direct,
+    w_attn_hbm,
+    w_qkv_hbm,
+    w_proj_hbm,
+    slide_embed,
+    grad_out,
+    w_attn,
+    w_qkv,
+    w_proj,
+    sems,
+):
+    pairs = [(w_attn_hbm, w_attn), (w_qkv_hbm, w_qkv), (w_proj_hbm, w_proj)]
+    loads = [pltpu.make_async_copy(src, dst, sems.at[i]) for i, (src, dst) in enumerate(pairs)]
+    for load in loads:
+        load.start()
     tiles = slide_of.shape[1]
-    high, low = halves(context[...])
-    attended = slide_rows[...].astype(F4) + dot_nn(high, w_attn[...]) + dot_nn(low, w_attn[...])
     group = lax.broadcasted_iota(jnp.int32, (16, tiles), 0)
     member = (slide_of[...] == group).astype(F4).astype(BF)
+    high, low = halves(context[...])
+    loads[0].wait()
+    attended = slide_rows[...].astype(F4) + dot_nn(high, w_attn[...]) + dot_nn(low, w_attn[...])
     high, low = halves(attended)
     sums = (dot_nn(member, high) + dot_nn(member, low)) / counts[...].astype(F4)
     own = sums[0:4, :]
     for index in range(1, 4):
         own = jnp.where(place[0] == index, sums[4 * index : 4 * index + 4, :], own)
     slide_embed[...] = own
-    high, low = halves(d_embed[...])
+    loads[1].wait()
+    d_slide = d_direct[...] + dot_nt(d_qkv[...], w_qkv[...])
+    loads[2].wait()
+    high, low = halves(dot_nt(d_slide.astype(BF), w_proj[...]))
     pair = pooled_pair[...]
     both = dot_tn(pair, high) + dot_tn(pair, low)
     rows = grad_out.shape[0]
     grad_out[...] = both[:rows, :] + both[128 : 128 + rows, :]
 
 
-def outputs(place, context, slide_rows, w_attn, slide_of, counts, pooled_pair, d_embed, rows):
-    slide_width = w_attn.shape[0]
-    width = d_embed.shape[1]
+def outputs(place, context, slide_rows, slide_of, counts, pooled_pair, d_qkv, d_direct, weights, rows):
+    w_attn, w_qkv, w_proj = weights
+    width, slide_width = w_proj.shape
     return pl.pallas_call(
         outputs_kernel,
-        in_specs=[pl.BlockSpec(memory_space=pltpu.SMEM)] + [pl.BlockSpec(memory_space=pltpu.VMEM)] * 7,
+        in_specs=[SMEM] + [VMEM] * 7 + [ANY] * 3,
         out_shape=[jax.ShapeDtypeStruct((4, slide_width), F4), jax.ShapeDtypeStruct((rows, width), F4)],
-        compiler_params=pltpu.CompilerParams(vmem_limit_bytes=16 * MIB),
+        scratch_shapes=[pltpu.VMEM(weight.shape, BF) for weight in weights] + [pltpu.SemaphoreType.DMA((3,))],
+        compiler_params=pltpu.CompilerParams(vmem_limit_bytes=20 * MIB),
         cost_estimate=pl.CostEstimate(flops=1000, bytes_accessed=1000, transcendentals=0),
         name="outputs",
-    )(place, context, slide_rows, w_attn, slide_of, counts, pooled_pair, d_embed)
+    )(
+        place,
+        context,
+        slide_rows,
+        slide_of,
+        counts,
+        pooled_pair,
+        d_qkv,
+        d_direct,
+        *[from_hbm(weight) for weight in weights],
+    )
 
 
 def grad_kernel(lhs, d_preact, out):
@@ -479,7 +571,7 @@
         out_shape=[jax.ShapeDtypeStruct((rows // 4, columns), BF)] * 4,
         compiler_params=pltpu.CompilerParams(vmem_limit_bytes=8 * MIB),
         name="add_four",
-    )(*parts, after)
+    )(*parts, from_hbm(after))
 
 
 def split_kernel(place, one, two, three, four, keep, send):
@@ -565,11 +657,11 @@
     slide_of = slide_of_tile.reshape(1, -1)
     order_of = order_of_tile.reshape(1, -1)
 
-    slope_send, slope_keep, pooled, shared, token_mean, normed = forward(place, flat, w_in, w_out, slide_cot, tile_count)
+    slope_send, slope_keep, pooled, shared, token_mean, normed = forward(flat, w_in, w_out, slide_cot, tile_count)
     parts = [shared] + [
         lax.ppermute(shared, "slide", [(i, (i + k) % 4) for i in range(4)]) for k in (1, 2, 3)
     ]
-    normed_t = transposed(normed, shared, patches)
+    normed_t = transposed(normed, shared, 2 * patches)
     slices = pooled.reshape(2 * tile_count, peers, hidden // peers).transpose(1, 0, 2)
     slices = jnp.pad(slices.reshape(peers * 2 * tile_count, -1), ((0, 0), (0, 128 - hidden // peers)))
     mine, cot_all, normed_t, slope_send = embed(
@@ -579,7 +671,7 @@
         mine.reshape(peers, 8, -1), "tile", split_axis=0, concat_axis=0, tiled=True
     ).reshape(peers * 8, -1)
     slope_other, normed_other = other_core(slope_send), other_core(normed_t)
-    d_preact, *lhs, d_embed, context, slide_rows, pooled_pair = attention(
+    d_preact, *lhs, d_qkv, d_direct, context, slide_rows, pooled_pair = attention(
         place,
         seg_len,
         gathered,
@@ -595,7 +687,16 @@
         chunks[k] = first_axis(grad_chunk(lhs[k], d_preact), k)
     chunks[0] = grad_chunk(lhs[0], d_preact)
     slide_embed, grad_out = outputs(
-        place, context, slide_rows, w_attn_out, slide_of, counts, pooled_pair, d_embed, hidden // peers
+        place,
+        context,
+        slide_rows,
+        slide_of,
+        counts,
+        pooled_pair,
+        d_qkv,
+        d_direct,
+        (w_attn_out, w_qkv, w_proj),
+        hidden // peers,
     )
     parts = add_four([chunks[k] for k in range(4)], slide_embed)
     parts = [parts[0]] + [second_axis(parts[k], k) for k in (1, 2, 3)]

time: 98.3 us -> 91.1 us (0.927)
  local copies, waits for them, and re-layouts: 4.07 us -> 0.35 us
  waiting for transfers between devices: 16.2 us -> 12.5 us
    ppermute x9, waiting for transfers between devices: 16.2 us -> 12.2 us  [moved(): return lax.ppermute(value, 'tile', pairs)]
    unnamed x18 -> x10, local copies, waits for them, and re-layouts: 3.74 us -> 0.02 us
    pallas_call x3, Pallas kernels: 31 us -> 32.6 us  [the longest x1 14.7 us: forward(): pl.pallas_call(forward_kernel, in_specs=[ANY] * 4, out_specs=[ANY, ANY, V...]
    pallas_call x1, Pallas kernels: 4.77 us -> 3.62 us  [transposed(): pl.pallas_call(transpose_kernel, grid=(tokens // patches,), in_specs=[ANY...]
  transfers between devices with their start and end apart: 12 -> 12, of which waited for: 6 -> 5; matrix products, arithmetic and copies ran while one was open for 0% -> 0% of each run, Pallas kernels for 10% -> 15%
where the time goes in v3:
time: 91.1 us; the launch traced here: 89.9 us
  Pallas kernels  44.6 us (49%)
  blocking collectives  19.1 us (21%)
  starting transfers between devices  12.6 us (14%)
  waiting for transfers between devices  12.5 us (14%)
    all_to_all x1, blocking collectives, on_device(): lax.all_to_all(mine.reshape(peers, 8, -1), 'tile', split_axis=0, concat_a...  19.1 us
    pallas_call x1, Pallas kernels, forward(): pl.pallas_call(forward_kernel, in_specs=[ANY] * 4, out_specs=[ANY, ANY, V...  14.7 us
    ppermute x9, waiting for transfers between devices, moved(): return lax.ppermute(value, 'tile', pairs)  12.2 us
    pallas_call x1, Pallas kernels, attention(): pl.pallas_call(attention_kernel, in_specs=[SMEM, SMEM] + [VMEM] * 2 + [AN...  11.3 us
    ppermute x9, starting transfers between devices, moved(): return lax.ppermute(value, 'tile', pairs)  7.69 us
    pallas_call x1, Pallas kernels, outputs(): pl.pallas_call(outputs_kernel, in_specs=[SMEM] + [VMEM] * 7 + [ANY] * 3,...  6.66 us
    pallas_call x4, Pallas kernels, grad_chunk(): pl.pallas_call(grad_kernel, in_specs=[VMEM] * 2, out_specs=VMEM, out_shap...  5.53 us
    ppermute x3, starting transfers between devices, on_device(): lax.ppermute(shared, 'slide', [(i, (i + k) % 4) for i in range(4)])  4.93 us
  transfers between devices with their start and end apart: 12, of which 5 were waited for; matrix products, arithmetic and copies ran while one was open for 0% of the time, Pallas kernels for 15%

profile of v3, /device:TPU:0, one launch (start us, length us, event | category | flops | bytes accessed | tf_op | source)
XLA Modules:
  0.0 89.9 jit_solution(629323004323131127)
XLA Ops:
  0.6 14.7 %forward.1 = (bf16[1024,768]{1,0:T(8,128)(2,1)}, bf16[1024,768]{1,0:T(8,128)(2,1)}, bf16[8,1536]{1,0:T(8,128)(2,1)S(1)}, f32[4,2304]{1,0:T(4,128)S(1)}, f32[4,15...) custom-call(bf16[1024,1536]{1,0:T(8,128)(2,1)} %bitcast.20, bf16[1536,1536]{1,0:T(8,128)(2,1)} %w_in_hbm.1, ...), custom_call_target="tpu_custom_call" | custom-call | tf_op jit(solution)/shard_map/forward/pallas_call | solution.py:181
  15.3 3.3 %collective-permute-start.2 = (f32[4,2304]{1,0:T(4,128)S(1)}, f32[4,2304]{1,0:T(4,128)S(1)}, u32[]{:S(2)}, u32[]{:S(2)}) collective-permute-start(f32[4,2304]{1,0:T(4,128)S(1)} %get-tuple-element.31.after.own), channel_id=1, source_target_pairs={{0,96},{32,0},{64,32},{96,64},{1,97},{33,1},{65,33},{97,65},{2,98}... | collective-permute-start | bytes 110600 | tf_op jit(solution)/shard_map/ppermute | solution.py:662
  18.7 0.6 collective-permute-start.1
  19.3 1.0 %collective-permute-start = (f32[4,2304]{1,0:T(4,128)S(1)}, f32[4,2304]{1,0:T(4,128)S(1)}, u32[]{:S(2)}, u32[]{:S(2)}) collective-permute-start(f32[4,2304]{1,0:T(4,128)S(1)} %get-tuple-element.31.after.own), channel_id=1, source_target_pairs={{0,32},{32,64},{64,96},{96,0},{1,33},{33,65},{65,97},{97,1},{2,34}... | collective-permute-start | bytes 110600 | tf_op jit(solution)/shard_map/ppermute | solution.py:662
  20.4 0.1 reshape.34
  20.6 0.1 stack.23.place
  20.6 3.6 %transposed.1.normed_in = bf16[1536,1024]{1,0:T(8,128)(2,1)} custom-call(f32[4,2304]{1,0:T(4,128)S(1)} %get-tuple-element.31.after.own, bf16[1024,1536]{1,0:T(8,128)(2,1)} %get-tuple-element.34.normed), custom_call_target="tpu_custom_call" | custom-call | flops 20000000 | bytes 9000000 | tf_op jit(solution)/shard_map/transposed/pallas_call | solution.py:219
  24.3 0.3 collective-permute-done.one
  24.5 0.6 embed.1
  25.2 0.1 collective-permute-start.3
  25.2 0.5 collective-permute-start.4
  25.7 19.1 %all_to_all.5 = bf16[32,8,896]{2,1,0:T(8,128)(2,1)} all-to-all(bf16[32,8,896]{2,1,0:T(8,128)(2,1)S(1)} %bitcast.16), channel_id=1, replica_groups=mesh['slide'=4,'tile'=32] {'tile'}, dimensions={0} | all-to-all | bytes 917504 | tf_op jit(solution)/shard_map/all_to_all | solution.py:670
  44.9 11.3 %attention.1 = (bf16[2048,768]{1,0:T(8,128)(2,1)S(1)}, bf16[384,2048]{1,0:T(8,128)(2,1)S(1)}, bf16[384,2048]{1,0:T(8,128)(2,1)S(1)}, bf16[384,2048]{1,0:T(8,128)...) custom-call(s32[5]{0:T(128)S(1)} %stack.23.place, ...), custom_call_target="tpu_custom_call" | custom-call | tf_op jit(solution)/shard_map/attention/pallas_call | solution.py:434
  56.2 1.4 %grad_chunk.6 = bf16[384,768]{1,0:T(8,128)(2,1)S(1)} custom-call(bf16[384,2048]{1,0:T(8,128)(2,1)S(1)} %get-tuple-element.50.lhs, bf16[2048,768]{1,0:T(8,128)(2,1)S(1)} %get-tuple-element.48.d_preact), custom_call_target="tpu_custom_call" | custom-call | flops 1000 | bytes 1000 | tf_op jit(solution)/shard_map/grad_chunk/pallas_call | solution.py:547
  57.5 1.4 %grad_chunk.7 = bf16[384,768]{1,0:T(8,128)(2,1)S(1)} custom-call(bf16[384,2048]{1,0:T(8,128)(2,1)S(1)} %get-tuple-element.51.lhs, bf16[2048,768]{1,0:T(8,128)(2,1)S(1)} %get-tuple-element.48.d_preact), custom_call_target="tpu_custom_call" | custom-call | flops 1000 | bytes 1000 | tf_op jit(solution)/shard_map/grad_chunk/pallas_call | solution.py:547
  58.9 0.8 collective-permute-start.7
  59.7 1.9 %collective-permute-start.6 = (bf16[384,768]{1,0:T(8,128)(2,1)S(1)}, bf16[384,768]{1,0:T(8,128)(2,1)S(1)}, u32[]{:S(2)}, u32[]{:S(2)}) collective-permute-start(bf16[384,768]{1,0:T(8,128)(2,1)S(1)} %grad_chunk.6), channel_id=1, source_target_pairs={{0,4},{1,17},{2,6},{3,19},{4,0},{5,21},{6,2},{7,23},{8,12},{9,25},... | collective-permute-start | bytes 1769480 | tf_op jit(solution)/shard_map/ppermute | solution.py:621
  61.6 1.4 %grad_chunk.5 = bf16[384,768]{1,0:T(8,128)(2,1)S(1)} custom-call(bf16[384,2048]{1,0:T(8,128)(2,1)S(1)} %get-tuple-element.49.lhs, bf16[2048,768]{1,0:T(8,128)(2,1)S(1)} %get-tuple-element.48.d_preact), custom_call_target="tpu_custom_call" | custom-call | flops 1000 | bytes 1000 | tf_op jit(solution)/shard_map/grad_chunk/pallas_call | solution.py:547
  63.0 0.1 collective-permute-start.5
  63.2 1.4 %grad_chunk.4.one = bf16[384,768]{1,0:T(8,128)(2,1)S(1)} custom-call(bf16[384,2048]{1,0:T(8,128)(2,1)S(1)} %get-tuple-element.47.lhs, bf16[2048,768]{1,0:T(8,128)(2,1)S(1)} %get-tuple-element.48.d_preact), custom_call_target="tpu_custom_call" | custom-call | flops 1000 | bytes 1000 | tf_op jit(solution)/shard_map/grad_chunk/pallas_call | solution.py:547
  64.5 6.7 %outputs.1 = (f32[4,768]{1,0:T(4,128)}, f32[48,1536]{1,0:T(8,128)}) custom-call(s32[5]{0:T(128)S(1)} %stack.23.place, f32[128,768]{1,0:T(8,128)S(1)} %get-tuple-element.41.context, bf16[128,768]{1,0:T(8,128)(2,1)S(1)} %get-tuple-element.42.slide_rows, s32[1,128]{1,0:T(1,128)S(1)} %bitcast.18, s32[16,1]{1,0:T(8,128)S(1)} %copy.17.counts, ...), custom_call_target="tpu_custom_call" | custom-call | flops 1000 | bytes 1000 | tf_op jit(solution)/shard_map/outputs/pallas_call | solution.py:519
  71.2 6.2 %collective-permute-done.5.two = bf16[384,768]{1,0:T(8,128)(2,1)S(1)} collective-permute-done((bf16[384,768]{1,0:T(8,128)(2,1)S(1)}, bf16[384,768]{1,0:T(8,128)(2,1)S(1)}, u32[]{:S(2)}, u32[]{:S(2)}) %collective-permute-start.5) | collective-permute-done | bytes 589856 | tf_op jit(solution)/shard_map/ppermute | solution.py:621
  77.4 0.3 add_four.1
  77.7 0.7 collective-permute-start.8
  78.4 1.9 %collective-permute-start.9 = (bf16[96,768]{1,0:T(8,128)(2,1)S(1)}, bf16[96,768]{1,0:T(8,128)(2,1)S(1)}, u32[]{:S(2)}, u32[]{:S(2)}) collective-permute-start(bf16[96,768]{1,0:T(8,128)(2,1)S(1)} %get-tuple-element.54), channel_id=1, source_target_pairs={{0,16},{1,5},{2,18},{3,7},{4,20},{5,1},{6,22},{7,3},{8,24},{9,13},... | collective-permute-start | bytes 442376 | tf_op jit(solution)/shard_map/ppermute | solution.py:621
  80.4 1.5 %collective-permute-start.10 = (bf16[96,768]{1,0:T(8,128)(2,1)S(1)}, bf16[96,768]{1,0:T(8,128)(2,1)S(1)}, u32[]{:S(2)}, u32[]{:S(2)}) collective-permute-start(bf16[96,768]{1,0:T(8,128)(2,1)S(1)} %get-tuple-element.55), channel_id=1, source_target_pairs={{0,24},{1,7},{2,26},{3,1},{4,28},{5,3},{6,30},{7,5},{8,0},{9,15},{... | collective-permute-start | bytes 442376 | tf_op jit(solution)/shard_map/ppermute | solution.py:621
  81.9 3.8 %collective-permute-done.8.two = bf16[96,768]{1,0:T(8,128)(2,1)S(1)} collective-permute-done((bf16[96,768]{1,0:T(8,128)(2,1)S(1)}, bf16[96,768]{1,0:T(8,128)(2,1)S(1)}, u32[]{:S(2)}, u32[]{:S(2)}) %collective-permute-start.8) | collective-permute-done | bytes 147488 | tf_op jit(solution)/shard_map/ppermute | solution.py:621
  85.7 0.9 collective-permute-done.10.four
  86.6 0.6 split.1
  87.2 0.1 collective-permute-start.11
  87.3 1.4 %collective-permute-done.11.received = f32[48,768]{1,0:T(8,128)S(1)} collective-permute-done((f32[48,768]{1,0:T(8,128)S(1)}, f32[48,768]{1,0:T(8,128)S(1)}, u32[]{:S(2)}, u32[]{:S(2)}) %collective-permute-start.11) | collective-permute-done | bytes 147488 | tf_op jit(solution)/shard_map/ppermute | solution.py:621
  88.6 1.3 %finish.1 = f32[48,1536]{1,0:T(8,128)} custom-call(s32[5]{0:T(128)S(1)} %stack.23.place, f32[48,768]{1,0:T(8,128)S(1)} %get-tuple-element.56.keep, f32[48,768]{1,0:T(8,128)S(1)} %collective-permute-done.11.received), custom_call_target="tpu_custom_call" | custom-call | tf_op jit(solution)/shard_map/finish/pallas_call | solution.py:605
  (20 shorter events, 0.2 us)
Async XLA Ops:
  0.6 19.6 %copy-start.4 = (s32[16]{0:T(128)S(1)}, s32[16]{0:T(128)}, u32[]{:S(2)}) copy-start(s32[16]{0:T(128)} %param.19) | copy-start | bytes 196
  15.3 8.9 %collective-permute-start.2 = (f32[4,2304]{1,0:T(4,128)S(1)}, f32[4,2304]{1,0:T(4,128)S(1)}, u32[]{:S(2)}, u32[]{:S(2)}) collective-permute-start(f32[4,2304]{1,0:T(4,128)S(1)} %get-tuple-element.31.after.own), channel_id=1, source_target_pairs={{0,96},{32,0},{64,32},{96,64},{1,97},{33,1},{65,33},{97,65},{2,98}... | collective-permute-start | bytes 110600 | tf_op jit(solution)/shard_map/ppermute | solution.py:662
  18.7 5.6 %collective-permute-start.1 = (f32[4,2304]{1,0:T(4,128)S(1)}, f32[4,2304]{1,0:T(4,128)S(1)}, u32[]{:S(2)}, u32[]{:S(2)}) collective-permute-start(f32[4,2304]{1,0:T(4,128)S(1)} %get-tuple-element.31.after.own), channel_id=1, source_target_pairs={{0,64},{32,96},{64,0},{96,32},{1,65},{33,97},{65,1},{97,33},{2,66}... | collective-permute-start | bytes 110600 | tf_op jit(solution)/shard_map/ppermute | solution.py:662
  19.3 5.2 %collective-permute-start = (f32[4,2304]{1,0:T(4,128)S(1)}, f32[4,2304]{1,0:T(4,128)S(1)}, u32[]{:S(2)}, u32[]{:S(2)}) collective-permute-start(f32[4,2304]{1,0:T(4,128)S(1)} %get-tuple-element.31.after.own), channel_id=1, source_target_pairs={{0,32},{32,64},{64,96},{96,0},{1,33},{33,65},{65,97},{97,1},{2,34}... | collective-permute-start | bytes 110600 | tf_op jit(solution)/shard_map/ppermute | solution.py:662
  24.5 20.3 %copy-start.1 = (s32[128]{0:T(128)S(1)}, s32[128]{0:T(128)}, u32[]{:S(2)}) copy-start(s32[128]{0:T(128)} %param.17) | copy-start | bytes 1540
  24.5 20.3 %copy-start.2 = (s32[3]{0:T(128)S(1)}, s32[3]{0:T(128)}, u32[]{:S(2)}) copy-start(s32[3]{0:T(128)} %seg_len.1) | copy-start | bytes 40
  24.5 20.3 %copy-start.3 = (s32[128]{0:T(128)S(1)}, s32[128]{0:T(128)}, u32[]{:S(2)}) copy-start(s32[128]{0:T(128)} %param.18) | copy-start | bytes 1540
  25.2 19.7 %copy-start = (f32[16,768]{1,0:T(8,128)}, f32[16,768]{1,0:T(8,128)S(1)}, u32[]{:S(2)}) copy-start(f32[16,768]{1,0:T(8,128)S(1)} %get-tuple-element.37.cot_hbm) | copy-start | bytes 147460
  25.2 19.7 %collective-permute-start.3 = (bf16[1536,1024]{1,0:T(8,128)(2,1)}, bf16[1536,1024]{1,0:T(8,128)(2,1)S(1)}, u32[]{:S(2)}, u32[]{:S(2)}) collective-permute-start(bf16[1536,1024]{1,0:T(8,128)(2,1)} %get-tuple-element.38.normed_own), channel_id=1, source_target_pairs={{0,1},{1,0},{2,3},{3,2},{4,5},{5,4},{6,7},{7,6},{8,9},{9,8},{10,11... | collective-permute-start | bytes 9437192 | tf_op jit(solution)/shard_map/ppermute | solution.py:621
  25.2 19.6 %collective-permute-start.4 = (bf16[1024,768]{1,0:T(8,128)(2,1)}, bf16[1024,768]{1,0:T(8,128)(2,1)S(1)}, u32[]{:S(2)}, u32[]{:S(2)}) collective-permute-start(bf16[1024,768]{1,0:T(8,128)(2,1)} %get-tuple-element.40), channel_id=1, source_target_pairs={{0,1},{1,0},{2,3},{3,2},{4,5},{5,4},{6,7},{7,6},{8,9},{9,8},{10,11... | collective-permute-start | bytes 4718600 | tf_op jit(solution)/shard_map/ppermute | solution.py:621
  58.9 12.3 %collective-permute-start.7 = (bf16[384,768]{1,0:T(8,128)(2,1)S(1)}, bf16[384,768]{1,0:T(8,128)(2,1)S(1)}, u32[]{:S(2)}, u32[]{:S(2)}) collective-permute-start(bf16[384,768]{1,0:T(8,128)(2,1)S(1)} %grad_chunk.7), channel_id=1, source_target_pairs={{0,6},{1,25},{2,0},{3,27},{4,2},{5,29},{6,4},{7,31},{8,14},{9,1},{... | collective-permute-start | bytes 1769480 | tf_op jit(solution)/shard_map/ppermute | solution.py:621
  59.7 11.5 %collective-permute-start.6 = (bf16[384,768]{1,0:T(8,128)(2,1)S(1)}, bf16[384,768]{1,0:T(8,128)(2,1)S(1)}, u32[]{:S(2)}, u32[]{:S(2)}) collective-permute-start(bf16[384,768]{1,0:T(8,128)(2,1)S(1)} %grad_chunk.6), channel_id=1, source_target_pairs={{0,4},{1,17},{2,6},{3,19},{4,0},{5,21},{6,2},{7,23},{8,12},{9,25},... | collective-permute-start | bytes 1769480 | tf_op jit(solution)/shard_map/ppermute | solution.py:621
  63.0 14.4 %collective-permute-start.5 = (bf16[384,768]{1,0:T(8,128)(2,1)S(1)}, bf16[384,768]{1,0:T(8,128)(2,1)S(1)}, u32[]{:S(2)}, u32[]{:S(2)}) collective-permute-start(bf16[384,768]{1,0:T(8,128)(2,1)S(1)} %grad_chunk.5), channel_id=1, source_target_pairs={{0,2},{1,9},{2,4},{3,11},{4,6},{5,13},{6,0},{7,15},{8,10},{9,17},{... | collective-permute-start | bytes 1769480 | tf_op jit(solution)/shard_map/ppermute | solution.py:621
  77.7 8.0 %collective-permute-start.8 = (bf16[96,768]{1,0:T(8,128)(2,1)S(1)}, bf16[96,768]{1,0:T(8,128)(2,1)S(1)}, u32[]{:S(2)}, u32[]{:S(2)}) collective-permute-start(bf16[96,768]{1,0:T(8,128)(2,1)S(1)} %get-tuple-element.53), channel_id=1, source_target_pairs={{0,8},{1,3},{2,10},{3,5},{4,12},{5,7},{6,14},{7,1},{8,16},{9,11},{... | collective-permute-start | bytes 442376 | tf_op jit(solution)/shard_map/ppermute | solution.py:621
  78.4 7.3 %collective-permute-start.9 = (bf16[96,768]{1,0:T(8,128)(2,1)S(1)}, bf16[96,768]{1,0:T(8,128)(2,1)S(1)}, u32[]{:S(2)}, u32[]{:S(2)}) collective-permute-start(bf16[96,768]{1,0:T(8,128)(2,1)S(1)} %get-tuple-element.54), channel_id=1, source_target_pairs={{0,16},{1,5},{2,18},{3,7},{4,20},{5,1},{6,22},{7,3},{8,24},{9,13},... | collective-permute-start | bytes 442376 | tf_op jit(solution)/shard_map/ppermute | solution.py:621
  80.4 6.2 %collective-permute-start.10 = (bf16[96,768]{1,0:T(8,128)(2,1)S(1)}, bf16[96,768]{1,0:T(8,128)(2,1)S(1)}, u32[]{:S(2)}, u32[]{:S(2)}) collective-permute-start(bf16[96,768]{1,0:T(8,128)(2,1)S(1)} %get-tuple-element.55), channel_id=1, source_target_pairs={{0,24},{1,7},{2,26},{3,1},{4,28},{5,3},{6,30},{7,5},{8,0},{9,15},{... | collective-permute-start | bytes 442376 | tf_op jit(solution)/shard_map/ppermute | solution.py:621
  87.2 1.5 %collective-permute-start.11 = (f32[48,768]{1,0:T(8,128)S(1)}, f32[48,768]{1,0:T(8,128)S(1)}, u32[]{:S(2)}, u32[]{:S(2)}) collective-permute-start(f32[48,768]{1,0:T(8,128)S(1)} %get-tuple-element.57), channel_id=1, source_target_pairs={{0,1},{1,0},{2,3},{3,2},{4,5},{5,4},{6,7},{7,6},{8,9},{9,8},{10,11... | collective-permute-start | bytes 442376 | tf_op jit(solution)/shard_map/ppermute | solution.py:621

commit v4 on v3

--- a/solution.py
+++ b/solution.py
@@ -40,7 +40,7 @@
 
 
 def gelu_pair(a):
-    bell = jnp.exp(a * a * -0.5)
+    bell = jnp.exp2(a * a * (-0.5 * 1.4426950408889634))
     t = 1.0 / (1.0 + jnp.abs(a) * (0.3275911 * 0.7071067811865476))
     series = t * (0.127414796 + t * (-0.142248368 + t * (0.7107068705 + t * (-0.7265760135 + t * 0.5307027145))))
     tail = series * bell
@@ -468,34 +468,11 @@
     )
 
 
-def outputs_kernel(
-    place,
-    context,
-    slide_rows,
-    slide_of,
-    counts,
-    pooled_pair,
-    d_qkv,
-    d_direct,
-    w_attn_hbm,
-    w_qkv_hbm,
-    w_proj_hbm,
-    slide_embed,
-    grad_out,
-    w_attn,
-    w_qkv,
-    w_proj,
-    sems,
-):
-    pairs = [(w_attn_hbm, w_attn), (w_qkv_hbm, w_qkv), (w_proj_hbm, w_proj)]
-    loads = [pltpu.make_async_copy(src, dst, sems.at[i]) for i, (src, dst) in enumerate(pairs)]
-    for load in loads:
-        load.start()
+def embed_out_kernel(place, context, slide_rows, slide_of, counts, w_attn, slide_embed):
     tiles = slide_of.shape[1]
     group = lax.broadcasted_iota(jnp.int32, (16, tiles), 0)
     member = (slide_of[...] == group).astype(F4).astype(BF)
     high, low = halves(context[...])
-    loads[0].wait()
     attended = slide_rows[...].astype(F4) + dot_nn(high, w_attn[...]) + dot_nn(low, w_attn[...])
     high, low = halves(attended)
     sums = (dot_nn(member, high) + dot_nn(member, low)) / counts[...].astype(F4)
@@ -503,9 +480,27 @@
     for index in range(1, 4):
         own = jnp.where(place[0] == index, sums[4 * index : 4 * index + 4, :], own)
     slide_embed[...] = own
+
+
+def embed_out(place, context, slide_rows, slide_of, counts, w_attn):
+    return pl.pallas_call(
+        embed_out_kernel,
+        in_specs=[SMEM] + [VMEM] * 5,
+        out_shape=jax.ShapeDtypeStruct((4, w_attn.shape[0]), F4),
+        compiler_params=pltpu.CompilerParams(vmem_limit_bytes=12 * MIB),
+        cost_estimate=pl.CostEstimate(flops=1000, bytes_accessed=1000, transcendentals=0),
+        name="embed_out",
+    )(place, context, slide_rows, slide_of, counts, w_attn)
+
+
+def grad_out_kernel(pooled_pair, d_qkv, d_direct, w_qkv_hbm, w_proj_hbm, grad_out, w_qkv, w_proj, sems):
+    pairs = [(w_qkv_hbm, w_qkv), (w_proj_hbm, w_proj)]
+    loads = [pltpu.make_async_copy(src, dst, sems.at[i]) for i, (src, dst) in enumerate(pairs)]
+    for load in loads:
+        load.start()
+    loads[0].wait()
+    d_slide = d_direct[...] + dot_nt(d_qkv[...], w_qkv[...])
     loads[1].wait()
-    d_slide = d_direct[...] + dot_nt(d_qkv[...], w_qkv[...])
-    loads[2].wait()
     high, low = halves(dot_nt(d_slide.astype(BF), w_proj[...]))
     pair = pooled_pair[...]
     both = dot_tn(pair, high) + dot_tn(pair, low)
@@ -513,68 +508,75 @@
     grad_out[...] = both[:rows, :] + both[128 : 128 + rows, :]
 
 
-def outputs(place, context, slide_rows, slide_of, counts, pooled_pair, d_qkv, d_direct, weights, rows):
-    w_attn, w_qkv, w_proj = weights
-    width, slide_width = w_proj.shape
-    return pl.pallas_call(
-        outputs_kernel,
-        in_specs=[SMEM] + [VMEM] * 7 + [ANY] * 3,
-        out_shape=[jax.ShapeDtypeStruct((4, slide_width), F4), jax.ShapeDtypeStruct((rows, width), F4)],
-        scratch_shapes=[pltpu.VMEM(weight.shape, BF) for weight in weights] + [pltpu.SemaphoreType.DMA((3,))],
+def grad_out_of(pooled_pair, d_qkv, d_direct, weights, rows):
+    return pl.pallas_call(
+        grad_out_kernel,
+        in_specs=[VMEM] * 3 + [ANY] * 2,
+        out_shape=jax.ShapeDtypeStruct((rows, weights[1].shape[0]), F4),
+        scratch_shapes=[pltpu.VMEM(weight.shape, BF) for weight in weights] + [pltpu.SemaphoreType.DMA((2,))],
         compiler_params=pltpu.CompilerParams(vmem_limit_bytes=20 * MIB),
         cost_estimate=pl.CostEstimate(flops=1000, bytes_accessed=1000, transcendentals=0),
-        name="outputs",
-    )(
-        place,
-        context,
-        slide_rows,
-        slide_of,
-        counts,
-        pooled_pair,
-        d_qkv,
-        d_direct,
-        *[from_hbm(weight) for weight in weights],
-    )
-
-
-def grad_kernel(lhs, d_preact, out):
-    out[...] = dot_nn(lhs[...], d_preact[...]).astype(BF)
-
-
-def grad_chunk(lhs, d_preact):
-    rows, tokens = lhs.shape
+        name="grad_out",
+    )(pooled_pair, d_qkv, d_direct, *[from_hbm(weight) for weight in weights])
+
+
+def grad_kernel(lhs, d_preact, *outs):
+    rows = outs[0].shape[0]
+    for index, out in enumerate(outs):
+        out[...] = dot_nn(lhs[index * rows : (index + 1) * rows, :], d_preact[...]).astype(BF)
+
+
+def grad_chunk(lhs, d_preact, parts=1):
+    rows = lhs.shape[0]
     hidden = d_preact.shape[1]
     return pl.pallas_call(
         grad_kernel,
         in_specs=[VMEM] * 2,
-        out_specs=VMEM,
-        out_shape=jax.ShapeDtypeStruct((rows, hidden), BF),
+        out_specs=[VMEM] * parts,
+        out_shape=[jax.ShapeDtypeStruct((rows // parts, hidden), BF)] * parts,
         compiler_params=pltpu.CompilerParams(vmem_limit_bytes=16 * MIB),
         cost_estimate=pl.CostEstimate(flops=1000, bytes_accessed=1000, transcendentals=0),
         name="grad_chunk",
     )(from_vmem(lhs), from_vmem(d_preact))
 
 
-def add_four_kernel(one, two, three, four, after, *outs):
+def relay_kernel(up, down, up_received, down_received, after, up_out, down_out):
+    half = up_received.shape[0]
+    up_out[:half, :] = (up[:half, :].astype(F4) + up_received[...].astype(F4)).astype(BF)
+    up_out[half:, :] = up[half:, :]
+    down_out[:half, :] = down[:half, :]
+    down_out[half:, :] = (down[half:, :].astype(F4) + down_received[...].astype(F4)).astype(BF)
+
+
+def relay(up, down, up_received, down_received, after):
+    return pl.pallas_call(
+        relay_kernel,
+        in_specs=[VMEM] * 4 + [ANY],
+        out_shape=[jax.ShapeDtypeStruct(up.shape, BF)] * 2,
+        compiler_params=pltpu.CompilerParams(vmem_limit_bytes=8 * MIB),
+        name="relay",
+    )(up, down, up_received, down_received, after)
+
+
+def add_three_kernel(one, two, three, after, *outs):
     rows = outs[0].shape[0]
     for index, out in enumerate(outs):
         at = pl.ds(index * rows, rows)
-        total = (one[at, :].astype(F4) + two[at, :].astype(F4)) + (three[at, :].astype(F4) + four[at, :].astype(F4))
-        out[...] = total.astype(BF)
-
-
-def add_four(parts, after):
+        out[...] = (one[at, :].astype(F4) + two[at, :].astype(F4) + three[at, :].astype(F4)).astype(BF)
+
+
+def add_three(parts, after):
     rows, columns = parts[0].shape
     return pl.pallas_call(
-        add_four_kernel,
-        in_specs=[VMEM] * 4 + [ANY],
+        add_three_kernel,
+        in_specs=[VMEM] * 3 + [ANY],
         out_shape=[jax.ShapeDtypeStruct((rows // 4, columns), BF)] * 4,
         compiler_params=pltpu.CompilerParams(vmem_limit_bytes=8 * MIB),
-        name="add_four",
+        name="add_three",
     )(*parts, from_hbm(after))
 
 
-def split_kernel(place, one, two, three, four, keep, send):
+def split_kernel(place, one, two, three, four, after, keep, send):
     total = (one[...].astype(F4) + two[...].astype(F4)) + (three[...].astype(F4) + four[...].astype(F4))
     rows = keep.shape[0]
     top, bottom = total[:rows, :], total[rows:, :]
@@ -582,15 +584,15 @@
     send[...] = jnp.where(place[2] == 0, bottom, top)
 
 
-def split(place, parts):
+def split(place, parts, after):
     rows, columns = parts[0].shape
     return pl.pallas_call(
         split_kernel,
-        in_specs=[SMEM] + [VMEM] * 4,
+        in_specs=[SMEM] + [VMEM] * 4 + [ANY],
         out_shape=[jax.ShapeDtypeStruct((rows // 2, columns), F4)] * 2,
         compiler_params=pltpu.CompilerParams(vmem_limit_bytes=8 * MIB),
         name="split",
-    )(place, *parts)
+    )(place, *parts, from_hbm(after))
 
 
 def finish_kernel(place, keep, received, out):
@@ -682,25 +684,17 @@
         (normed_t, normed_other),
         (slope_keep, slope_other),
     )
-    chunks = {}
-    for k in (2, 1, 3):
-        chunks[k] = first_axis(grad_chunk(lhs[k], d_preact), k)
-    chunks[0] = grad_chunk(lhs[0], d_preact)
-    slide_embed, grad_out = outputs(
-        place,
-        context,
-        slide_rows,
-        slide_of,
-        counts,
-        pooled_pair,
-        d_qkv,
-        d_direct,
-        (w_attn_out, w_qkv, w_proj),
-        hidden // peers,
-    )
-    parts = add_four([chunks[k] for k in range(4)], slide_embed)
+    upper, lower = grad_chunk(lhs[2], d_preact, 2)
+    up_received, down_received = first_axis(upper, 1), first_axis(lower, 3)
+    up, down = grad_chunk(lhs[1], d_preact)[0], grad_chunk(lhs[3], d_preact)[0]
+    own = grad_chunk(lhs[0], d_preact)[0]
+    up, down = relay(up, down, up_received, down_received, own)
+    parts = [own, first_axis(up, 1), first_axis(down, 3)]
+    grad_out = grad_out_of(pooled_pair, d_qkv, d_direct, (w_qkv, w_proj), hidden // peers)
+    slide_embed = embed_out(place, context, slide_rows, slide_of, counts, w_attn_out)
+    parts = add_three(parts, grad_out)
     parts = [parts[0]] + [second_axis(parts[k], k) for k in (1, 2, 3)]
-    keep, send = split(place, parts)
+    keep, send = split(place, parts, slide_embed)
     return (slide_embed, finish(place, keep, other_core(send)), grad_out)
 
 

time: 91.1 us -> 90.5 us (level)
  waiting for transfers between devices: 12.5 us -> 7.56 us
  starting transfers between devices: 12.6 us -> 15.9 us
  Pallas kernels: 44.6 us -> 45.6 us
    ppermute x9 -> x10, waiting for transfers between devices: 12.2 us -> 7.29 us  [moved(): return lax.ppermute(value, 'tile', pairs)]
    ppermute x9 -> x10, starting transfers between devices: 7.69 us -> 10.9 us  [moved(): return lax.ppermute(value, 'tile', pairs)]
    pallas_call x7 -> x9, Pallas kernels: 13.1 us -> 14.2 us  [the longest x1 5.82 us: grad_out_of(): pl.pallas_call(grad_out_kernel, in_specs=[VMEM] * 3 + [ANY] * 2, out_shap...]
  transfers between devices with their start and end apart: 12 -> 13, of which waited for: 5 -> 6; matrix products, arithmetic and copies ran while one was open for 0% -> 0% of each run, Pallas kernels for 15% -> 17%
where the time goes in v4:
time: 90.5 us; the launch traced here: 89.3 us
  Pallas kernels  45.6 us (50%)
  blocking collectives  19.1 us (21%)
  starting transfers between devices  15.9 us (18%)
  waiting for transfers between devices  7.56 us (8%)
    all_to_all x1, blocking collectives, on_device(): lax.all_to_all(mine.reshape(peers, 8, -1), 'tile', split_axis=0, concat_a...  19.1 us
    pallas_call x1, Pallas kernels, forward(): pl.pallas_call(forward_kernel, in_specs=[ANY] * 4, out_specs=[ANY, ANY, V...  14.6 us
    pallas_call x1, Pallas kernels, attention(): pl.pallas_call(attention_kernel, in_specs=[SMEM, SMEM] + [VMEM] * 2 + [AN...  11.3 us
    ppermute x10, starting transfers between devices, moved(): return lax.ppermute(value, 'tile', pairs)  10.9 us
    ppermute x10, waiting for transfers between devices, moved(): return lax.ppermute(value, 'tile', pairs)  7.29 us
    pallas_call x1, Pallas kernels, grad_out_of(): pl.pallas_call(grad_out_kernel, in_specs=[VMEM] * 3 + [ANY] * 2, out_shap...  5.82 us
    pallas_call x4, Pallas kernels, grad_chunk(): pl.pallas_call(grad_kernel, in_specs=[VMEM] * 2, out_specs=[VMEM] * parts...  5.53 us
    ppermute x3, starting transfers between devices, on_device(): lax.ppermute(shared, 'slide', [(i, (i + k) % 4) for i in range(4)])  4.92 us
  transfers between devices with their start and end apart: 13, of which 6 were waited for; matrix products, arithmetic and copies ran while one was open for 0% of the time, Pallas kernels for 17%

profile of v4, /device:TPU:0, one launch (start us, length us, event | category | flops | bytes accessed | tf_op | source)
XLA Modules:
  0.0 89.3 jit_solution(16550671566195823438)
XLA Ops:
  0.6 14.6 %forward.1 = (bf16[1024,768]{1,0:T(8,128)(2,1)}, bf16[1024,768]{1,0:T(8,128)(2,1)}, bf16[8,1536]{1,0:T(8,128)(2,1)S(1)}, f32[4,2304]{1,0:T(4,128)S(1)}, f32[4,15...) custom-call(bf16[1024,1536]{1,0:T(8,128)(2,1)} %bitcast.20, bf16[1536,1536]{1,0:T(8,128)(2,1)} %w_in_hbm.1, ...), custom_call_target="tpu_custom_call" | custom-call | tf_op jit(solution)/shard_map/forward/pallas_call | solution.py:181
  15.2 3.3 %collective-permute-start.2 = (f32[4,2304]{1,0:T(4,128)S(1)}, f32[4,2304]{1,0:T(4,128)S(1)}, u32[]{:S(2)}, u32[]{:S(2)}) collective-permute-start(f32[4,2304]{1,0:T(4,128)S(1)} %get-tuple-element.33.after.own), channel_id=1, source_target_pairs={{0,96},{32,0},{64,32},{96,64},{1,97},{33,1},{65,33},{97,65},{2,98}... | collective-permute-start | bytes 110600 | tf_op jit(solution)/shard_map/ppermute | solution.py:664
  18.5 0.6 collective-permute-start.1
  19.2 1.0 %collective-permute-start = (f32[4,2304]{1,0:T(4,128)S(1)}, f32[4,2304]{1,0:T(4,128)S(1)}, u32[]{:S(2)}, u32[]{:S(2)}) collective-permute-start(f32[4,2304]{1,0:T(4,128)S(1)} %get-tuple-element.33.after.own), channel_id=1, source_target_pairs={{0,32},{32,64},{64,96},{96,0},{1,33},{33,65},{65,97},{97,1},{2,34}... | collective-permute-start | bytes 110600 | tf_op jit(solution)/shard_map/ppermute | solution.py:664
  20.2 0.1 reshape.34
  20.4 0.1 stack.23.place
  20.5 3.6 %transposed.1.normed_in = bf16[1536,1024]{1,0:T(8,128)(2,1)} custom-call(f32[4,2304]{1,0:T(4,128)S(1)} %get-tuple-element.33.after.own, bf16[1024,1536]{1,0:T(8,128)(2,1)} %get-tuple-element.36.normed), custom_call_target="tpu_custom_call" | custom-call | flops 20000000 | bytes 9000000 | tf_op jit(solution)/shard_map/transposed/pallas_call | solution.py:219
  24.1 0.3 collective-permute-done.one
  24.4 0.6 embed.1
  25.1 0.5 collective-permute-start.4
  25.6 19.1 %all_to_all.5 = bf16[32,8,896]{2,1,0:T(8,128)(2,1)} all-to-all(bf16[32,8,896]{2,1,0:T(8,128)(2,1)S(1)} %bitcast.16), channel_id=1, replica_groups=mesh['slide'=4,'tile'=32] {'tile'}, dimensions={0} | all-to-all | bytes 917504 | tf_op jit(solution)/shard_map/all_to_all | solution.py:672
  44.8 11.3 %attention.1 = (bf16[2048,768]{1,0:T(8,128)(2,1)S(1)}, bf16[384,2048]{1,0:T(8,128)(2,1)S(1)}, bf16[384,2048]{1,0:T(8,128)(2,1)S(1)}, bf16[384,2048]{1,0:T(8,128)...) custom-call(s32[5]{0:T(128)S(1)} %stack.23.place, ...), custom_call_target="tpu_custom_call" | custom-call | tf_op jit(solution)/shard_map/attention/pallas_call | solution.py:434
  56.0 1.4 %grad_chunk.7 = (bf16[192,768]{1,0:T(8,128)(2,1)S(1)}, bf16[192,768]{1,0:T(8,128)(2,1)S(1)}) custom-call(bf16[384,2048]{1,0:T(8,128)(2,1)S(1)} %get-tuple-element.49.lhs, bf16[2048,768]{1,0:T(8,128)(2,1)S(1)} %get-tuple-element.46.d_preact), custom_call_target="tpu_custom_call" | custom-call | flops 1000 | bytes 1000 | tf_op jit(solution)/shard_map/grad_chunk/pallas_call | solution.py:532
  57.4 0.6 collective-permute-start.5
  58.1 2.7 %collective-permute-start.6 = (bf16[192,768]{1,0:T(8,128)(2,1)S(1)}, bf16[192,768]{1,0:T(8,128)(2,1)S(1)}, u32[]{:S(2)}, u32[]{:S(2)}) collective-permute-start(bf16[192,768]{1,0:T(8,128)(2,1)S(1)} %get-tuple-element.51), channel_id=1, source_target_pairs={{0,6},{1,25},{2,0},{3,27},{4,2},{5,29},{6,4},{7,31},{8,14},{9,1},{... | collective-permute-start | bytes 884744 | tf_op jit(solution)/shard_map/ppermute | solution.py:623
  60.7 1.4 %grad_chunk.4.after.one = bf16[384,768]{1,0:T(8,128)(2,1)S(1)} custom-call(bf16[384,2048]{1,0:T(8,128)(2,1)S(1)} %get-tuple-element.45.lhs, bf16[2048,768]{1,0:T(8,128)(2,1)S(1)} %get-tuple-element.46.d_preact), custom_call_target="tpu_custom_call" | custom-call | flops 1000 | bytes 1000 | tf_op jit(solution)/shard_map/grad_chunk/pallas_call | solution.py:532
  62.1 1.4 %grad_chunk.5.up = bf16[384,768]{1,0:T(8,128)(2,1)S(1)} custom-call(bf16[384,2048]{1,0:T(8,128)(2,1)S(1)} %get-tuple-element.47.lhs, bf16[2048,768]{1,0:T(8,128)(2,1)S(1)} %get-tuple-element.46.d_preact), custom_call_target="tpu_custom_call" | custom-call | flops 1000 | bytes 1000 | tf_op jit(solution)/shard_map/grad_chunk/pallas_call | solution.py:532
  63.5 1.4 %grad_chunk.6.down = bf16[384,768]{1,0:T(8,128)(2,1)S(1)} custom-call(bf16[384,2048]{1,0:T(8,128)(2,1)S(1)} %get-tuple-element.48.lhs, bf16[2048,768]{1,0:T(8,128)(2,1)S(1)} %get-tuple-element.46.d_preact), custom_call_target="tpu_custom_call" | custom-call | flops 1000 | bytes 1000 | tf_op jit(solution)/shard_map/grad_chunk/pallas_call | solution.py:532
  64.9 0.5 collective-permute-done.5.up_received
  65.4 0.2 relay.1
  65.7 3.3 %collective-permute-start.8 = (bf16[384,768]{1,0:T(8,128)(2,1)S(1)}, bf16[384,768]{1,0:T(8,128)(2,1)S(1)}, u32[]{:S(2)}, u32[]{:S(2)}) collective-permute-start(bf16[384,768]{1,0:T(8,128)(2,1)S(1)} %get-tuple-element.53), channel_id=1, source_target_pairs={{0,6},{1,25},{2,0},{3,27},{4,2},{5,29},{6,4},{7,31},{8,14},{9,1},{... | collective-permute-start | bytes 1769480 | tf_op jit(solution)/shard_map/ppermute | solution.py:623
  69.0 5.8 %grad_out.1.after = f32[48,1536]{1,0:T(8,128)} custom-call(bf16[128,256]{1,0:T(8,128)(2,1)S(1)} %get-tuple-element.54.pooled_pair, bf16[128,2304]{1,0:T(8,128)(2,1)S(1)} %get-tuple-element.55.d_qkv, f32[128,768]{1,0:T(8,128)S(1)} %get-tuple-element.56.d_direct, bf16[768,2304]{1,0:T(8,128)(2,1)} %w_qkv_hbm.3, bf16[1536,768]{1,0:T(8,128)(2,1)} %w_proj_hbm.3), custom_call_target="tpu_custom_call" | custom-call | flops 1000 | bytes 1000 | tf_op jit(solution)/shard_map/grad_out/pallas_call | solution.py:512
  74.8 1.9 %collective-permute-done.7.two = bf16[384,768]{1,0:T(8,128)(2,1)S(1)} collective-permute-done((bf16[384,768]{1,0:T(8,128)(2,1)S(1)}, bf16[384,768]{1,0:T(8,128)(2,1)S(1)}, u32[]{:S(2)}, u32[]{:S(2)}) %collective-permute-start.7) | collective-permute-done | bytes 589856 | tf_op jit(solution)/shard_map/ppermute | solution.py:623
  76.8 0.2 add_three.1
  77.1 2.2 %collective-permute-start.10 = (bf16[96,768]{1,0:T(8,128)(2,1)S(1)}, bf16[96,768]{1,0:T(8,128)(2,1)S(1)}, u32[]{:S(2)}, u32[]{:S(2)}) collective-permute-start(bf16[96,768]{1,0:T(8,128)(2,1)S(1)} %get-tuple-element.59), channel_id=1, source_target_pairs={{0,16},{1,5},{2,18},{3,7},{4,20},{5,1},{6,22},{7,3},{8,24},{9,13},... | collective-permute-start | bytes 442376 | tf_op jit(solution)/shard_map/ppermute | solution.py:623
  79.3 1.3 %collective-permute-start.11 = (bf16[96,768]{1,0:T(8,128)(2,1)S(1)}, bf16[96,768]{1,0:T(8,128)(2,1)S(1)}, u32[]{:S(2)}, u32[]{:S(2)}) collective-permute-start(bf16[96,768]{1,0:T(8,128)(2,1)S(1)} %get-tuple-element.60), channel_id=1, source_target_pairs={{0,24},{1,7},{2,26},{3,1},{4,28},{5,3},{6,30},{7,5},{8,0},{9,15},{... | collective-permute-start | bytes 442376 | tf_op jit(solution)/shard_map/ppermute | solution.py:623
  80.6 1.9 %embed_out.1.after = f32[4,768]{1,0:T(4,128)} custom-call(s32[5]{0:T(128)S(1)} %stack.23.place, f32[128,768]{1,0:T(8,128)S(1)} %get-tuple-element.43.context, bf16[128,768]{1,0:T(8,128)(2,1)S(1)} %get-tuple-element.44.slide_rows, s32[1,128]{1,0:T(1,128)S(1)} %bitcast.18, s32[16,1]{1,0:T(8,128)S(1)} %copy.17.counts, bf16[768,768]{1,0:T(8,128)(2,1)S(1)} %copy-done), custom_call_target="tpu_custom_call" | custom-call | flops 1000 | bytes 1000 | tf_op jit(solution)/shard_map/embed_out/pallas_call | solution.py:486
  82.4 2.6 %collective-permute-done.9.two = bf16[96,768]{1,0:T(8,128)(2,1)S(1)} collective-permute-done((bf16[96,768]{1,0:T(8,128)(2,1)S(1)}, bf16[96,768]{1,0:T(8,128)(2,1)S(1)}, u32[]{:S(2)}, u32[]{:S(2)}) %collective-permute-start.9) | collective-permute-done | bytes 147488 | tf_op jit(solution)/shard_map/ppermute | solution.py:623
  85.0 0.9 %collective-permute-done.11.four = bf16[96,768]{1,0:T(8,128)(2,1)S(1)} collective-permute-done((bf16[96,768]{1,0:T(8,128)(2,1)S(1)}, bf16[96,768]{1,0:T(8,128)(2,1)S(1)}, u32[]{:S(2)}, u32[]{:S(2)}) %collective-permute-start.11) | collective-permute-done | bytes 147488 | tf_op jit(solution)/shard_map/ppermute | solution.py:623
  85.9 0.6 split.1
  86.6 1.4 %collective-permute-done.12.received = f32[48,768]{1,0:T(8,128)S(1)} collective-permute-done((f32[48,768]{1,0:T(8,128)S(1)}, f32[48,768]{1,0:T(8,128)S(1)}, u32[]{:S(2)}, u32[]{:S(2)}) %collective-permute-start.12) | collective-permute-done | bytes 147488 | tf_op jit(solution)/shard_map/ppermute | solution.py:623
  88.0 1.3 %finish.1 = f32[48,1536]{1,0:T(8,128)} custom-call(s32[5]{0:T(128)S(1)} %stack.23.place, f32[48,768]{1,0:T(8,128)S(1)} %get-tuple-element.61.keep, f32[48,768]{1,0:T(8,128)S(1)} %collective-permute-done.12.received), custom_call_target="tpu_custom_call" | custom-call | tf_op jit(solution)/shard_map/finish/pallas_call | solution.py:607
  (26 shorter events, 0.5 us)
Async XLA Ops:
  0.6 19.5 %copy-start.5 = (s32[16]{0:T(128)S(1)}, s32[16]{0:T(128)}, u32[]{:S(2)}) copy-start(s32[16]{0:T(128)} %param.19) | copy-start | bytes 196
  15.2 8.9 %collective-permute-start.2 = (f32[4,2304]{1,0:T(4,128)S(1)}, f32[4,2304]{1,0:T(4,128)S(1)}, u32[]{:S(2)}, u32[]{:S(2)}) collective-permute-start(f32[4,2304]{1,0:T(4,128)S(1)} %get-tuple-element.33.after.own), channel_id=1, source_target_pairs={{0,96},{32,0},{64,32},{96,64},{1,97},{33,1},{65,33},{97,65},{2,98}... | collective-permute-start | bytes 110600 | tf_op jit(solution)/shard_map/ppermute | solution.py:664
  18.5 5.6 %collective-permute-start.1 = (f32[4,2304]{1,0:T(4,128)S(1)}, f32[4,2304]{1,0:T(4,128)S(1)}, u32[]{:S(2)}, u32[]{:S(2)}) collective-permute-start(f32[4,2304]{1,0:T(4,128)S(1)} %get-tuple-element.33.after.own), channel_id=1, source_target_pairs={{0,64},{32,96},{64,0},{96,32},{1,65},{33,97},{65,1},{97,33},{2,66}... | collective-permute-start | bytes 110600 | tf_op jit(solution)/shard_map/ppermute | solution.py:664
  19.2 5.2 %collective-permute-start = (f32[4,2304]{1,0:T(4,128)S(1)}, f32[4,2304]{1,0:T(4,128)S(1)}, u32[]{:S(2)}, u32[]{:S(2)}) collective-permute-start(f32[4,2304]{1,0:T(4,128)S(1)} %get-tuple-element.33.after.own), channel_id=1, source_target_pairs={{0,32},{32,64},{64,96},{96,0},{1,33},{33,65},{65,97},{97,1},{2,34}... | collective-permute-start | bytes 110600 | tf_op jit(solution)/shard_map/ppermute | solution.py:664
  24.4 20.3 %copy-start.2 = (s32[128]{0:T(128)S(1)}, s32[128]{0:T(128)}, u32[]{:S(2)}) copy-start(s32[128]{0:T(128)} %param.17) | copy-start | bytes 1540
  24.4 20.3 %copy-start.3 = (s32[3]{0:T(128)S(1)}, s32[3]{0:T(128)}, u32[]{:S(2)}) copy-start(s32[3]{0:T(128)} %seg_len.1) | copy-start | bytes 40
  24.4 20.3 %copy-start.4 = (s32[128]{0:T(128)S(1)}, s32[128]{0:T(128)}, u32[]{:S(2)}) copy-start(s32[128]{0:T(128)} %param.18) | copy-start | bytes 1540
  25.0 19.7 %copy-start.1 = (f32[16,768]{1,0:T(8,128)}, f32[16,768]{1,0:T(8,128)S(1)}, u32[]{:S(2)}) copy-start(f32[16,768]{1,0:T(8,128)S(1)} %get-tuple-element.39.cot_hbm) | copy-start | bytes 147460
  25.0 19.7 %collective-permute-start.3 = (bf16[1536,1024]{1,0:T(8,128)(2,1)}, bf16[1536,1024]{1,0:T(8,128)(2,1)S(1)}, u32[]{:S(2)}, u32[]{:S(2)}) collective-permute-start(bf16[1536,1024]{1,0:T(8,128)(2,1)} %get-tuple-element.40.normed_own), channel_id=1, source_target_pairs={{0,1},{1,0},{2,3},{3,2},{4,5},{5,4},{6,7},{7,6},{8,9},{9,8},{10,11... | collective-permute-start | bytes 9437192 | tf_op jit(solution)/shard_map/ppermute | solution.py:623
  25.1 19.6 %collective-permute-start.4 = (bf16[1024,768]{1,0:T(8,128)(2,1)}, bf16[1024,768]{1,0:T(8,128)(2,1)S(1)}, u32[]{:S(2)}, u32[]{:S(2)}) collective-permute-start(bf16[1024,768]{1,0:T(8,128)(2,1)} %get-tuple-element.42), channel_id=1, source_target_pairs={{0,1},{1,0},{2,3},{3,2},{4,5},{5,4},{6,7},{7,6},{8,9},{9,8},{10,11... | collective-permute-start | bytes 4718600 | tf_op jit(solution)/shard_map/ppermute | solution.py:623
  57.4 8.0 %collective-permute-start.5 = (bf16[192,768]{1,0:T(8,128)(2,1)S(1)}, bf16[192,768]{1,0:T(8,128)(2,1)S(1)}, u32[]{:S(2)}, u32[]{:S(2)}) collective-permute-start(bf16[192,768]{1,0:T(8,128)(2,1)S(1)} %get-tuple-element.50), channel_id=1, source_target_pairs={{0,2},{1,9},{2,4},{3,11},{4,6},{5,13},{6,0},{7,15},{8,10},{9,17},{... | collective-permute-start | bytes 884744 | tf_op jit(solution)/shard_map/ppermute | solution.py:623
  58.1 7.4 %collective-permute-start.6 = (bf16[192,768]{1,0:T(8,128)(2,1)S(1)}, bf16[192,768]{1,0:T(8,128)(2,1)S(1)}, u32[]{:S(2)}, u32[]{:S(2)}) collective-permute-start(bf16[192,768]{1,0:T(8,128)(2,1)S(1)} %get-tuple-element.51), channel_id=1, source_target_pairs={{0,6},{1,25},{2,0},{3,27},{4,2},{5,29},{6,4},{7,31},{8,14},{9,1},{... | collective-permute-start | bytes 884744 | tf_op jit(solution)/shard_map/ppermute | solution.py:623
  65.6 11.2 %collective-permute-start.7 = (bf16[384,768]{1,0:T(8,128)(2,1)S(1)}, bf16[384,768]{1,0:T(8,128)(2,1)S(1)}, u32[]{:S(2)}, u32[]{:S(2)}) collective-permute-start(bf16[384,768]{1,0:T(8,128)(2,1)S(1)} %get-tuple-element.52), channel_id=1, source_target_pairs={{0,2},{1,9},{2,4},{3,11},{4,6},{5,13},{6,0},{7,15},{8,10},{9,17},{... | collective-permute-start | bytes 1769480 | tf_op jit(solution)/shard_map/ppermute | solution.py:623
  65.7 11.1 %collective-permute-start.8 = (bf16[384,768]{1,0:T(8,128)(2,1)S(1)}, bf16[384,768]{1,0:T(8,128)(2,1)S(1)}, u32[]{:S(2)}, u32[]{:S(2)}) collective-permute-start(bf16[384,768]{1,0:T(8,128)(2,1)S(1)} %get-tuple-element.53), channel_id=1, source_target_pairs={{0,6},{1,25},{2,0},{3,27},{4,2},{5,29},{6,4},{7,31},{8,14},{9,1},{... | collective-permute-start | bytes 1769480 | tf_op jit(solution)/shard_map/ppermute | solution.py:623
  74.8 5.8 %copy-start = (bf16[768,768]{1,0:T(8,128)(2,1)S(1)}, bf16[768,768]{1,0:T(8,128)(2,1)}, u32[]{:S(2)}) copy-start(bf16[768,768]{1,0:T(8,128)(2,1)} %w_attn.1) | copy-start | bytes 3538948
  77.0 8.0 %collective-permute-start.9 = (bf16[96,768]{1,0:T(8,128)(2,1)S(1)}, bf16[96,768]{1,0:T(8,128)(2,1)S(1)}, u32[]{:S(2)}, u32[]{:S(2)}) collective-permute-start(bf16[96,768]{1,0:T(8,128)(2,1)S(1)} %get-tuple-element.58), channel_id=1, source_target_pairs={{0,8},{1,3},{2,10},{3,5},{4,12},{5,7},{6,14},{7,1},{8,16},{9,11},{... | collective-permute-start | bytes 442376 | tf_op jit(solution)/shard_map/ppermute | solution.py:623
  77.1 7.9 %collective-permute-start.10 = (bf16[96,768]{1,0:T(8,128)(2,1)S(1)}, bf16[96,768]{1,0:T(8,128)(2,1)S(1)}, u32[]{:S(2)}, u32[]{:S(2)}) collective-permute-start(bf16[96,768]{1,0:T(8,128)(2,1)S(1)} %get-tuple-element.59), channel_id=1, source_target_pairs={{0,16},{1,5},{2,18},{3,7},{4,20},{5,1},{6,22},{7,3},{8,24},{9,13},... | collective-permute-start | bytes 442376 | tf_op jit(solution)/shard_map/ppermute | solution.py:623
  79.3 6.6 %collective-permute-start.11 = (bf16[96,768]{1,0:T(8,128)(2,1)S(1)}, bf16[96,768]{1,0:T(8,128)(2,1)S(1)}, u32[]{:S(2)}, u32[]{:S(2)}) collective-permute-start(bf16[96,768]{1,0:T(8,128)(2,1)S(1)} %get-tuple-element.60), channel_id=1, source_target_pairs={{0,24},{1,7},{2,26},{3,1},{4,28},{5,3},{6,30},{7,5},{8,0},{9,15},{... | collective-permute-start | bytes 442376 | tf_op jit(solution)/shard_map/ppermute | solution.py:623
  86.5 1.5 %collective-permute-start.12 = (f32[48,768]{1,0:T(8,128)S(1)}, f32[48,768]{1,0:T(8,128)S(1)}, u32[]{:S(2)}, u32[]{:S(2)}) collective-permute-start(f32[48,768]{1,0:T(8,128)S(1)} %get-tuple-element.62), channel_id=1, source_target_pairs={{0,1},{1,0},{2,3},{3,2},{4,5},{5,4},{6,7},{7,6},{8,9},{9,8},{10,11... | collective-permute-start | bytes 442376 | tf_op jit(solution)/shard_map/ppermute | solution.py:623

commit v5 on v4

--- a/solution.py
+++ b/solution.py
@@ -133,7 +133,6 @@
     size = 128
     blocks = tiles.shape[0] // size
     per_tile = patches // size
-    total[...] = jnp.zeros_like(total)
 
     def product(item):
         j, part = item // blocks, item % blocks
@@ -145,7 +144,7 @@
                 load_out(j + 2).start()
         return dot_nn(normed[pl.ds(part * size, size), :], w_in[j])
 
-    preact, sums = product(0), []
+    preact, sums, boths = product(0), [], []
     for item in range(steps * blocks):
         j, part = item // blocks, item % blocks
         later = product(item + 1) if item + 1 < steps * blocks else None
@@ -159,11 +158,13 @@
             high, low = halves(jnp.concatenate(means, axis=0))
             both = jnp.concatenate([high, low], axis=0)
             pooled[:, columns(j)] = both
-            load_out(j).wait()
-            total[...] += dot_nn(both, w_out[j])
+            boths.append(both)
             sums = []
     for j in range(steps):
         store_slope(j, slope_send if j < half else slope_keep).wait()
+    for j in range(steps):
+        load_out(j).wait()
+    total[...] = dot_nn(jnp.concatenate(boths, axis=1), w_out[...].reshape(-1, w_out.shape[2]))
     width = total.shape[1]
     shared[:, :width] = total[:tile_count, :] + total[tile_count:, :]
     load_cot.wait()
@@ -286,13 +287,15 @@
     d_preact,
     lhs0,
     lhs1,
-    lhs2,
     lhs3,
+    upper,
+    lower,
     d_qkv,
     d_direct,
     context,
     slide_rows,
     pooled_pair,
+    lhs2,
     slope,
     w_proj,
     w_qkv,
@@ -423,6 +426,9 @@
     for tile in range(8):
         at = pl.ds(tile * patches, patches)
         d_preact[at, :] = (slope[at, :].astype(F4) * back[tile : tile + 1, :]).astype(BF)
+    half_chunk = upper.shape[0]
+    upper[...] = dot_nn(lhs2[:half_chunk, :], d_preact[...]).astype(BF)
+    lower[...] = dot_nn(lhs2[half_chunk:, :], d_preact[...]).astype(BF)
 
 
 def attention(place, seg_len, gathered, weights, cot_all, slide_of, order_of, normed, slopes):
@@ -434,10 +440,11 @@
     return pl.pallas_call(
         attention_kernel,
         in_specs=[SMEM, SMEM] + [VMEM] * 2 + [ANY] * 10,
-        out_specs=[VMEM] * 10,
+        out_specs=[VMEM] * 11,
         out_shape=[
             pltpu.VMEM((2 * tokens, hidden), BF),
-            *[pltpu.VMEM((width // 4, 2 * tokens), BF)] * 4,
+            *[pltpu.VMEM((width // 4, 2 * tokens), BF)] * 3,
+            *[jax.ShapeDtypeStruct((width // 8, hidden), BF)] * 2,
             jax.ShapeDtypeStruct((tiles, 3 * slide_width), BF),
             jax.ShapeDtypeStruct((tiles, slide_width), F4),
             jax.ShapeDtypeStruct((tiles, slide_width), F4),
@@ -445,6 +452,7 @@
             jax.ShapeDtypeStruct((tiles, 256), BF),
         ],
         scratch_shapes=[
+            pltpu.VMEM((width // 4, 2 * tokens), BF),
             pltpu.VMEM((2 * tokens, hidden), BF),
             pltpu.VMEM(w_proj.shape, BF),
             pltpu.VMEM(w_qkv.shape, BF),
@@ -454,7 +462,7 @@
             pltpu.VMEM(cot_all.shape, F4),
             pltpu.SemaphoreType.DMA((40,)),
         ],
-        compiler_params=pltpu.CompilerParams(vmem_limit_bytes=24 * MIB),
+        compiler_params=pltpu.CompilerParams(vmem_limit_bytes=28 * MIB),
         name="attention",
     )(
         place,
@@ -673,7 +681,7 @@
         mine.reshape(peers, 8, -1), "tile", split_axis=0, concat_axis=0, tiled=True
     ).reshape(peers * 8, -1)
     slope_other, normed_other = other_core(slope_send), other_core(normed_t)
-    d_preact, *lhs, d_qkv, d_direct, context, slide_rows, pooled_pair = attention(
+    d_preact, lhs0, lhs1, lhs3, upper, lower, d_qkv, d_direct, context, slide_rows, pooled_pair = attention(
         place,
         seg_len,
         gathered,
@@ -684,10 +692,9 @@
         (normed_t, normed_other),
         (slope_keep, slope_other),
     )
-    upper, lower = grad_chunk(lhs[2], d_preact, 2)
     up_received, down_received = first_axis(upper, 1), first_axis(lower, 3)
-    up, down = grad_chunk(lhs[1], d_preact)[0], grad_chunk(lhs[3], d_preact)[0]
-    own = grad_chunk(lhs[0], d_preact)[0]
+    up, down = grad_chunk(lhs1, d_preact)[0], grad_chunk(lhs3, d_preact)[0]
+    own = grad_chunk(lhs0, d_preact)[0]
     up, down = relay(up, down, up_received, down_received, own)
     parts = [own, first_axis(up, 1), first_axis(down, 3)]
     grad_out = grad_out_of(pooled_pair, d_qkv, d_direct, (w_qkv, w_proj), hidden // peers)

time: 90.5 us -> 89.8 us (level)
    pallas_call x4 -> x3, Pallas kernels: 5.53 us -> 4.15 us  [grad_chunk(): pl.pallas_call(grad_kernel, in_specs=[VMEM] * 2, out_specs=[VMEM] * parts...]
    pallas_call x1, Pallas kernels: 11.3 us -> 12.2 us  [attention(): pl.pallas_call(attention_kernel, in_specs=[SMEM, SMEM] + [VMEM] * 2 + [AN...]
  transfers between devices with their start and end apart: 13 -> 13, of which waited for: 6 -> 6; matrix products, arithmetic and copies ran while one was open for 0% -> 0% of each run, Pallas kernels for 17% -> 18%
where the time goes in v5:
time: 89.8 us; the launch traced here: 88.6 us
  Pallas kernels  45.2 us (50%)
  blocking collectives  19.1 us (21%)
  starting transfers between devices  15.7 us (17%)
  waiting for transfers between devices  7.41 us (8%)
    all_to_all x1, blocking collectives, on_device(): lax.all_to_all(mine.reshape(peers, 8, -1), 'tile', split_axis=0, concat_a...  19.1 us
    pallas_call x1, Pallas kernels, forward(): pl.pallas_call(forward_kernel, in_specs=[ANY] * 4, out_specs=[ANY, ANY, V...  14.6 us
    pallas_call x1, Pallas kernels, attention(): pl.pallas_call(attention_kernel, in_specs=[SMEM, SMEM] + [VMEM] * 2 + [AN...  12.2 us
    ppermute x10, starting transfers between devices, moved(): return lax.ppermute(value, 'tile', pairs)  10.9 us
    ppermute x10, waiting for transfers between devices, moved(): return lax.ppermute(value, 'tile', pairs)  7.17 us
    pallas_call x1, Pallas kernels, grad_out_of(): pl.pallas_call(grad_out_kernel, in_specs=[VMEM] * 3 + [ANY] * 2, out_shap...  5.91 us
    ppermute x3, starting transfers between devices, on_device(): lax.ppermute(shared, 'slide', [(i, (i + k) % 4) for i in range(4)])  4.75 us
    pallas_call x3, Pallas kernels, grad_chunk(): pl.pallas_call(grad_kernel, in_specs=[VMEM] * 2, out_specs=[VMEM] * parts...  4.15 us
  transfers between devices with their start and end apart: 13, of which 6 were waited for; matrix products, arithmetic and copies ran while one was open for 0% of the time, Pallas kernels for 18%

profile of v5, /device:TPU:0, one launch (start us, length us, event | category | flops | bytes accessed | tf_op | source)
XLA Modules:
  0.0 88.6 jit_solution(17198449539195925749)
XLA Ops:
  0.6 14.6 %forward.1 = (bf16[1024,768]{1,0:T(8,128)(2,1)}, bf16[1024,768]{1,0:T(8,128)(2,1)}, bf16[8,1536]{1,0:T(8,128)(2,1)S(1)}, f32[4,2304]{1,0:T(4,128)S(1)}, f32[4,15...) custom-call(bf16[1024,1536]{1,0:T(8,128)(2,1)} %bitcast.20, bf16[1536,1536]{1,0:T(8,128)(2,1)} %w_in_hbm.1, ...), custom_call_target="tpu_custom_call" | custom-call | tf_op jit(solution)/shard_map/forward/pallas_call | solution.py:182
  15.2 3.1 %collective-permute-start.2 = (f32[4,2304]{1,0:T(4,128)S(1)}, f32[4,2304]{1,0:T(4,128)S(1)}, u32[]{:S(2)}, u32[]{:S(2)}) collective-permute-start(f32[4,2304]{1,0:T(4,128)S(1)} %get-tuple-element.32.after.own), channel_id=1, source_target_pairs={{0,96},{32,0},{64,32},{96,64},{1,97},{33,1},{65,33},{97,65},{2,98}... | collective-permute-start | bytes 110600 | tf_op jit(solution)/shard_map/ppermute | solution.py:672
  18.4 0.6 collective-permute-start.1
  19.0 1.0 %collective-permute-start = (f32[4,2304]{1,0:T(4,128)S(1)}, f32[4,2304]{1,0:T(4,128)S(1)}, u32[]{:S(2)}, u32[]{:S(2)}) collective-permute-start(f32[4,2304]{1,0:T(4,128)S(1)} %get-tuple-element.32.after.own), channel_id=1, source_target_pairs={{0,32},{32,64},{64,96},{96,0},{1,33},{33,65},{65,97},{97,1},{2,34}... | collective-permute-start | bytes 110600 | tf_op jit(solution)/shard_map/ppermute | solution.py:672
  20.1 0.1 reshape.34
  20.3 0.1 stack.23.place
  20.4 3.6 %transposed.1.normed_in = bf16[1536,1024]{1,0:T(8,128)(2,1)} custom-call(f32[4,2304]{1,0:T(4,128)S(1)} %get-tuple-element.32.after.own, bf16[1024,1536]{1,0:T(8,128)(2,1)} %get-tuple-element.35.normed), custom_call_target="tpu_custom_call" | custom-call | flops 20000000 | bytes 9000000 | tf_op jit(solution)/shard_map/transposed/pallas_call | solution.py:220
  24.0 0.2 collective-permute-done.one
  24.2 0.6 embed.1
  25.0 0.5 collective-permute-start.4
  25.5 19.1 %all_to_all.5 = bf16[32,8,896]{2,1,0:T(8,128)(2,1)} all-to-all(bf16[32,8,896]{2,1,0:T(8,128)(2,1)S(1)} %bitcast.16), channel_id=1, replica_groups=mesh['slide'=4,'tile'=32] {'tile'}, dimensions={0} | all-to-all | bytes 917504 | tf_op jit(solution)/shard_map/all_to_all | solution.py:680
  44.6 12.2 %attention.1 = (bf16[2048,768]{1,0:T(8,128)(2,1)S(1)}, bf16[384,2048]{1,0:T(8,128)(2,1)S(1)}, bf16[384,2048]{1,0:T(8,128)(2,1)S(1)}, bf16[384,2048]{1,0:T(8,128)...) custom-call(s32[5]{0:T(128)S(1)} %stack.23.place, ...), custom_call_target="tpu_custom_call" | custom-call | tf_op jit(solution)/shard_map/attention/pallas_call | solution.py:440
  56.8 0.6 collective-permute-start.5
  57.4 2.7 %collective-permute-start.6 = (bf16[192,768]{1,0:T(8,128)(2,1)S(1)}, bf16[192,768]{1,0:T(8,128)(2,1)S(1)}, u32[]{:S(2)}, u32[]{:S(2)}) collective-permute-start(bf16[192,768]{1,0:T(8,128)(2,1)S(1)} %get-tuple-element.49), channel_id=1, source_target_pairs={{0,6},{1,25},{2,0},{3,27},{4,2},{5,29},{6,4},{7,31},{8,14},{9,1},{... | collective-permute-start | bytes 884744 | tf_op jit(solution)/shard_map/ppermute | solution.py:631
  60.1 1.4 %grad_chunk.3.after.one = bf16[384,768]{1,0:T(8,128)(2,1)S(1)} custom-call(bf16[384,2048]{1,0:T(8,128)(2,1)S(1)} %get-tuple-element.44.lhs, bf16[2048,768]{1,0:T(8,128)(2,1)S(1)} %get-tuple-element.45.d_preact), custom_call_target="tpu_custom_call" | custom-call | flops 1000 | bytes 1000 | tf_op jit(solution)/shard_map/grad_chunk/pallas_call | solution.py:540
  61.5 1.4 %grad_chunk.4.up = bf16[384,768]{1,0:T(8,128)(2,1)S(1)} custom-call(bf16[384,2048]{1,0:T(8,128)(2,1)S(1)} %get-tuple-element.46.lhs, bf16[2048,768]{1,0:T(8,128)(2,1)S(1)} %get-tuple-element.45.d_preact), custom_call_target="tpu_custom_call" | custom-call | flops 1000 | bytes 1000 | tf_op jit(solution)/shard_map/grad_chunk/pallas_call | solution.py:540
  62.9 1.4 %grad_chunk.5.down = bf16[384,768]{1,0:T(8,128)(2,1)S(1)} custom-call(bf16[384,2048]{1,0:T(8,128)(2,1)S(1)} %get-tuple-element.47.lhs, bf16[2048,768]{1,0:T(8,128)(2,1)S(1)} %get-tuple-element.45.d_preact), custom_call_target="tpu_custom_call" | custom-call | flops 1000 | bytes 1000 | tf_op jit(solution)/shard_map/grad_chunk/pallas_call | solution.py:540
  64.2 0.5 collective-permute-done.5.up_received
  64.8 0.2 relay.1
  65.0 3.3 %collective-permute-start.8 = (bf16[384,768]{1,0:T(8,128)(2,1)S(1)}, bf16[384,768]{1,0:T(8,128)(2,1)S(1)}, u32[]{:S(2)}, u32[]{:S(2)}) collective-permute-start(bf16[384,768]{1,0:T(8,128)(2,1)S(1)} %get-tuple-element.51), channel_id=1, source_target_pairs={{0,6},{1,25},{2,0},{3,27},{4,2},{5,29},{6,4},{7,31},{8,14},{9,1},{... | collective-permute-start | bytes 1769480 | tf_op jit(solution)/shard_map/ppermute | solution.py:631
  68.3 5.9 %grad_out.1.after = f32[48,1536]{1,0:T(8,128)} custom-call(bf16[128,256]{1,0:T(8,128)(2,1)S(1)} %get-tuple-element.52.pooled_pair, bf16[128,2304]{1,0:T(8,128)(2,1)S(1)} %get-tuple-element.53.d_qkv, f32[128,768]{1,0:T(8,128)S(1)} %get-tuple-element.54.d_direct, bf16[768,2304]{1,0:T(8,128)(2,1)} %w_qkv_hbm.3, bf16[1536,768]{1,0:T(8,128)(2,1)} %w_proj_hbm.3), custom_call_target="tpu_custom_call" | custom-call | flops 1000 | bytes 1000 | tf_op jit(solution)/shard_map/grad_out/pallas_call | solution.py:520
  74.2 1.9 %collective-permute-done.7.two = bf16[384,768]{1,0:T(8,128)(2,1)S(1)} collective-permute-done((bf16[384,768]{1,0:T(8,128)(2,1)S(1)}, bf16[384,768]{1,0:T(8,128)(2,1)S(1)}, u32[]{:S(2)}, u32[]{:S(2)}) %collective-permute-start.7) | collective-permute-done | bytes 589856 | tf_op jit(solution)/shard_map/ppermute | solution.py:631
  76.1 0.2 add_three.1
  76.4 2.3 %collective-permute-start.10 = (bf16[96,768]{1,0:T(8,128)(2,1)S(1)}, bf16[96,768]{1,0:T(8,128)(2,1)S(1)}, u32[]{:S(2)}, u32[]{:S(2)}) collective-permute-start(bf16[96,768]{1,0:T(8,128)(2,1)S(1)} %get-tuple-element.57), channel_id=1, source_target_pairs={{0,16},{1,5},{2,18},{3,7},{4,20},{5,1},{6,22},{7,3},{8,24},{9,13},... | collective-permute-start | bytes 442376 | tf_op jit(solution)/shard_map/ppermute | solution.py:631
  78.7 1.3 %collective-permute-start.11 = (bf16[96,768]{1,0:T(8,128)(2,1)S(1)}, bf16[96,768]{1,0:T(8,128)(2,1)S(1)}, u32[]{:S(2)}, u32[]{:S(2)}) collective-permute-start(bf16[96,768]{1,0:T(8,128)(2,1)S(1)} %get-tuple-element.58), channel_id=1, source_target_pairs={{0,24},{1,7},{2,26},{3,1},{4,28},{5,3},{6,30},{7,5},{8,0},{9,15},{... | collective-permute-start | bytes 442376 | tf_op jit(solution)/shard_map/ppermute | solution.py:631
  79.9 1.9 %embed_out.1.after = f32[4,768]{1,0:T(4,128)} custom-call(s32[5]{0:T(128)S(1)} %stack.23.place, f32[128,768]{1,0:T(8,128)S(1)} %get-tuple-element.42.context, bf16[128,768]{1,0:T(8,128)(2,1)S(1)} %get-tuple-element.43.slide_rows, s32[1,128]{1,0:T(1,128)S(1)} %bitcast.18, s32[16,1]{1,0:T(8,128)S(1)} %copy.17.counts, bf16[768,768]{1,0:T(8,128)(2,1)S(1)} %copy-done), custom_call_target="tpu_custom_call" | custom-call | flops 1000 | bytes 1000 | tf_op jit(solution)/shard_map/embed_out/pallas_call | solution.py:494
  81.8 2.5 %collective-permute-done.9.two = bf16[96,768]{1,0:T(8,128)(2,1)S(1)} collective-permute-done((bf16[96,768]{1,0:T(8,128)(2,1)S(1)}, bf16[96,768]{1,0:T(8,128)(2,1)S(1)}, u32[]{:S(2)}, u32[]{:S(2)}) %collective-permute-start.9) | collective-permute-done | bytes 147488 | tf_op jit(solution)/shard_map/ppermute | solution.py:631
  84.3 0.9 collective-permute-done.11.four
  85.2 0.6 split.1
  85.8 0.1 collective-permute-start.12
  85.9 1.4 %collective-permute-done.12.received = f32[48,768]{1,0:T(8,128)S(1)} collective-permute-done((f32[48,768]{1,0:T(8,128)S(1)}, f32[48,768]{1,0:T(8,128)S(1)}, u32[]{:S(2)}, u32[]{:S(2)}) %collective-permute-start.12) | collective-permute-done | bytes 147488 | tf_op jit(solution)/shard_map/ppermute | solution.py:631
  87.3 1.3 %finish.1 = f32[48,1536]{1,0:T(8,128)} custom-call(s32[5]{0:T(128)S(1)} %stack.23.place, f32[48,768]{1,0:T(8,128)S(1)} %get-tuple-element.59.keep, f32[48,768]{1,0:T(8,128)S(1)} %collective-permute-done.12.received), custom_call_target="tpu_custom_call" | custom-call | tf_op jit(solution)/shard_map/finish/pallas_call | solution.py:615
  (25 shorter events, 0.4 us)
Async XLA Ops:
  0.6 19.4 %copy-start.5 = (s32[16]{0:T(128)S(1)}, s32[16]{0:T(128)}, u32[]{:S(2)}) copy-start(s32[16]{0:T(128)} %param.19) | copy-start | bytes 196
  15.2 8.7 %collective-permute-start.2 = (f32[4,2304]{1,0:T(4,128)S(1)}, f32[4,2304]{1,0:T(4,128)S(1)}, u32[]{:S(2)}, u32[]{:S(2)}) collective-permute-start(f32[4,2304]{1,0:T(4,128)S(1)} %get-tuple-element.32.after.own), channel_id=1, source_target_pairs={{0,96},{32,0},{64,32},{96,64},{1,97},{33,1},{65,33},{97,65},{2,98}... | collective-permute-start | bytes 110600 | tf_op jit(solution)/shard_map/ppermute | solution.py:672
  18.4 5.6 %collective-permute-start.1 = (f32[4,2304]{1,0:T(4,128)S(1)}, f32[4,2304]{1,0:T(4,128)S(1)}, u32[]{:S(2)}, u32[]{:S(2)}) collective-permute-start(f32[4,2304]{1,0:T(4,128)S(1)} %get-tuple-element.32.after.own), channel_id=1, source_target_pairs={{0,64},{32,96},{64,0},{96,32},{1,65},{33,97},{65,1},{97,33},{2,66}... | collective-permute-start | bytes 110600 | tf_op jit(solution)/shard_map/ppermute | solution.py:672
  19.0 5.2 %collective-permute-start = (f32[4,2304]{1,0:T(4,128)S(1)}, f32[4,2304]{1,0:T(4,128)S(1)}, u32[]{:S(2)}, u32[]{:S(2)}) collective-permute-start(f32[4,2304]{1,0:T(4,128)S(1)} %get-tuple-element.32.after.own), channel_id=1, source_target_pairs={{0,32},{32,64},{64,96},{96,0},{1,33},{33,65},{65,97},{97,1},{2,34}... | collective-permute-start | bytes 110600 | tf_op jit(solution)/shard_map/ppermute | solution.py:672
  24.0 20.6 %copy-start.2 = (s32[128]{0:T(128)S(1)}, s32[128]{0:T(128)}, u32[]{:S(2)}) copy-start(s32[128]{0:T(128)} %param.17) | copy-start | bytes 1540
  24.0 20.6 %copy-start.3 = (s32[3]{0:T(128)S(1)}, s32[3]{0:T(128)}, u32[]{:S(2)}) copy-start(s32[3]{0:T(128)} %seg_len.1) | copy-start | bytes 40
  24.0 20.6 %copy-start.4 = (s32[128]{0:T(128)S(1)}, s32[128]{0:T(128)}, u32[]{:S(2)}) copy-start(s32[128]{0:T(128)} %param.18) | copy-start | bytes 1540
  24.9 19.7 %copy-start.1 = (f32[16,768]{1,0:T(8,128)}, f32[16,768]{1,0:T(8,128)S(1)}, u32[]{:S(2)}) copy-start(f32[16,768]{1,0:T(8,128)S(1)} %get-tuple-element.38.cot_hbm) | copy-start | bytes 147460
  24.9 19.7 %collective-permute-start.3 = (bf16[1536,1024]{1,0:T(8,128)(2,1)}, bf16[1536,1024]{1,0:T(8,128)(2,1)S(1)}, u32[]{:S(2)}, u32[]{:S(2)}) collective-permute-start(bf16[1536,1024]{1,0:T(8,128)(2,1)} %get-tuple-element.39.normed_own), channel_id=1, source_target_pairs={{0,1},{1,0},{2,3},{3,2},{4,5},{5,4},{6,7},{7,6},{8,9},{9,8},{10,11... | collective-permute-start | bytes 9437192 | tf_op jit(solution)/shard_map/ppermute | solution.py:631
  25.0 19.6 %collective-permute-start.4 = (bf16[1024,768]{1,0:T(8,128)(2,1)}, bf16[1024,768]{1,0:T(8,128)(2,1)S(1)}, u32[]{:S(2)}, u32[]{:S(2)}) collective-permute-start(bf16[1024,768]{1,0:T(8,128)(2,1)} %get-tuple-element.41), channel_id=1, source_target_pairs={{0,1},{1,0},{2,3},{3,2},{4,5},{5,4},{6,7},{7,6},{8,9},{9,8},{10,11... | collective-permute-start | bytes 4718600 | tf_op jit(solution)/shard_map/ppermute | solution.py:631
  56.8 8.0 %collective-permute-start.5 = (bf16[192,768]{1,0:T(8,128)(2,1)S(1)}, bf16[192,768]{1,0:T(8,128)(2,1)S(1)}, u32[]{:S(2)}, u32[]{:S(2)}) collective-permute-start(bf16[192,768]{1,0:T(8,128)(2,1)S(1)} %get-tuple-element.48), channel_id=1, source_target_pairs={{0,2},{1,9},{2,4},{3,11},{4,6},{5,13},{6,0},{7,15},{8,10},{9,17},{... | collective-permute-start | bytes 884744 | tf_op jit(solution)/shard_map/ppermute | solution.py:631
  57.4 7.4 %collective-permute-start.6 = (bf16[192,768]{1,0:T(8,128)(2,1)S(1)}, bf16[192,768]{1,0:T(8,128)(2,1)S(1)}, u32[]{:S(2)}, u32[]{:S(2)}) collective-permute-start(bf16[192,768]{1,0:T(8,128)(2,1)S(1)} %get-tuple-element.49), channel_id=1, source_target_pairs={{0,6},{1,25},{2,0},{3,27},{4,2},{5,29},{6,4},{7,31},{8,14},{9,1},{... | collective-permute-start | bytes 884744 | tf_op jit(solution)/shard_map/ppermute | solution.py:631
  64.9 11.2 %collective-permute-start.7 = (bf16[384,768]{1,0:T(8,128)(2,1)S(1)}, bf16[384,768]{1,0:T(8,128)(2,1)S(1)}, u32[]{:S(2)}, u32[]{:S(2)}) collective-permute-start(bf16[384,768]{1,0:T(8,128)(2,1)S(1)} %get-tuple-element.50), channel_id=1, source_target_pairs={{0,2},{1,9},{2,4},{3,11},{4,6},{5,13},{6,0},{7,15},{8,10},{9,17},{... | collective-permute-start | bytes 1769480 | tf_op jit(solution)/shard_map/ppermute | solution.py:631
  65.0 11.1 %collective-permute-start.8 = (bf16[384,768]{1,0:T(8,128)(2,1)S(1)}, bf16[384,768]{1,0:T(8,128)(2,1)S(1)}, u32[]{:S(2)}, u32[]{:S(2)}) collective-permute-start(bf16[384,768]{1,0:T(8,128)(2,1)S(1)} %get-tuple-element.51), channel_id=1, source_target_pairs={{0,6},{1,25},{2,0},{3,27},{4,2},{5,29},{6,4},{7,31},{8,14},{9,1},{... | collective-permute-start | bytes 1769480 | tf_op jit(solution)/shard_map/ppermute | solution.py:631
  68.3 11.6 %copy-start = (bf16[768,768]{1,0:T(8,128)(2,1)S(1)}, bf16[768,768]{1,0:T(8,128)(2,1)}, u32[]{:S(2)}) copy-start(bf16[768,768]{1,0:T(8,128)(2,1)} %w_attn.1) | copy-start | bytes 3538948
  76.3 8.0 %collective-permute-start.9 = (bf16[96,768]{1,0:T(8,128)(2,1)S(1)}, bf16[96,768]{1,0:T(8,128)(2,1)S(1)}, u32[]{:S(2)}, u32[]{:S(2)}) collective-permute-start(bf16[96,768]{1,0:T(8,128)(2,1)S(1)} %get-tuple-element.56), channel_id=1, source_target_pairs={{0,8},{1,3},{2,10},{3,5},{4,12},{5,7},{6,14},{7,1},{8,16},{9,11},{... | collective-permute-start | bytes 442376 | tf_op jit(solution)/shard_map/ppermute | solution.py:631
  76.4 7.9 %collective-permute-start.10 = (bf16[96,768]{1,0:T(8,128)(2,1)S(1)}, bf16[96,768]{1,0:T(8,128)(2,1)S(1)}, u32[]{:S(2)}, u32[]{:S(2)}) collective-permute-start(bf16[96,768]{1,0:T(8,128)(2,1)S(1)} %get-tuple-element.57), channel_id=1, source_target_pairs={{0,16},{1,5},{2,18},{3,7},{4,20},{5,1},{6,22},{7,3},{8,24},{9,13},... | collective-permute-start | bytes 442376 | tf_op jit(solution)/shard_map/ppermute | solution.py:631
  78.7 6.5 %collective-permute-start.11 = (bf16[96,768]{1,0:T(8,128)(2,1)S(1)}, bf16[96,768]{1,0:T(8,128)(2,1)S(1)}, u32[]{:S(2)}, u32[]{:S(2)}) collective-permute-start(bf16[96,768]{1,0:T(8,128)(2,1)S(1)} %get-tuple-element.58), channel_id=1, source_target_pairs={{0,24},{1,7},{2,26},{3,1},{4,28},{5,3},{6,30},{7,5},{8,0},{9,15},{... | collective-permute-start | bytes 442376 | tf_op jit(solution)/shard_map/ppermute | solution.py:631
  85.8 1.5 %collective-permute-start.12 = (f32[48,768]{1,0:T(8,128)S(1)}, f32[48,768]{1,0:T(8,128)S(1)}, u32[]{:S(2)}, u32[]{:S(2)}) collective-permute-start(f32[48,768]{1,0:T(8,128)S(1)} %get-tuple-element.60), channel_id=1, source_target_pairs={{0,1},{1,0},{2,3},{3,2},{4,5},{5,4},{6,7},{7,6},{8,9},{9,8},{10,11... | collective-permute-start | bytes 442376 | tf_op jit(solution)/shard_map/ppermute | solution.py:631
